TPU v7x, 256 devices: a whole 4x4x8 slice. The times are simulated.
256 devices in a mesh: pipe: 8 (over z), dp: 4 (over x), expert: 8 (over y, core).
Axes of the slice: x: 4, y: 4, z: 8, core: 2. Of those that a mesh axis runs over, the one named last changes fastest.
Arguments:
- handoff: bfloat16 [8, 1024, 3072], P('pipe', ('dp', 'expert')), may hold values from -6 to 6
- expert_ids: int32 [8, 1024, 4], P('pipe', ('dp', 'expert')), may hold values from 0 to 7, all different within a row; in each aligned block of 32 rows (0 to 31, 32 to 63, ..., all dimensions but the last counted through in order) at most 24 rows name the same one
- gates: bfloat16 [8, 1024, 4], P('pipe', ('dp', 'expert')), may hold values from 0.049804688 to 0.59765625
- down_weight: bfloat16 [8, 8, 5632, 3072], P('pipe', 'expert', 'dp'), may hold values from -0.078125 to 0.078125
- hidden: bfloat16 [8, 8, 768, 5632], P('pipe', 'expert', None, 'dp'), may hold values from -0.29882812 to 0.29882812
Outputs:
- hidden_grad: bfloat16 [8, 8, 768, 5632], P('pipe', 'expert', None, 'dp')
- gate_grad: float32 [8, 1024, 4], P('pipe', ('dp', 'expert'))
Inputs may be any that keep to these rules, and one draw needn't show every extreme that they name: `expert_ids`: each token names 4 distinct experts. Among the 32 tokens of one device (aligned blocks) no expert is named more than 24 times, and in every draw some device names some expert exactly 24 times.
All inputs are finite; a program needn't handle non-finite values.
Results may differ from a plain program's by a relative error of at most 0.001.
Values may be sent and summed in bfloat16 or wider, within the bound.
No kernel may reach another device: no remote copies, remote signals or barrier semaphores. Data moves between devices by JAX's collectives and lax.ppermute only.
A program may use at most 64 MiB of HBM per device.

v0:
```python
import jax
import jax.numpy as jnp
from jax import lax
from jax.sharding import PartitionSpec as P

EXPERTS = 8
TOP = 4
CAP = 24


def shifted(x, axis, by):
    size = lax.axis_size(axis)
    return lax.ppermute(x, axis, [(i, (i + by) % size) for i in range(size)])


def slot_index(route_flat):
    onehot = (route_flat[:, None] == jnp.arange(EXPERTS, dtype=jnp.int32)[None, :]).astype(
        jnp.int32
    )
    before = jnp.cumsum(onehot, axis=0) - onehot
    return jnp.sum(before * onehot, axis=1)


def column_of(route_flat):
    return route_flat * CAP + slot_index(route_flat)


def pack(route_flat, token_rows, gate_flat):
    column = column_of(route_flat)
    chosen = column[None, :] == jnp.arange(EXPERTS * CAP, dtype=jnp.int32)[:, None]
    by_token = (
        chosen.reshape(EXPERTS * CAP, token_rows.shape[0], TOP).any(axis=2).astype(jnp.bfloat16)
    )
    packed = jnp.dot(by_token, token_rows, preferred_element_type=jnp.float32).astype(jnp.bfloat16)
    gate_column = jnp.sum(
        jnp.where(chosen, gate_flat[None, :].astype(jnp.float32), 0.0), axis=1
    ).astype(jnp.bfloat16)
    return (packed, gate_column)


def on_device(handoff, expert_ids, gates, down_weight, hidden):
    incoming = shifted(handoff, "pipe", -1)[0]
    token_count = incoming.shape[0]
    feature_width = incoming.shape[1]
    replicas = lax.axis_size("dp")
    expert_devices = lax.axis_size("expert")
    local_experts = EXPERTS // expert_devices
    own_routes = expert_ids[0].reshape(-1)
    own_column = column_of(own_routes)
    packed, gate_column = pack(own_routes, incoming, gates[0].reshape(-1))
    packed = packed.reshape(1, expert_devices, local_experts, CAP, feature_width)
    gate_column = gate_column.reshape(1, expert_devices, local_experts, CAP)
    copies = jnp.broadcast_to(
        packed, (replicas, expert_devices, local_experts, CAP, feature_width)
    ).reshape(replicas * expert_devices, local_experts, CAP, feature_width)
    gate_copies = jnp.broadcast_to(
        gate_column, (replicas, expert_devices, local_experts, CAP)
    ).reshape(replicas * expert_devices, local_experts, CAP)
    arrived, arrived_gates = (
        lax.all_to_all(copies, ("dp", "expert"), split_axis=0, concat_axis=0, tiled=True),
        lax.all_to_all(gate_copies, ("dp", "expert"), split_axis=0, concat_axis=0, tiled=True),
    )
    arrived = arrived.reshape(replicas, expert_devices, local_experts, CAP, feature_width)
    arrived_gates = arrived_gates.reshape(replicas, expert_devices, local_experts, CAP)
    layout_form = "djecx"
    gate_order = (2, 0, 1, 3)
    products = jnp.einsum(
        layout_form + ",efx->edjcf", arrived, down_weight[0], preferred_element_type=jnp.float32
    )
    scales = jnp.transpose(arrived_gates, gate_order).astype(jnp.float32)
    hidden_units = down_weight.shape[2]
    hidden_grad = (
        (scales[..., None] * products).astype(jnp.bfloat16).reshape(local_experts, -1, hidden_units)
    )
    saved_rows = hidden[0].reshape(local_experts, replicas, expert_devices, CAP, hidden_units)
    slice_sums = jnp.sum(saved_rows.astype(jnp.float32) * products, axis=4)
    own_sums = lax.psum_scatter(slice_sums, "dp", scatter_dimension=1, tiled=True)
    totals = lax.all_to_all(own_sums, "expert", split_axis=2, concat_axis=0, tiled=True).reshape(
        EXPERTS * CAP
    )
    gate_grad = jnp.take(totals, own_column).reshape(token_count, TOP)
    return (hidden_grad[None], gate_grad[None])


def solution(mesh):
    return jax.shard_map(
        on_device,
        mesh=mesh,
        in_specs=(
            P("pipe", ("dp", "expert"), None),
            P("pipe", ("dp", "expert"), None),
            P("pipe", ("dp", "expert"), None),
            P("pipe", "expert", "dp", None),
            P("pipe", "expert", None, "dp"),
        ),
        out_specs=(P("pipe", "expert", None, "dp"), P("pipe", ("dp", "expert"), None)),
        check_vma=False,
    )
```

profile of v0, /device:TPU:1, one launch (start us, length us, event | category | flops | bytes accessed | tf_op | source)
XLA Modules:
  0.0 136.5 jit_solution(13766018077637162354)
XLA Ops:
  0.6 0.8 copy.38
  1.4 0.1 reshape_squeeze.4
  1.5 0.1 fusion.6
  1.6 0.2 reduce_window_sum.12
  1.8 0.2 select_reduce_fusion.1
  2.0 0.8 copy.39
  2.7 0.1 reshape.134
  2.8 0.1 select_reduce_fusion
  3.0 0.1 convert_element_type.56
  3.0 0.6 copy.40
  3.7 8.6 %all-to-all-start = ((bf16[32,1,24]{2,1,0:T(2,128)(2,1)}), bf16[32,1,24]{2,1,0:T(2,128)(2,1)S(1)}, u32[]{:S(2)}, u32[]{:S(2)}) async-start(bf16[32,1,24]{2,1,0:T(2,128)(2,1)} %copy.40), calls=%async_computation | async-start | bytes 32768 | tf_op jit(solution)/shard_map/all_to_all | solution.py:61
  12.3 5.7 %collective-permute-start = (bf16[1,32,3072]{2,1,0:T(8,128)(2,1)}, bf16[1,32,3072]{2,1,0:T(8,128)(2,1)S(1)}, u32[]{:S(2)}, u32[]{:S(2)}) collective-permute-start(bf16[1,32,3072]{2,1,0:T(8,128)(2,1)} %param.5), channel_id=1, source_target_pairs={{0,224},{32,0},{64,32},{96,64},{128,96},{160,128},{192,160},{224,1... | collective-permute-start | bytes 589832 | tf_op jit(solution)/shard_map/ppermute | solution.py:13
  17.9 0.1 reduce_sum.41
  18.0 0.1 copy.43
  18.1 0.1 copy.42
  18.2 0.1 fusion.5
  18.3 4.0 %collective-permute-done = bf16[1,32,3072]{2,1,0:T(8,128)(2,1)S(1)} collective-permute-done((bf16[1,32,3072]{2,1,0:T(8,128)(2,1)}, bf16[1,32,3072]{2,1,0:T(8,128)(2,1)S(1)}, u32[]{:S(2)}, u32[]{:S(2)}) %collective-permute-start) | collective-permute-done | bytes 196640 | tf_op jit(solution)/shard_map/ppermute | solution.py:13
  22.3 0.5 convolution_convert_fusion
  22.8 0.0 all-to-all-done
  22.8 2.8 %broadcast_in_dim.44 = bf16[4,8,24,3072]{3,2,1,0:T(8,128)(2,1)} broadcast(bf16[8,24,3072]{2,1,0:T(8,128)(2,1)S(1)} %bitcast.43), dimensions={1,2,3} | broadcast | bytes 5898240 | tf_op jit(solution)/shard_map/broadcast_in_dim | solution.py:53
  25.6 0.0 copy-start.1
  25.6 0.0 copy-start
  25.6 8.2 %all-to-all-start.1 = ((bf16[32,1,24,3072]{3,2,1,0:T(8,128)(2,1)}), bf16[32,1,24,3072]{3,2,1,0:T(8,128)(2,1)}, u32[]{:S(2)}, u32[]{:S(2)}) async-start(bf16[32,1,24,3072]{3,2,1,0:T(8,128)(2,1)} %bitcast.42), calls=%async_computation.1 | async-start | bytes 9437184 | tf_op jit(solution)/shard_map/all_to_all | solution.py:60
  33.9 0.1 mul.51
  34.0 0.0 copy-done.1
  34.0 0.6 dynamic-slice
  34.6 57.7 %all-to-all-done.1 = bf16[32,1,24,3072]{3,2,1,0:T(8,128)(2,1)} async-done(((bf16[32,1,24,3072]{3,2,1,0:T(8,128)(2,1)}), bf16[32,1,24,3072]{3,2,1,0:T(8,128)(2,1)}, u32[]{:S(2)}, u32[]{:S(2)}) %all-to-all-start.1) | async-done | bytes 4718624 | tf_op jit(solution)/shard_map/all_to_all | solution.py:60
  92.3 0.0 copy-done
  92.3 13.1 %fusion.3 = (f32[4,8,24]{2,1,0:T(8,128)S(1)}, bf16[4,8,24,1408]{3,2,1,0:T(8,128)(2,1)}) fusion(bf16[4,8,24,1408]{3,2,1,0:T(8,128)(2,1)S(1)} %bitcast.46, f32[4,8,24]{2,1,0:T(8,128)S(1)} %bitcast.44, bf16[1,1,1408,3072]{3,2,1,0:T(8,128)(2,1)} %param.8, bf16[4,8,24,3072]{3,2,1,0:T(8,128)(2,1)} %bitcast.41), kind=kOutput, calls=%fused_computation.5 | convolution fusion | flops 6649183232 | bytes 17700864 | tf_op jit(solution)/shard_map/djecx,efx->edjcf/dot_general | solution.py:67
  105.4 12.0 %all-reduce = f32[1,4,8,24]{3,2,1,0:T(8,128)S(1)} all-reduce(f32[1,4,8,24]{3,2,1,0:T(8,128)S(1)} %bitcast.45), channel_id=2, replica_groups=mesh['pipe'=8,'dp'=4,'expert'=8] {'dp'}, use_global_device_ids=true, to_apply=%region_5.6.clone | all-reduce | flops 768 | bytes 6144
  117.4 1.2 constant_dynamic-slice_fusion
  118.6 10.0 %all-to-all-start.2 = ((f32[1,1,8,24]{3,1,0,2:T(1,128)}), f32[1,1,8,24]{3,1,0,2:T(1,128)S(1)}, u32[]{:S(2)}, u32[]{:S(2)}) async-start(f32[1,1,8,24]{3,1,0,2:T(1,128)} %bitcast.13), calls=%async_computation.2 | async-start | bytes 8192 | tf_op jit(solution)/shard_map/all_to_all | solution.py:78
  128.6 0.1 reduce_sum.42
  128.7 4.5 %all-to-all-done.2 = f32[1,1,8,24]{3,1,0,2:T(1,128)S(1)} async-done(((f32[1,1,8,24]{3,1,0,2:T(1,128)}), f32[1,1,8,24]{3,1,0,2:T(1,128)S(1)}, u32[]{:S(2)}, u32[]{:S(2)}) %all-to-all-start.2) | async-done | bytes 800 | tf_op jit(solution)/shard_map/all_to_all | solution.py:78
  133.2 0.5 broadcast.84
  133.7 0.7 reduce.5
  134.4 0.1 reshape.133
  134.5 1.3 gather_fusion
  135.7 0.1 gather.7
  135.9 0.7 copy.45
  (8 shorter events, 0.1 us)
Async XLA Ops:
  3.7 19.1 %all-to-all-start = ((bf16[32,1,24]{2,1,0:T(2,128)(2,1)}), bf16[32,1,24]{2,1,0:T(2,128)(2,1)S(1)}, u32[]{:S(2)}, u32[]{:S(2)}) async-start(bf16[32,1,24]{2,1,0:T(2,128)(2,1)} %copy.40), calls=%async_computation | async-start | bytes 32768 | tf_op jit(solution)/shard_map/all_to_all | solution.py:61
  12.3 10.0 %collective-permute-start = (bf16[1,32,3072]{2,1,0:T(8,128)(2,1)}, bf16[1,32,3072]{2,1,0:T(8,128)(2,1)S(1)}, u32[]{:S(2)}, u32[]{:S(2)}) collective-permute-start(bf16[1,32,3072]{2,1,0:T(8,128)(2,1)} %param.5), channel_id=1, source_target_pairs={{0,224},{32,0},{64,32},{96,64},{128,96},{160,128},{192,160},{224,1... | collective-permute-start | bytes 589832 | tf_op jit(solution)/shard_map/ppermute | solution.py:13
  25.6 8.4 %copy-start.1 = (u32[256]{0:T(256)S(1)}, u32[256]{0:T(256)}, u32[]{:S(2)}) copy-start(u32[256]{0:T(256)} %constant.35) | copy-start | bytes 3076
  25.6 66.7 %copy-start = (bf16[1,1,768,1408]{3,2,1,0:T(8,128)(2,1)S(1)}, bf16[1,1,768,1408]{3,2,1,0:T(8,128)(2,1)}, u32[]{:S(2)}) copy-start(bf16[1,1,768,1408]{3,2,1,0:T(8,128)(2,1)} %param.9) | copy-start | bytes 6488068
  25.6 66.7 %all-to-all-start.1 = ((bf16[32,1,24,3072]{3,2,1,0:T(8,128)(2,1)}), bf16[32,1,24,3072]{3,2,1,0:T(8,128)(2,1)}, u32[]{:S(2)}, u32[]{:S(2)}) async-start(bf16[32,1,24,3072]{3,2,1,0:T(8,128)(2,1)} %bitcast.42), calls=%async_computation.1 | async-start | bytes 9437184 | tf_op jit(solution)/shard_map/all_to_all | solution.py:60
  118.6 14.5 %all-to-all-start.2 = ((f32[1,1,8,24]{3,1,0,2:T(1,128)}), f32[1,1,8,24]{3,1,0,2:T(1,128)S(1)}, u32[]{:S(2)}, u32[]{:S(2)}) async-start(f32[1,1,8,24]{3,1,0,2:T(1,128)} %bitcast.13), calls=%async_computation.2 | async-start | bytes 8192 | tf_op jit(solution)/shard_map/all_to_all | solution.py:78
where the time goes:
time: 137 us
  waiting for transfers between devices  66.1 us (48%)
  starting transfers between devices  32.5 us (24%)
  matrix products  13.6 us (10%)
  blocking collectives  12 us (9%)
  local copies, waits for them, and re-layouts  10.1 us (7%)
  other arithmetic  1.37 us (1%)
    all_to_all x1, waiting for transfers between devices, on_device(): lax.all_to_all(copies, ('dp', 'expert'), split_axis=0, concat_axis=0, til...  57.7 us
    dot_general x1, matrix products, on_device(): jnp.einsum(layout_form + ',efx->edjcf', arrived, down_weight[0], preferre...  13.1 us
    unnamed x1, blocking collectives  12 us
    all_to_all x1, starting transfers between devices, on_device(): lax.all_to_all(own_sums, 'expert', split_axis=2, concat_axis=0, tiled=True)  9.97 us
    all_to_all x1, starting transfers between devices, on_device(): lax.all_to_all(gate_copies, ('dp', 'expert'), split_axis=0, concat_axis=0...  8.59 us
    all_to_all x1, starting transfers between devices, on_device(): lax.all_to_all(copies, ('dp', 'expert'), split_axis=0, concat_axis=0, til...  8.25 us
    ppermute x1, starting transfers between devices, shifted(): return lax.ppermute(x, axis, [(i, (i + by) % size) for i in range(size)])  5.65 us
    all_to_all x1, waiting for transfers between devices, on_device(): lax.all_to_all(own_sums, 'expert', split_axis=2, concat_axis=0, tiled=True)  4.47 us
  transfers between devices with their start and end apart: 4, of which 3 were waited for; matrix products, arithmetic and copies ran while one was open for 1% of the time, Pallas kernels for 0%

commit v1 on v0

v1 whole, which is shorter than its diff:
```python
import functools

import jax
import jax.numpy as jnp
from jax import lax
from jax.experimental import pallas as pl
from jax.experimental.pallas import tpu as pltpu
from jax.sharding import PartitionSpec as P

EXPERTS = 8
TOP = 4
CAP = 24
ROWS = 32
META = 128
TILE = 256
OFFSETS = (0, -1, 1, 2)
AXES = ("pipe", "dp", "expert")
VMEM_LIMIT = 44 * 1024 * 1024
F32 = jnp.float32
BF16 = jnp.bfloat16


def moved(x, to):
    nz, nx, ne = (lax.axis_size(a) for a in AXES)
    ny = ne // 2

    def index(z, i, j, c):
        return ((z % nz) * nx + i % nx) * ne + (j % ny) * 2 + c

    pairs = [
        (index(z, i, j, c), index(*to(z, i, j, c)))
        for z in range(nz)
        for i in range(nx)
        for j in range(ny)
        for c in range(2)
    ]
    return lax.ppermute(x, AXES, pairs)


def first(k):
    return lambda z, i, j, c: (z, i + k, j, c) if c == 0 else (z, i, j + k, c)


def second(k):
    return lambda z, i, j, c: (z, i, j + k, c) if c == 0 else (z, i + k, j, c)


def other_core(z, i, j, c):
    return (z, i, j, 1 - c)


def previous_section(z, i, j, c):
    return (z - 1, i, j, c)


def rows(*parts):
    return jnp.concatenate(parts, axis=0)


def load_weight(weight, held, sems):
    units = held.shape[0]
    copies = []
    for n, at in enumerate(range(0, units, TILE)):
        size = min(TILE, units - at)
        span = pl.ds(at, size)
        copies.append(pltpu.make_async_copy(weight.at[span, :], held.at[span, :], sems.at[n]))
    for copy in copies:
        copy.start()
    return copies


def pack(expert, token_refs, packed, gates):
    lane = lax.broadcasted_iota(jnp.int32, (16, META), 1)
    line = lax.broadcasted_iota(jnp.int32, (16, META), 0)
    pick = ((line == 0) & (lane == expert)).astype(F32).astype(BF16)
    spread = (
        lax.broadcasted_iota(jnp.int32, (META, META), 0) == EXPERTS + expert
    ).astype(F32).astype(BF16)
    at = 0
    for ref in token_refs:
        count, width = ref.shape
        width = width - META
        height = count // ROWS * CAP
        meta = ref[:, width:]
        slot = lax.dot_general(pick, meta, (((1,), (1,)), ((), ())), preferred_element_type=F32)[0:1, :]
        block = lax.broadcasted_iota(jnp.int32, (1, count), 1) // ROWS
        target = jnp.where(slot >= 0.0, slot.astype(jnp.int32) + block * CAP, -1)
        chosen = (
            lax.broadcasted_iota(jnp.int32, (height, count), 0) == target
        ).astype(F32).astype(BF16)
        for start in range(0, width, 512):
            packed[at : at + height, start : start + 512] = jnp.dot(
                chosen, ref[:, start : start + 512], preferred_element_type=F32
            ).astype(BF16)
        own = jnp.dot(chosen, meta, preferred_element_type=F32).astype(BF16)
        gates[at : at + height, :] = jnp.dot(own, spread, preferred_element_type=F32)
        at += height


def multiply(packed, held, copies, out):
    units = held.shape[0]
    for n, at in enumerate(range(0, units, TILE)):
        size = min(TILE, units - at)
        copies[n].wait()
        out[:, at : at + size] = lax.dot_general(
            packed[...],
            held[at : at + size, :],
            (((1,), (1,)), ((), ())),
            preferred_element_type=F32,
        )


def products_kernel(count, *refs):
    place = refs[0]
    tokens = refs[1 : 1 + count]
    weight, out, gates, held, packed, sems = refs[1 + count :]
    copies = load_weight(weight, held, sems)
    pack(place[3], tokens, packed, gates)
    multiply(packed, held, copies, out)


def smem():
    return pl.BlockSpec(memory_space=pltpu.SMEM)


def vmem():
    return pl.BlockSpec(memory_space=pltpu.VMEM)


def scratch(units, width, height):
    return [
        pltpu.VMEM((units, width), BF16),
        pltpu.VMEM((height, width), BF16),
        pltpu.SemaphoreType.DMA((pl.cdiv(units, TILE),)),
    ]


def cost(height, units, width):
    return pl.CostEstimate(
        flops=2 * height * units * width,
        bytes_accessed=2 * units * width + 4 * height * units,
        transcendentals=0,
    )


def products_of(place, tokens, weight):
    units, width = weight.shape
    height = sum(t.shape[0] for t in tokens) // ROWS * CAP
    return pl.pallas_call(
        functools.partial(products_kernel, len(tokens)),
        out_shape=(
            jax.ShapeDtypeStruct((height, units), F32),
            jax.ShapeDtypeStruct((height, META), F32),
        ),
        in_specs=[smem()] + [vmem()] * len(tokens) + [pl.BlockSpec(memory_space=pl.ANY)],
        out_specs=(vmem(), vmem()),
        scratch_shapes=scratch(units, width, height),
        compiler_params=pltpu.CompilerParams(vmem_limit_bytes=VMEM_LIMIT),
        cost_estimate=cost(height, units, width),
    )(place, *tokens, weight)


def last_kernel(
    place, mine, theirs, weight, hidden, near, near_gates, mid, mid_gates, out, sums,
    held, packed, sems, far, far_gates,
):
    copies = load_weight(weight, held, sems)
    pack(place[3], (mine, theirs), packed, far_gates)
    multiply(packed, held, copies, far)
    units = held.shape[0]
    core = place[2]
    diagonal = lax.broadcasted_iota(jnp.int32, (CAP, META), 0) == lax.broadcasted_iota(
        jnp.int32, (CAP, META), 1
    )

    def part(kind, along, across):
        which = jnp.where(core == kind, 0, 1)
        a = OFFSETS.index(along)
        if across == 0:
            return near, near_gates, (which * 4 + a) * CAP
        if across == 2:
            return far, far_gates, (which * 4 + a) * CAP
        return mid, mid_gates, (which * 8 + (0 if across == -1 else 4) + a) * CAP

    for i in OFFSETS:
        for j in OFFSETS:
            chip = ((place[0] + (i + 4)) % 4) * 4 + (place[1] + (j + 4)) % 4
            at = pl.multiple_of(chip * (2 * CAP), 16)
            pieces = [part(0, i, j), part(1, j, i)]
            spans = [pl.ds(pl.multiple_of(p[2], 8), CAP) for p in pieces]
            scale = jnp.concatenate([p[1][s, :] for p, s in zip(pieces, spans)], axis=0)
            total = jnp.zeros((2 * CAP, META), F32)
            for col in range(0, units, META):
                value = jnp.concatenate(
                    [p[0][s, col : col + META] for p, s in zip(pieces, spans)], axis=0
                )
                out[pl.ds(at, 2 * CAP), col : col + META] = (scale * value).astype(BF16)
                saved = hidden[pl.ds(at, 2 * CAP), col : col + META].astype(F32)
                total = total + saved * value
            total = jnp.sum(total, axis=1, keepdims=True)
            for kind in range(2):
                line = jnp.sum(
                    jnp.where(diagonal, total[kind * CAP : (kind + 1) * CAP], 0.0),
                    axis=0,
                    keepdims=True,
                )
                sums[pl.ds(chip * 2 + kind, 1), :] = line


def last_of(place, mine, theirs, weight, hidden, near, near_gates, mid, mid_gates):
    units, width = weight.shape
    height = 2 * mine.shape[0] // ROWS * CAP
    return pl.pallas_call(
        last_kernel,
        out_shape=(
            jax.ShapeDtypeStruct(hidden.shape, BF16),
            jax.ShapeDtypeStruct((hidden.shape[0] // CAP, META), F32),
        ),
        in_specs=[smem(), vmem(), vmem(), pl.BlockSpec(memory_space=pl.ANY)] + [vmem()] * 5,
        out_specs=(vmem(), vmem()),
        scratch_shapes=scratch(units, width, height)
        + [pltpu.VMEM((height, units), F32), pltpu.VMEM((height, META), F32)],
        compiler_params=pltpu.CompilerParams(vmem_limit_bytes=VMEM_LIMIT),
        cost_estimate=cost(height, units, width),
    )(place, mine, theirs, weight, hidden, near, near_gates, mid, mid_gates)


def gather_kernel(totals, ids, slots, out):
    quarter = totals.shape[0] // 4
    total = totals[0:quarter, :]
    for n in range(1, 4):
        total = total + totals[n * quarter : (n + 1) * quarter, :]
    tokens = ids.shape[0]
    lane = lax.broadcasted_iota(jnp.int32, (tokens, META), 1)
    place = lax.broadcasted_iota(jnp.int32, (tokens, TOP), 1)
    result = jnp.zeros((tokens, TOP), F32)
    for k in range(TOP):
        expert = ids[:, k : k + 1]
        line = jnp.zeros((tokens, META), F32)
        for e in range(EXPERTS):
            line = jnp.where(expert == e, total[e : e + 1, :], line)
        value = jnp.sum(jnp.where(lane == slots[:, k : k + 1], line, 0.0), axis=1, keepdims=True)
        result = jnp.where(place == k, value, result)
    out[...] = result


def on_device(handoff, expert_ids, gates, down_weight, hidden):
    dp, expert = lax.axis_index("dp"), lax.axis_index("expert")
    place = jnp.stack([dp, expert // 2, expert % 2, expert]).astype(jnp.int32)
    ids = expert_ids[0]
    weight = down_weight[0, 0]
    incoming = moved(handoff[0], previous_section)
    named = ids[:, :, None] == jnp.arange(EXPERTS, dtype=jnp.int32)
    any_named = named.any(axis=1).astype(jnp.int32)
    before = jnp.cumsum(any_named, axis=0) - any_named
    slot_map = jnp.where(any_named > 0, before, -1)
    gate_map = jnp.sum(jnp.where(named, gates[0][:, :, None].astype(F32), 0.0), axis=1)
    slots = jnp.sum(jnp.where(named, before[:, None, :], 0), axis=2)
    meta = jnp.concatenate([slot_map.astype(F32), gate_map], axis=1).astype(BF16)
    meta = jnp.pad(meta, ((0, 0), (0, META - 2 * EXPERTS)))
    own = jnp.concatenate([incoming, meta], axis=1)

    near = rows(own, *[moved(own, first(k)) for k in (1, 3, 2)])
    low, high = moved(near, second(1)), moved(near, second(3))
    half = near.shape[0] // 2
    far = rows(moved(high[:half], second(3)), moved(low[half:], second(1)))
    mid = rows(low, high)
    near_other = moved(near, other_core)
    mid_other = moved(mid, other_core)
    far_other = moved(far, other_core)
    near_products, near_gates = products_of(place, (near, near_other), weight)
    mid_products, mid_gates = products_of(place, (mid, mid_other), weight)
    hidden_grad, sums = last_of(
        place, far, far_other, weight, hidden[0, 0], near_products, near_gates, mid_products, mid_gates
    )
    totals = lax.all_to_all(sums, ("dp", "expert"), split_axis=0, concat_axis=0, tiled=True)
    gate_grad = pl.pallas_call(
        gather_kernel,
        out_shape=jax.ShapeDtypeStruct(ids.shape, F32),
        in_specs=[vmem()] * 3,
        out_specs=vmem(),
    )(totals, ids, slots)
    return (hidden_grad[None, None], gate_grad[None])


def solution(mesh):
    return jax.shard_map(
        on_device,
        mesh=mesh,
        in_specs=(
            P("pipe", ("dp", "expert"), None),
            P("pipe", ("dp", "expert"), None),
            P("pipe", ("dp", "expert"), None),
            P("pipe", "expert", "dp", None),
            P("pipe", "expert", None, "dp"),
        ),
        out_specs=(P("pipe", "expert", None, "dp"), P("pipe", ("dp", "expert"), None)),
        check_vma=False,
    )
```

time: 137 us -> 96.8 us (0.71)
  waiting for transfers between devices: 66.1 us -> 28.9 us
  Pallas kernels: 0 us -> 31.6 us
  matrix products: 13.6 us -> 0 us
  blocking collectives: 12 us -> 0 us
  starting transfers between devices: 32.5 us -> 27 us
  local copies, waits for them, and re-layouts: 10.1 us -> 5.62 us
    all_to_all x3 -> x1, waiting for transfers between devices: 62.1 us -> 5.52 us  [on_device(): lax.all_to_all(sums, ('dp', 'expert'), split_axis=0, concat_axis=0, tiled...]
    pallas_call x0 -> x4, Pallas kernels: none -> 31.6 us  [the longest x2 19.6 us: products_of(): pl.pallas_call(functools.partial(products_kernel, len(tokens)), out_shape...]
    all_to_all x3 -> x1, starting transfers between devices: 26.8 us -> 3.61 us  [on_device(): lax.all_to_all(sums, ('dp', 'expert'), split_axis=0, concat_axis=0, tiled...]
    ppermute x1 -> x11, waiting for transfers between devices: 4 us -> 23.4 us  [moved(): return lax.ppermute(x, AXES, pairs)]
    ppermute x1 -> x11, starting transfers between devices: 5.65 us -> 23.4 us  [moved(): return lax.ppermute(x, AXES, pairs)]
    dot_general x2 -> x0, matrix products: 13.6 us -> none  [the longest x1 13.1 us: on_device(): jnp.einsum(layout_form + ',efx->edjcf', arrived, down_weight[0], preferre...]
    unnamed x1 -> x0, blocking collectives: 12 us -> none
    broadcast_in_dim x3 -> x0, local copies, waits for them, and re-layouts: 3.39 us -> none  [the longest x1 2.76 us: on_device(): jnp.broadcast_to(packed, (replicas, expert_devices, local_experts, CAP, f...]
  transfers between devices with their start and end apart: 4 -> 12, of which waited for: 3 -> 7; matrix products, arithmetic and copies ran while one was open for 1% -> 6% of each run, Pallas kernels for 0% -> 20%
where the time goes in v1:
time: 96.8 us; the launch traced here: 96.3 us
  Pallas kernels  31.6 us (33%)
  waiting for transfers between devices  28.9 us (30%)
  starting transfers between devices  27 us (28%)
  local copies, waits for them, and re-layouts  5.62 us (6%)
  other arithmetic  2.4 us (2%)
    ppermute x11, waiting for transfers between devices, moved(): return lax.ppermute(x, AXES, pairs)  23.4 us
    ppermute x11, starting transfers between devices, moved(): return lax.ppermute(x, AXES, pairs)  23.4 us
    pallas_call x2, Pallas kernels, products_of(): pl.pallas_call(functools.partial(products_kernel, len(tokens)), out_shape...  19.6 us
    pallas_call x1, Pallas kernels, last_of(): pl.pallas_call(last_kernel, out_shape=(jax.ShapeDtypeStruct(hidden.shape,...  10.1 us
    all_to_all x1, waiting for transfers between devices, on_device(): lax.all_to_all(sums, ('dp', 'expert'), split_axis=0, concat_axis=0, tiled...  5.52 us
    all_to_all x1, starting transfers between devices, on_device(): lax.all_to_all(sums, ('dp', 'expert'), split_axis=0, concat_axis=0, tiled...  3.61 us
  transfers between devices with their start and end apart: 12, of which 7 were waited for; matrix products, arithmetic and copies ran while one was open for 6% of the time, Pallas kernels for 20%

profile of v1, /device:TPU:1, one launch (start us, length us, event | category | flops | bytes accessed | tf_op | source)
XLA Modules:
  0.0 96.3 jit_solution(14129925551650847673)
XLA Ops:
  0.6 6.5 %collective-permute-start = (bf16[32,3072]{1,0:T(8,128)(2,1)}, bf16[32,3072]{1,0:T(8,128)(2,1)S(1)}, u32[]{:S(2)}, u32[]{:S(2)}) collective-permute-start(bf16[32,3072]{1,0:T(8,128)(2,1)} %bitcast.28), channel_id=1, source_target_pairs={{0,224},{1,225},{2,226},{3,227},{4,228},{5,229},{6,230},{7,231},{8... | collective-permute-start | bytes 589832 | tf_op jit(solution)/shard_map/ppermute | solution.py:37
  7.1 0.7 fusion.2
  7.8 0.1 copy.23
  7.9 0.1 reduce_window_sum.11
  8.0 0.7 bitcast_convert_fusion
  8.7 0.7 select_reduce_fusion.1
  9.3 0.1 copy.24
  9.4 0.1 fusion.3
  9.5 1.5 %collective-permute-done = bf16[32,3072]{1,0:T(8,128)(2,1)S(1)} collective-permute-done((bf16[32,3072]{1,0:T(8,128)(2,1)}, bf16[32,3072]{1,0:T(8,128)(2,1)S(1)}, u32[]{:S(2)}, u32[]{:S(2)}) %collective-permute-start) | collective-permute-done | bytes 196640 | tf_op jit(solution)/shard_map/ppermute | solution.py:37
  11.0 1.4 %collective-permute-start.1 = (bf16[32,3200]{1,0:T(8,128)(2,1)S(1)}, bf16[32,3200]{1,0:T(8,128)(2,1)S(1)}, u32[]{:S(2)}, u32[]{:S(2)}) collective-permute-start(bf16[32,3200]{1,0:T(8,128)(2,1)S(1)} %pad_maximum_fusion.1), channel_id=1, source_target_pairs={{0,8},{1,3},{2,10},{3,5},{4,12},{5,7},{6,14},{7,1},{8,16},{9,11},{... | collective-permute-start | bytes 614408 | tf_op jit(solution)/shard_map/ppermute | solution.py:37
  12.4 1.5 %collective-permute-start.2 = (bf16[32,3200]{1,0:T(8,128)(2,1)S(1)}, bf16[32,3200]{1,0:T(8,128)(2,1)S(1)}, u32[]{:S(2)}, u32[]{:S(2)}) collective-permute-start(bf16[32,3200]{1,0:T(8,128)(2,1)S(1)} %pad_maximum_fusion.1), channel_id=1, source_target_pairs={{0,24},{1,7},{2,26},{3,1},{4,28},{5,3},{6,30},{7,5},{8,0},{9,15},{... | collective-permute-start | bytes 614408 | tf_op jit(solution)/shard_map/ppermute | solution.py:37
  13.9 1.6 %collective-permute-start.3 = (bf16[32,3200]{1,0:T(8,128)(2,1)S(1)}, bf16[32,3200]{1,0:T(8,128)(2,1)S(1)}, u32[]{:S(2)}, u32[]{:S(2)}) collective-permute-start(bf16[32,3200]{1,0:T(8,128)(2,1)S(1)} %pad_maximum_fusion.1), channel_id=1, source_target_pairs={{0,16},{1,5},{2,18},{3,7},{4,20},{5,1},{6,22},{7,3},{8,24},{9,13},... | collective-permute-start | bytes 614408 | tf_op jit(solution)/shard_map/ppermute | solution.py:37
  15.5 1.8 %collective-permute-done.1 = bf16[32,3200]{1,0:T(8,128)(2,1)S(1)} collective-permute-done((bf16[32,3200]{1,0:T(8,128)(2,1)S(1)}, bf16[32,3200]{1,0:T(8,128)(2,1)S(1)}, u32[]{:S(2)}, u32[]{:S(2)}) %collective-permute-start.1) | collective-permute-done | bytes 204832 | tf_op jit(solution)/shard_map/ppermute | solution.py:37
  17.3 1.5 %collective-permute-done.2 = bf16[32,3200]{1,0:T(8,128)(2,1)S(1)} collective-permute-done((bf16[32,3200]{1,0:T(8,128)(2,1)S(1)}, bf16[32,3200]{1,0:T(8,128)(2,1)S(1)}, u32[]{:S(2)}, u32[]{:S(2)}) %collective-permute-start.2) | collective-permute-done | bytes 204832 | tf_op jit(solution)/shard_map/ppermute | solution.py:37
  18.8 1.8 %collective-permute-done.3 = bf16[32,3200]{1,0:T(8,128)(2,1)S(1)} collective-permute-done((bf16[32,3200]{1,0:T(8,128)(2,1)S(1)}, bf16[32,3200]{1,0:T(8,128)(2,1)S(1)}, u32[]{:S(2)}, u32[]{:S(2)}) %collective-permute-start.3) | collective-permute-done | bytes 204832 | tf_op jit(solution)/shard_map/ppermute | solution.py:37
  20.6 0.1 pad_maximum_fusion.refs_1_
  20.7 2.6 %collective-permute-start.4 = (bf16[128,3200]{1,0:T(8,128)(2,1)S(1)}, bf16[128,3200]{1,0:T(8,128)(2,1)S(1)}, u32[]{:S(2)}, u32[]{:S(2)}) collective-permute-start(bf16[128,3200]{1,0:T(8,128)(2,1)S(1)} %pad_maximum_fusion.refs_1_), channel_id=1, source_target_pairs={{0,6},{1,25},{2,0},{3,27},{4,2},{5,29},{6,4},{7,31},{8,14},{9,1},{... | collective-permute-start | bytes 2457608 | tf_op jit(solution)/shard_map/ppermute | solution.py:37
  23.3 0.0 collective-permute-start.6
  23.3 9.3 %collective-permute-done.4 = bf16[128,3200]{1,0:T(8,128)(2,1)S(1)} collective-permute-done((bf16[128,3200]{1,0:T(8,128)(2,1)S(1)}, bf16[128,3200]{1,0:T(8,128)(2,1)S(1)}, u32[]{:S(2)}, u32[]{:S(2)}) %collective-permute-start.4) | collective-permute-done | bytes 819232 | tf_op jit(solution)/shard_map/ppermute | solution.py:37
  32.6 3.5 %collective-permute-start.5 = (bf16[64,3200]{1,0:T(8,128)(2,1)S(1)}, bf16[64,3200]{1,0:T(8,128)(2,1)S(1)}, u32[]{:S(2)}, u32[]{:S(2)}) collective-permute-start(bf16[64,3200]{1,0:T(8,128)(2,1)S(1)} %slice.8), channel_id=1, source_target_pairs={{0,6},{1,25},{2,0},{3,27},{4,2},{5,29},{6,4},{7,31},{8,14},{9,1},{... | collective-permute-start | bytes 1228808 | tf_op jit(solution)/shard_map/ppermute | solution.py:37
  36.1 0.0 collective-permute-done.6
  36.1 0.9 constant_dynamic-update-slice_fusion.3
  37.0 0.9 constant_dynamic-update-slice_fusion.2.refs_1_
  38.0 3.9 %collective-permute-start.10 = (bf16[256,3200]{1,0:T(8,128)(2,1)}, bf16[256,3200]{1,0:T(8,128)(2,1)}, u32[]{:S(2)}, u32[]{:S(2)}) collective-permute-start(bf16[256,3200]{1,0:T(8,128)(2,1)} %constant_dynamic-update-slice_fusion.2.refs_1_), channel_id=1, source_target_pairs={{0,1},{1,0},{2,3},{3,2},{4,5},{5,4},{6,7},{7,6},{8,9},{9,8},{10,11... | collective-permute-start | bytes 4915208 | tf_op jit(solution)/shard_map/ppermute | solution.py:37
  41.9 0.0 collective-permute-start.9
  41.9 0.9 collective-permute-start.7
  42.8 0.0 collective-permute-done.5
  42.8 7.5 %collective-permute-done.7 = bf16[64,3200]{1,0:T(8,128)(2,1)S(1)} collective-permute-done((bf16[64,3200]{1,0:T(8,128)(2,1)S(1)}, bf16[64,3200]{1,0:T(8,128)(2,1)S(1)}, u32[]{:S(2)}, u32[]{:S(2)}) %collective-permute-start.7) | collective-permute-done | bytes 409632 | tf_op jit(solution)/shard_map/ppermute | solution.py:37
  50.3 1.6 %collective-permute-start.8 = (bf16[128,3200]{1,0:T(8,128)(2,1)S(1)}, bf16[128,3200]{1,0:T(8,128)(2,1)S(1)}, u32[]{:S(2)}, u32[]{:S(2)}) collective-permute-start(bf16[128,3200]{1,0:T(8,128)(2,1)S(1)} %constant_dynamic-update-slice_fusion.mine), channel_id=1, source_target_pairs={{0,1},{1,0},{2,3},{3,2},{4,5},{5,4},{6,7},{7,6},{8,9},{9,8},{10,11... | collective-permute-start | bytes 2457608 | tf_op jit(solution)/shard_map/ppermute | solution.py:37
  52.0 0.1 copy.26
  52.0 0.1 pad_add_fusion.refs_0_.place
  52.1 0.0 collective-permute-done.9.refs_2_
  52.1 7.7 %shard_map.68 = (f32[192,1408]{1,0:T(8,128)S(1)}, f32[192,128]{1,0:T(8,128)S(1)}) custom-call(s32[4]{0:T(128)S(1)} %pad_add_fusion.refs_0_.place, bf16[128,3200]{1,0:T(8,128)(2,1)S(1)} %pad_maximum_fusion.refs_1_, bf16[128,3200]{1,0:T(8,128)(2,1)S(1)} %collective-permute-done.9.refs_2_, bf16[1408,3072]{1,0:T(8,128)(2,1)} %bitcast.18), custom_call_target="tpu_custom_call" | custom-call | flops 1660944384 | bytes 9732096 | tf_op jit(solution)/shard_map/pallas_call | solution.py:149
  59.8 0.0 copy-start
  59.9 0.0 collective-permute-done.10.refs_2_
  59.9 11.9 %shard_map.69 = (f32[384,1408]{1,0:T(8,128)S(1)}, f32[384,128]{1,0:T(8,128)S(1)}) custom-call(s32[4]{0:T(128)S(1)} %pad_add_fusion.refs_0_.place, bf16[256,3200]{1,0:T(8,128)(2,1)} %constant_dynamic-update-slice_fusion.2.refs_1_, bf16[256,3200]{1,0:T(8,128)(2,1)} %collective-permute-done.10.refs_2_, bf16[1408,3072]{1,0:T(8,128)(2,1)} %bitcast.19), custom_call_target="tpu_custom_call" | custom-call | flops 3321888768 | bytes 10813440 | tf_op jit(solution)/shard_map/pallas_call | solution.py:149
  71.8 0.0 collective-permute-done.8.theirs
  71.8 0.0 copy-done
  71.8 0.0 copy-start.2
  71.8 10.1 %shard_map.70 = (bf16[768,1408]{1,0:T(8,128)(2,1)}, f32[32,128]{1,0:T(8,128)}) custom-call(s32[4]{0:T(128)S(1)} %pad_add_fusion.refs_0_.place, bf16[128,3200]{1,0:T(8,128)(2,1)S(1)} %constant_dynamic-update-slice_fusion.mine, bf16[128,3200]{1,0:T(8,128)(2,1)S(1)} %collective-permute-done.8.theirs, bf16[1408,3072]{1,0:T(8,128)(2,1)} %bitcast.20, ...), custom_call_target="tpu_custom_call" | custom-call | flops 1660944384 | bytes 9732096 | tf_op jit(solution)/shard_map/pallas_call | solution.py:213
  81.9 3.6 %all-to-all-start = ((f32[32,1,128]{2,1,0:T(1,128)}), f32[32,1,128]{2,1,0:T(1,128)S(1)}, u32[]{:S(2)}, u32[]{:S(2)}) async-start(f32[32,1,128]{2,1,0:T(1,128)} %bitcast.11), calls=%async_computation | async-start | bytes 32768 | tf_op jit(solution)/shard_map/all_to_all | solution.py:276
  85.5 0.0 copy-done.2
  85.6 0.7 copy.27.ids
  86.3 0.7 copy.28.slots
  86.9 5.5 %all-to-all-done = f32[32,1,128]{2,1,0:T(1,128)S(1)} async-done(((f32[32,1,128]{2,1,0:T(1,128)}), f32[32,1,128]{2,1,0:T(1,128)S(1)}, u32[]{:S(2)}, u32[]{:S(2)}) %all-to-all-start) | async-done | bytes 16416 | tf_op jit(solution)/shard_map/all_to_all | solution.py:276
  92.5 0.6 copy-done.1
  93.1 1.9 %shard_map.71 = f32[32,4]{1,0:T(8,128)} custom-call(f32[32,128]{1,0:T(8,128)} %bitcast.21, s32[32,4]{1,0:T(8,128)} %copy.27.ids, s32[32,4]{1,0:T(8,128)} %copy.28.slots), custom_call_target="tpu_custom_call" | custom-call | tf_op jit(solution)/shard_map/pallas_call | solution.py:277
  95.0 1.4 %copy.29 = f32[32,4]{0,1:T(4,128)} copy(f32[32,4]{1,0:T(8,128)} %shard_map.71) | data formatting | bytes 1024 | tf_op jit(solution)/shard_map/pallas_call | solution.py:277
  (9 shorter events, 0.2 us)
Async XLA Ops:
  0.6 10.4 %collective-permute-start = (bf16[32,3072]{1,0:T(8,128)(2,1)}, bf16[32,3072]{1,0:T(8,128)(2,1)S(1)}, u32[]{:S(2)}, u32[]{:S(2)}) collective-permute-start(bf16[32,3072]{1,0:T(8,128)(2,1)} %bitcast.28), channel_id=1, source_target_pairs={{0,224},{1,225},{2,226},{3,227},{4,228},{5,229},{6,230},{7,231},{8... | collective-permute-start | bytes 589832 | tf_op jit(solution)/shard_map/ppermute | solution.py:37
  11.0 6.3 %collective-permute-start.1 = (bf16[32,3200]{1,0:T(8,128)(2,1)S(1)}, bf16[32,3200]{1,0:T(8,128)(2,1)S(1)}, u32[]{:S(2)}, u32[]{:S(2)}) collective-permute-start(bf16[32,3200]{1,0:T(8,128)(2,1)S(1)} %pad_maximum_fusion.1), channel_id=1, source_target_pairs={{0,8},{1,3},{2,10},{3,5},{4,12},{5,7},{6,14},{7,1},{8,16},{9,11},{... | collective-permute-start | bytes 614408 | tf_op jit(solution)/shard_map/ppermute | solution.py:37
  12.4 6.4 %collective-permute-start.2 = (bf16[32,3200]{1,0:T(8,128)(2,1)S(1)}, bf16[32,3200]{1,0:T(8,128)(2,1)S(1)}, u32[]{:S(2)}, u32[]{:S(2)}) collective-permute-start(bf16[32,3200]{1,0:T(8,128)(2,1)S(1)} %pad_maximum_fusion.1), channel_id=1, source_target_pairs={{0,24},{1,7},{2,26},{3,1},{4,28},{5,3},{6,30},{7,5},{8,0},{9,15},{... | collective-permute-start | bytes 614408 | tf_op jit(solution)/shard_map/ppermute | solution.py:37
  13.9 6.7 %collective-permute-start.3 = (bf16[32,3200]{1,0:T(8,128)(2,1)S(1)}, bf16[32,3200]{1,0:T(8,128)(2,1)S(1)}, u32[]{:S(2)}, u32[]{:S(2)}) collective-permute-start(bf16[32,3200]{1,0:T(8,128)(2,1)S(1)} %pad_maximum_fusion.1), channel_id=1, source_target_pairs={{0,16},{1,5},{2,18},{3,7},{4,20},{5,1},{6,22},{7,3},{8,24},{9,13},... | collective-permute-start | bytes 614408 | tf_op jit(solution)/shard_map/ppermute | solution.py:37
  20.7 11.8 %collective-permute-start.4 = (bf16[128,3200]{1,0:T(8,128)(2,1)S(1)}, bf16[128,3200]{1,0:T(8,128)(2,1)S(1)}, u32[]{:S(2)}, u32[]{:S(2)}) collective-permute-start(bf16[128,3200]{1,0:T(8,128)(2,1)S(1)} %pad_maximum_fusion.refs_1_), channel_id=1, source_target_pairs={{0,6},{1,25},{2,0},{3,27},{4,2},{5,29},{6,4},{7,31},{8,14},{9,1},{... | collective-permute-start | bytes 2457608 | tf_op jit(solution)/shard_map/ppermute | solution.py:37
  23.3 12.8 %collective-permute-start.6 = (bf16[128,3200]{1,0:T(8,128)(2,1)S(1)}, bf16[128,3200]{1,0:T(8,128)(2,1)S(1)}, u32[]{:S(2)}, u32[]{:S(2)}) collective-permute-start(bf16[128,3200]{1,0:T(8,128)(2,1)S(1)} %pad_maximum_fusion.refs_1_), channel_id=1, source_target_pairs={{0,2},{1,9},{2,4},{3,11},{4,6},{5,13},{6,0},{7,15},{8,10},{9,17},{... | collective-permute-start | bytes 2457608 | tf_op jit(solution)/shard_map/ppermute | solution.py:37
  32.6 10.2 %collective-permute-start.5 = (bf16[64,3200]{1,0:T(8,128)(2,1)S(1)}, bf16[64,3200]{1,0:T(8,128)(2,1)S(1)}, u32[]{:S(2)}, u32[]{:S(2)}) collective-permute-start(bf16[64,3200]{1,0:T(8,128)(2,1)S(1)} %slice.8), channel_id=1, source_target_pairs={{0,6},{1,25},{2,0},{3,27},{4,2},{5,29},{6,4},{7,31},{8,14},{9,1},{... | collective-permute-start | bytes 1228808 | tf_op jit(solution)/shard_map/ppermute | solution.py:37
  38.0 21.9 %collective-permute-start.10 = (bf16[256,3200]{1,0:T(8,128)(2,1)}, bf16[256,3200]{1,0:T(8,128)(2,1)}, u32[]{:S(2)}, u32[]{:S(2)}) collective-permute-start(bf16[256,3200]{1,0:T(8,128)(2,1)} %constant_dynamic-update-slice_fusion.2.refs_1_), channel_id=1, source_target_pairs={{0,1},{1,0},{2,3},{3,2},{4,5},{5,4},{6,7},{7,6},{8,9},{9,8},{10,11... | collective-permute-start | bytes 4915208 | tf_op jit(solution)/shard_map/ppermute | solution.py:37
  41.9 10.2 %collective-permute-start.9 = (bf16[128,3200]{1,0:T(8,128)(2,1)S(1)}, bf16[128,3200]{1,0:T(8,128)(2,1)S(1)}, u32[]{:S(2)}, u32[]{:S(2)}) collective-permute-start(bf16[128,3200]{1,0:T(8,128)(2,1)S(1)} %pad_maximum_fusion.refs_1_), channel_id=1, source_target_pairs={{0,1},{1,0},{2,3},{3,2},{4,5},{5,4},{6,7},{7,6},{8,9},{9,8},{10,11... | collective-permute-start | bytes 2457608 | tf_op jit(solution)/shard_map/ppermute | solution.py:37
  41.9 8.4 %collective-permute-start.7 = (bf16[64,3200]{1,0:T(8,128)(2,1)S(1)}, bf16[64,3200]{1,0:T(8,128)(2,1)S(1)}, u32[]{:S(2)}, u32[]{:S(2)}) collective-permute-start(bf16[64,3200]{1,0:T(8,128)(2,1)S(1)} %slice.9), channel_id=1, source_target_pairs={{0,2},{1,9},{2,4},{3,11},{4,6},{5,13},{6,0},{7,15},{8,10},{9,17},{... | collective-permute-start | bytes 1228808 | tf_op jit(solution)/shard_map/ppermute | solution.py:37
  50.3 21.5 %collective-permute-start.8 = (bf16[128,3200]{1,0:T(8,128)(2,1)S(1)}, bf16[128,3200]{1,0:T(8,128)(2,1)S(1)}, u32[]{:S(2)}, u32[]{:S(2)}) collective-permute-start(bf16[128,3200]{1,0:T(8,128)(2,1)S(1)} %constant_dynamic-update-slice_fusion.mine), channel_id=1, source_target_pairs={{0,1},{1,0},{2,3},{3,2},{4,5},{5,4},{6,7},{7,6},{8,9},{9,8},{10,11... | collective-permute-start | bytes 2457608 | tf_op jit(solution)/shard_map/ppermute | solution.py:37
  59.8 11.9 %copy-start = (bf16[1,1,768,1408]{3,2,1,0:T(8,128)(2,1)S(1)}, bf16[1,1,768,1408]{3,2,1,0:T(8,128)(2,1)}, u32[]{:S(2)}) copy-start(bf16[1,1,768,1408]{3,2,1,0:T(8,128)(2,1)} %param.9) | copy-start | bytes 6488068
  71.8 13.7 %copy-start.2 = (s32[1,32,4]{1,2,0:T(4,128)S(1)}, s32[1,32,4]{1,2,0:T(4,128)}, u32[]{:S(2)}) copy-start(s32[1,32,4]{1,2,0:T(4,128)} %param.6) | copy-start | bytes 1540
  81.9 10.5 %all-to-all-start = ((f32[32,1,128]{2,1,0:T(1,128)}), f32[32,1,128]{2,1,0:T(1,128)S(1)}, u32[]{:S(2)}, u32[]{:S(2)}) async-start(f32[32,1,128]{2,1,0:T(1,128)} %bitcast.11), calls=%async_computation | async-start | bytes 32768 | tf_op jit(solution)/shard_map/all_to_all | solution.py:276
  92.5 0.6 copy-start.1

commit v2 on v1

v2 whole, which is shorter than its diff:
```python
import jax
import jax.numpy as jnp
from jax import lax
from jax.experimental import pallas as pl
from jax.experimental.pallas import tpu as pltpu
from jax.sharding import PartitionSpec as P

EXPERTS = 8
TOP = 4
CAP = 24
ROWS = 32
META = 128
TILE = 256
OFFSETS = (0, -1, 1, 2)
HALVES = tuple((0, 2, j) for j in (0, -1, 1)) + tuple((1, i, 2) for i in (0, -1, 1))
AXES = ("pipe", "dp", "expert")
VMEM_LIMIT = 20
F32 = jnp.float32
BF16 = jnp.bfloat16


def moved(x, to):
    nz, nx, ne = (lax.axis_size(a) for a in AXES)
    ny = ne // 2

    def index(z, i, j, c):
        return ((z % nz) * nx + i % nx) * ne + (j % ny) * 2 + c

    pairs = [
        (index(z, i, j, c), index(*to(z, i, j, c)))
        for z in range(nz)
        for i in range(nx)
        for j in range(ny)
        for c in range(2)
    ]
    return lax.ppermute(x, AXES, pairs)


def first(k):
    return lambda z, i, j, c: (z, i + k, j, c) if c == 0 else (z, i, j + k, c)


def second(k):
    return lambda z, i, j, c: (z, i, j + k, c) if c == 0 else (z, i + k, j, c)


def other_core(z, i, j, c):
    return (z, i, j, 1 - c)


def previous_section(z, i, j, c):
    return (z - 1, i, j, c)


def rows(*parts):
    return jnp.concatenate(parts, axis=0)


def pack(expert, token_refs, packed, gates):
    lane = lax.broadcasted_iota(jnp.int32, (16, META), 1)
    line = lax.broadcasted_iota(jnp.int32, (16, META), 0)
    pick = ((line == 0) & (lane == expert)).astype(F32).astype(BF16)
    spread = (
        lax.broadcasted_iota(jnp.int32, (META, META), 0) == EXPERTS + expert
    ).astype(F32).astype(BF16)
    at = 0
    for ref in token_refs:
        count, width = ref.shape
        width = width - META
        height = count // ROWS * CAP
        meta = ref[:, width:]
        slot = lax.dot_general(pick, meta, (((1,), (1,)), ((), ())), preferred_element_type=F32)[0:1, :]
        block = lax.broadcasted_iota(jnp.int32, (1, count), 1) // ROWS
        target = jnp.where(slot >= 0.0, slot.astype(jnp.int32) + block * CAP, -1)
        chosen = (
            lax.broadcasted_iota(jnp.int32, (height, count), 0) == target
        ).astype(F32).astype(BF16)
        for start in range(0, width, 512):
            packed[at : at + height, start : start + 512] = jnp.dot(
                chosen, ref[:, start : start + 512], preferred_element_type=F32
            ).astype(BF16)
        own = jnp.dot(chosen, meta, preferred_element_type=F32).astype(BF16)
        gates[at : at + height, :] = jnp.dot(own, spread, preferred_element_type=F32)
        at += height


def multiply(packed, turned, out):
    units = turned.shape[1]
    for at in range(0, units, TILE):
        size = min(TILE, units - at)
        out[:, at : at + size] = jnp.dot(
            packed[...], turned[:, at : at + size], preferred_element_type=F32
        )


def smem():
    return pl.BlockSpec(memory_space=pltpu.SMEM)


def vmem():
    return pl.BlockSpec(memory_space=pltpu.VMEM)


def anywhere():
    return pl.BlockSpec(memory_space=pl.ANY)


def params(mebibytes=VMEM_LIMIT):
    return pltpu.CompilerParams(vmem_limit_bytes=mebibytes << 20)


def cost(height, units, width):
    return pl.CostEstimate(
        flops=2 * height * units * width,
        bytes_accessed=2 * units * width + 4 * height * units,
        transcendentals=0,
    )


def meta_kernel(place, ids, gates, meta, lines, spot):
    for n in range(4):
        spot[n] = place[n]
    tokens = ids.shape[1]
    expert = lax.broadcasted_iota(jnp.int32, (EXPERTS, tokens), 0)
    named = [ids[k : k + 1, :] == expert for k in range(TOP)]
    some = jnp.zeros((EXPERTS, tokens), F32)
    gate = jnp.zeros((EXPERTS, tokens), F32)
    weights = gates[...].astype(F32)
    for k in range(TOP):
        some = jnp.where(named[k], 1.0, some)
        gate = jnp.where(named[k], weights[k : k + 1, :], gate)
    row = lax.broadcasted_iota(jnp.int32, (tokens, tokens), 0)
    col = lax.broadcasted_iota(jnp.int32, (tokens, tokens), 1)
    earlier = (row < col).astype(F32).astype(BF16)
    before = jnp.dot(some.astype(BF16), earlier, preferred_element_type=F32)
    slot = jnp.where(some > 0.0, before, -1.0)
    lines[...] = jnp.zeros(lines.shape, jnp.int32)
    for k in range(TOP):
        own = jnp.sum(jnp.where(named[k], before, 0.0), axis=0, keepdims=True)
        lines[0:1, k * tokens : (k + 1) * tokens] = own.astype(jnp.int32)
        lines[1:2, k * tokens : (k + 1) * tokens] = ids[k : k + 1, :]
    table = jnp.concatenate(
        [slot, gate, jnp.zeros((META - 2 * EXPERTS, tokens), F32)], axis=0
    ).astype(BF16)
    unit = (row == col).astype(F32).astype(BF16)
    meta[...] = lax.dot_general(
        unit, table, (((1,), (1,)), ((), ())), preferred_element_type=F32
    ).astype(BF16)


def meta_of(place, ids, gates):
    return pl.pallas_call(
        meta_kernel,
        out_shape=(
            jax.ShapeDtypeStruct((ids.shape[1], META), BF16),
            jax.ShapeDtypeStruct((8, META), jnp.int32),
            jax.ShapeDtypeStruct((4,), jnp.int32),
        ),
        in_specs=[smem(), vmem(), vmem()],
        out_specs=(vmem(), vmem(), smem()),
        compiler_params=params(2),
    )(place, ids, gates)


def join_kernel(*refs):
    at = 0
    for ref in refs[:-1]:
        refs[-1][at : at + ref.shape[0], :] = ref[...]
        at += ref.shape[0]


def join(*parts):
    shape = (sum(p.shape[0] for p in parts), parts[0].shape[1])
    return pl.pallas_call(
        join_kernel,
        out_shape=pltpu.VMEM(shape, parts[0].dtype),
        in_specs=[vmem()] * len(parts),
        out_specs=vmem(),
        compiler_params=params(6),
    )(*parts)


def turn_kernel(place, weight, turned, held, sems):
    units, width = weight.shape
    copies = [
        pltpu.make_async_copy(
            weight.at[pl.ds(at, META), :], held.at[pl.ds(at, META), :], sems.at[at // META]
        )
        for at in range(0, units, META)
    ]
    for copy in copies:
        copy.start()
    for copy, at in zip(copies, range(0, units, META)):
        copy.wait()
        for col in range(0, width, 512):
            turned[col : col + 512, at : at + META] = held[at : at + META, col : col + 512].T


def turn(place, weight):
    units, width = weight.shape
    return pl.pallas_call(
        turn_kernel,
        out_shape=pltpu.VMEM((width, units), BF16),
        in_specs=[smem(), anywhere()],
        out_specs=vmem(),
        scratch_shapes=[
            pltpu.VMEM((units, width), BF16),
            pltpu.SemaphoreType.DMA((units // META,)),
        ],
        compiler_params=params(),
        cost_estimate=pl.CostEstimate(
            flops=0, bytes_accessed=4 * units * width, transcendentals=0
        ),
    )(place, pltpu.with_memory_space_constraint(weight, pltpu.HBM))


def near_kernel(place, mine, theirs, turned, out, gates, packed):
    pack(place[3], (mine, theirs), packed, gates)
    multiply(packed, turned, out)


def near_of(place, mine, theirs, turned):
    width, units = turned.shape
    height = 2 * mine.shape[0] // ROWS * CAP
    return pl.pallas_call(
        near_kernel,
        out_shape=(pltpu.VMEM((height, units), F32), pltpu.VMEM((height, META), F32)),
        in_specs=[smem()] + [vmem()] * 3,
        out_specs=(vmem(), vmem()),
        scratch_shapes=[pltpu.VMEM((height, width), BF16)],
        compiler_params=params(),
        cost_estimate=cost(height, units, width),
    )(place, mine, theirs, turned)


def chip_of(place, i, j):
    return ((place[0] + (i + 4)) % 4) * 4 + (place[1] + (j + 4)) % 4


def pair_rows(chip):
    return pl.ds(pl.multiple_of(chip * (2 * CAP), 16), 2 * CAP)


def block_rows(place, kind, group, along):
    which = jnp.where(place[2] == kind, 0, 1)
    return pl.ds(pl.multiple_of((which * group + along) * CAP, 8), CAP)


def finish(chip, pieces, saved, sums, write):
    diagonal = lax.broadcasted_iota(jnp.int32, (CAP, META), 0) == lax.broadcasted_iota(
        jnp.int32, (CAP, META), 1
    )
    scales = [None if p is None or p[1] is None else p[1][p[2], :] for p in pieces]
    totals = [jnp.zeros((CAP, META), F32) for _ in pieces]
    for col in range(0, saved.shape[1], META):
        span = slice(col, col + META)
        factor = saved[pair_rows(chip), span].astype(F32)
        scaled = []
        for kind, piece in enumerate(pieces):
            if piece is None:
                scaled.append(None)
                continue
            value = piece[0][piece[2], span]
            if scales[kind] is not None:
                totals[kind] += factor[kind * CAP : (kind + 1) * CAP] * value
                value = scales[kind] * value
            scaled.append(value)
        write(span, scaled)
    for kind, scale in enumerate(scales):
        if scale is not None:
            total = jnp.sum(totals[kind], axis=1, keepdims=True)
            sums[pl.ds(chip * 2 + kind, 1), :] = jnp.sum(
                jnp.where(diagonal, total, 0.0), axis=0, keepdims=True
            )


def staged(stage, slot):
    def write(span, scaled):
        stage[slot, :, span] = jnp.concatenate(scaled, axis=0).astype(BF16)

    return write


def mid_kernel(
    place, mine, theirs, turned, hidden, near, near_gates,
    grad, sums, halves, packed, mid, mid_gates, stage, sems,
):
    pack(place[3], (mine, theirs), packed, mid_gates)
    multiply(packed, turned, mid)

    def piece(kind, along, across):
        a = OFFSETS.index(along)
        if across == 0:
            return near, near_gates, block_rows(place, kind, 4, a)
        return mid, mid_gates, block_rows(place, kind, 8, (0 if across == -1 else 4) + a)

    copies = []
    for i in (0, -1, 1):
        for j in (0, -1, 1):
            chip, slot = chip_of(place, i, j), len(copies)
            finish(chip, (piece(0, i, j), piece(1, j, i)), hidden, sums, staged(stage, slot))
            copy = pltpu.make_async_copy(stage.at[slot], grad.at[pair_rows(chip), :], sems.at[slot])
            copy.start()
            copies.append(copy)
    for n, (kind, i, j) in enumerate(HALVES):
        def write(span, scaled, kind=kind, n=n):
            halves[n * CAP : (n + 1) * CAP, span] = scaled[kind]

        pieces = (piece(0, i, j), None) if kind == 0 else (None, piece(1, j, i))
        finish(chip_of(place, i, j), pieces, hidden, sums, write)
    for copy in copies:
        copy.wait()


def mid_of(place, mine, theirs, turned, hidden, near, near_gates):
    width, units = turned.shape
    height = 2 * mine.shape[0] // ROWS * CAP
    return pl.pallas_call(
        mid_kernel,
        out_shape=(
            jax.ShapeDtypeStruct(hidden.shape, BF16),
            pltpu.VMEM((hidden.shape[0] // CAP, META), F32),
            pltpu.VMEM((len(HALVES) * CAP, units), F32),
        ),
        in_specs=[smem()] + [vmem()] * 6,
        out_specs=(anywhere(), vmem(), vmem()),
        scratch_shapes=[
            pltpu.VMEM((height, width), BF16),
            pltpu.VMEM((height, units), F32),
            pltpu.VMEM((height, META), F32),
            pltpu.VMEM((9, 2 * CAP, units), BF16),
            pltpu.SemaphoreType.DMA((9,)),
        ],
        compiler_params=params(),
        cost_estimate=cost(height, units, width),
    )(place, mine, theirs, turned, hidden, near, near_gates)


def far_kernel(
    place, mine, theirs, turned, hidden, halves, early, _, grad, sums,
    packed, far, far_gates, stage, sems,
):
    sums[...] = early[...]
    pack(place[3], (mine, theirs), packed, far_gates)
    multiply(packed, turned, far)
    copies = []
    for i in OFFSETS:
        for j in OFFSETS:
            if i != 2 and j != 2:
                continue
            pieces = []
            for kind, along, across in ((0, i, j), (1, j, i)):
                if across == 2:
                    rows_of = block_rows(place, kind, 4, OFFSETS.index(along))
                    pieces.append((far, far_gates, rows_of))
                else:
                    n = HALVES.index((kind, i, j))
                    pieces.append((halves, None, pl.ds(n * CAP, CAP)))
            chip, slot = chip_of(place, i, j), len(copies)
            finish(chip, pieces, hidden, sums, staged(stage, slot))
            copy = pltpu.make_async_copy(stage.at[slot], grad.at[pair_rows(chip), :], sems.at[slot])
            copy.start()
            copies.append(copy)
    for copy in copies:
        copy.wait()


def far_of(place, mine, theirs, turned, hidden, halves, early, grad):
    width, units = turned.shape
    height = 2 * mine.shape[0] // ROWS * CAP
    return pl.pallas_call(
        far_kernel,
        out_shape=(
            jax.ShapeDtypeStruct(grad.shape, BF16),
            pltpu.VMEM(early.shape, F32),
        ),
        in_specs=[smem()] + [vmem()] * 6 + [anywhere()],
        out_specs=(anywhere(), vmem()),
        scratch_shapes=[
            pltpu.VMEM((height, width), BF16),
            pltpu.VMEM((height, units), F32),
            pltpu.VMEM((height, META), F32),
            pltpu.VMEM((7, 2 * CAP, units), BF16),
            pltpu.SemaphoreType.DMA((7,)),
        ],
        input_output_aliases={7: 0},
        compiler_params=params(),
        cost_estimate=cost(height, units, width),
    )(place, mine, theirs, turned, hidden, halves, early, grad)


def gather_kernel(totals, lines, out):
    quarter = totals.shape[0] // 4
    total = totals[0:quarter, :]
    for n in range(1, 4):
        total = total + totals[n * quarter : (n + 1) * quarter, :]
    pick = (lax.broadcasted_iota(jnp.int32, (META, META), 0) == lines[0:1, :]).astype(F32)
    line = jnp.dot(total, pick, precision=lax.Precision.HIGHEST, preferred_element_type=F32)
    chosen = lax.broadcasted_iota(jnp.int32, line.shape, 0) == lines[1:2, :]
    line = jnp.sum(jnp.where(chosen, line, 0.0), axis=0, keepdims=True)
    tokens = out.shape[1]
    for k in range(TOP):
        out[k : k + 1, :] = line[:, k * tokens : (k + 1) * tokens]


def on_device(handoff, expert_ids, gates, down_weight, hidden):
    dp, expert = lax.axis_index("dp"), lax.axis_index("expert")
    place = jnp.stack([dp, expert // 2, expert % 2, expert]).astype(jnp.int32)
    ids = expert_ids[0].T
    incoming = moved(handoff[0], previous_section)
    meta, lines, place = meta_of(place, ids, gates[0].T)
    own = jnp.concatenate([incoming, meta], axis=1)
    own, lines, place = lax.optimization_barrier((own, lines, place))

    ahead, back, across = [moved(own, first(k)) for k in (1, 3, 2)]
    ahead, back, across = lax.optimization_barrier((ahead, back, across))
    near = rows(own, ahead), rows(back, across)
    high = [moved(near[0], second(3)), None]
    low = [None, moved(near[1], second(1))]
    low[0] = moved(near[0], second(1))
    high[1] = moved(near[1], second(3))
    near = rows(*near)
    near, later = lax.optimization_barrier((near, place))
    turned = turn(later, down_weight[0, 0])
    near_other = moved(near, other_core)
    near_products, near_gates = near_of(place, near, near_other, turned)
    high[0], low[1], near_products, near_gates = lax.optimization_barrier(
        (high[0], low[1], near_products, near_gates)
    )
    far = moved(high[0], second(3)), moved(low[1], second(1))
    mid = join(*low, *high)
    mid_other = moved(mid, other_core)
    grad, sums, halves = mid_of(
        place, mid, mid_other, turned, hidden[0, 0], near_products, near_gates
    )
    far, grad, sums, halves = lax.optimization_barrier((far, grad, sums, halves))
    far = join(*far)
    far_other = moved(far, other_core)
    grad, sums = far_of(place, far, far_other, turned, hidden[0, 0], halves, sums, grad)
    totals = lax.all_to_all(sums, ("dp", "expert"), split_axis=0, concat_axis=0, tiled=True)
    gate_grad = pl.pallas_call(
        gather_kernel,
        out_shape=jax.ShapeDtypeStruct(ids.shape, F32),
        in_specs=[vmem()] * 2,
        out_specs=vmem(),
        compiler_params=params(2),
    )(totals, lines)
    return (grad[None, None], gate_grad.T[None])


def solution(mesh):
    return jax.shard_map(
        on_device,
        mesh=mesh,
        in_specs=(
            P("pipe", ("dp", "expert"), None),
            P("pipe", ("dp", "expert"), None),
            P("pipe", ("dp", "expert"), None),
            P("pipe", "expert", "dp", None),
            P("pipe", "expert", None, "dp"),
        ),
        out_specs=(P("pipe", "expert", None, "dp"), P("pipe", ("dp", "expert"), None)),
        check_vma=False,
    )
```

time: 96.8 us -> 69.1 us (0.71)
  waiting for transfers between devices: 28.9 us -> 11.3 us
  Pallas kernels: 31.6 us -> 21.5 us
  blocking collectives: 0 us -> 10 us
  local copies, waits for them, and re-layouts: 5.62 us -> 1.44 us
  starting transfers between devices: 27 us -> 23.7 us
  other arithmetic: 2.4 us -> 0.15 us
    ppermute x11 -> x13, waiting for transfers between devices: 23.4 us -> 11.3 us  [moved(): return lax.ppermute(x, AXES, pairs)]
    all_to_all x0 -> x1, blocking collectives: none -> 10 us  [on_device(): lax.all_to_all(sums, ('dp', 'expert'), split_axis=0, concat_axis=0, tiled...]
    pallas_call x3 -> x7, Pallas kernels: 29.7 us -> 20.7 us  [the longest x1 6.79 us: mid_of(): pl.pallas_call(mid_kernel, out_shape=(jax.ShapeDtypeStruct(hidden.shape,...]
    all_to_all x1 -> x0, waiting for transfers between devices: 5.52 us -> none  [on_device(): lax.all_to_all(sums, ('dp', 'expert'), split_axis=0, concat_axis=0, tiled...]
    all_to_all x1 -> x0, starting transfers between devices: 3.61 us -> none  [on_device(): lax.all_to_all(sums, ('dp', 'expert'), split_axis=0, concat_axis=0, tiled...]
    pallas_call x1 -> x0, local copies, waits for them, and re-layouts: 1.37 us -> none  [on_device(): pl.pallas_call(gather_kernel, out_shape=jax.ShapeDtypeStruct(ids.shape, F...]
    pallas_call x1, Pallas kernels: 1.89 us -> 0.82 us  [on_device(): pl.pallas_call(gather_kernel, out_shape=jax.ShapeDtypeStruct(ids.shape, F...]
    ppermute x11 -> x13, starting transfers between devices: 23.4 us -> 23.7 us  [moved(): return lax.ppermute(x, AXES, pairs)]
  transfers between devices with their start and end apart: 12 -> 13, of which waited for: 7 -> 7; matrix products, arithmetic and copies ran while one was open for 6% -> 0% of each run, Pallas kernels for 20% -> 23%
where the time goes in v2:
time: 69.1 us; the launch traced here: 69 us
  starting transfers between devices  23.7 us (34%)
  Pallas kernels  21.5 us (31%)
  waiting for transfers between devices  11.3 us (16%)
  blocking collectives  10 us (14%)
  local copies, waits for them, and re-layouts  1.44 us (2%)
  between operations  0.76 us (1%)
    ppermute x13, starting transfers between devices, moved(): return lax.ppermute(x, AXES, pairs)  23.7 us
    ppermute x13, waiting for transfers between devices, moved(): return lax.ppermute(x, AXES, pairs)  11.3 us
    all_to_all x1, blocking collectives, on_device(): lax.all_to_all(sums, ('dp', 'expert'), split_axis=0, concat_axis=0, tiled...  10 us
    pallas_call x1, Pallas kernels, mid_of(): pl.pallas_call(mid_kernel, out_shape=(jax.ShapeDtypeStruct(hidden.shape,...  6.79 us
    pallas_call x1, Pallas kernels, turn(): pl.pallas_call(turn_kernel, out_shape=pltpu.VMEM((width, units), BF16), i...  4.62 us
    pallas_call x1, Pallas kernels, far_of(): pl.pallas_call(far_kernel, out_shape=(jax.ShapeDtypeStruct(grad.shape, BF...  4.6 us
    pallas_call x1, Pallas kernels, near_of(): pl.pallas_call(near_kernel, out_shape=(pltpu.VMEM((height, units), F32),...  3.38 us
    unnamed x8, local copies, waits for them, and re-layouts  1.4 us
  transfers between devices with their start and end apart: 13, of which 7 were waited for; matrix products, arithmetic and copies ran while one was open for 0% of the time, Pallas kernels for 23%

profile of v2, /device:TPU:1, one launch (start us, length us, event | category | flops | bytes accessed | tf_op | source)
XLA Modules:
  0.0 69.0 jit_solution(5133176751284193514)
XLA Ops:
  0.6 6.5 %collective-permute-start = (bf16[32,3072]{1,0:T(8,128)(2,1)}, bf16[32,3072]{1,0:T(8,128)(2,1)S(1)}, u32[]{:S(2)}, u32[]{:S(2)}) collective-permute-start(bf16[32,3072]{1,0:T(8,128)(2,1)} %bitcast.30), channel_id=1, source_target_pairs={{0,224},{1,225},{2,226},{3,227},{4,228},{5,229},{6,230},{7,231},{8... | collective-permute-start | bytes 589832 | tf_op jit(solution)/shard_map/ppermute | solution.py:36
  7.1 0.1 pad_add_fusion.place
  7.2 0.0 copy-start.1
  7.2 0.7 copy-done.1
  7.9 0.0 copy-start.2
  7.9 0.7 copy-done.2
  8.6 1.1 %shard_map.68 = (bf16[32,128]{1,0:T(8,128)(2,1)S(1)}, s32[8,128]{1,0:T(8,128)S(1)}, s32[4]{0:T(128)S(1)}) custom-call(s32[4]{0:T(128)S(1)} %pad_add_fusion.place, s32[4,32]{1,0:T(4,128)S(1)} %bitcast.25, bf16[4,32]{1,0:T(4,128)(2,1)S(1)} %bitcast.26), custom_call_target="tpu_custom_call" | custom-call | tf_op jit(solution)/shard_map/pallas_call | solution.py:152
  9.7 1.3 %collective-permute-done = bf16[32,3072]{1,0:T(8,128)(2,1)S(1)} collective-permute-done((bf16[32,3072]{1,0:T(8,128)(2,1)}, bf16[32,3072]{1,0:T(8,128)(2,1)S(1)}, u32[]{:S(2)}, u32[]{:S(2)}) %collective-permute-start) | collective-permute-done | bytes 196640 | tf_op jit(solution)/shard_map/ppermute | solution.py:36
  11.0 3.0 %collective-permute-start.3 = (bf16[32,3200]{1,0:T(8,128)(2,1)S(1)}, bf16[32,3200]{1,0:T(8,128)(2,1)S(1)}, u32[]{:S(2)}, u32[]{:S(2)}) collective-permute-start(bf16[32,3200]{1,0:T(8,128)(2,1)S(1)} %pad_maximum_fusion.1), channel_id=1, source_target_pairs={{0,16},{1,5},{2,18},{3,7},{4,20},{5,1},{6,22},{7,3},{8,24},{9,13},... | collective-permute-start | bytes 614408 | tf_op jit(solution)/shard_map/ppermute | solution.py:36
  14.0 0.8 %collective-permute-start.2 = (bf16[32,3200]{1,0:T(8,128)(2,1)S(1)}, bf16[32,3200]{1,0:T(8,128)(2,1)S(1)}, u32[]{:S(2)}, u32[]{:S(2)}) collective-permute-start(bf16[32,3200]{1,0:T(8,128)(2,1)S(1)} %pad_maximum_fusion.1), channel_id=1, source_target_pairs={{0,24},{1,7},{2,26},{3,1},{4,28},{5,3},{6,30},{7,5},{8,0},{9,15},{... | collective-permute-start | bytes 614408 | tf_op jit(solution)/shard_map/ppermute | solution.py:36
  14.8 0.7 %collective-permute-start.1 = (bf16[32,3200]{1,0:T(8,128)(2,1)S(1)}, bf16[32,3200]{1,0:T(8,128)(2,1)S(1)}, u32[]{:S(2)}, u32[]{:S(2)}) collective-permute-start(bf16[32,3200]{1,0:T(8,128)(2,1)S(1)} %pad_maximum_fusion.1), channel_id=1, source_target_pairs={{0,8},{1,3},{2,10},{3,5},{4,12},{5,7},{6,14},{7,1},{8,16},{9,11},{... | collective-permute-start | bytes 614408 | tf_op jit(solution)/shard_map/ppermute | solution.py:36
  15.5 2.0 %collective-permute-done.3 = bf16[32,3200]{1,0:T(8,128)(2,1)S(1)} collective-permute-done((bf16[32,3200]{1,0:T(8,128)(2,1)S(1)}, bf16[32,3200]{1,0:T(8,128)(2,1)S(1)}, u32[]{:S(2)}, u32[]{:S(2)}) %collective-permute-start.3) | collective-permute-done | bytes 204832 | tf_op jit(solution)/shard_map/ppermute | solution.py:36
  17.5 2.5 %collective-permute-done.2 = bf16[32,3200]{1,0:T(8,128)(2,1)S(1)} collective-permute-done((bf16[32,3200]{1,0:T(8,128)(2,1)S(1)}, bf16[32,3200]{1,0:T(8,128)(2,1)S(1)}, u32[]{:S(2)}, u32[]{:S(2)}) %collective-permute-start.2) | collective-permute-done | bytes 204832 | tf_op jit(solution)/shard_map/ppermute | solution.py:36
  20.1 0.6 collective-permute-done.1
  20.6 0.1 pad_maximum_fusion.mine
  20.7 3.3 %collective-permute-start.6 = (bf16[128,3200]{1,0:T(8,128)(2,1)S(1)}, bf16[128,3200]{1,0:T(8,128)(2,1)S(1)}, u32[]{:S(2)}, u32[]{:S(2)}) collective-permute-start(bf16[128,3200]{1,0:T(8,128)(2,1)S(1)} %pad_maximum_fusion.mine), channel_id=1, source_target_pairs={{0,1},{1,0},{2,3},{3,2},{4,5},{5,4},{6,7},{7,6},{8,9},{9,8},{10,11... | collective-permute-start | bytes 2457608 | tf_op jit(solution)/shard_map/ppermute | solution.py:36
  24.0 0.9 %collective-permute-start.4 = (bf16[64,3200]{1,0:T(8,128)(2,1)S(1)}, bf16[64,3200]{1,0:T(8,128)(2,1)S(1)}, u32[]{:S(2)}, u32[]{:S(2)}) collective-permute-start(bf16[64,3200]{1,0:T(8,128)(2,1)S(1)} %constant_dynamic-update-slice_fusion), channel_id=1, source_target_pairs={{0,6},{1,25},{2,0},{3,27},{4,2},{5,29},{6,4},{7,31},{8,14},{9,1},{... | collective-permute-start | bytes 1228808 | tf_op jit(solution)/shard_map/ppermute | solution.py:36
  24.9 0.7 collective-permute-start.5
  25.5 0.0 collective-permute-start.9
  25.6 2.6 %collective-permute-start.10 = (bf16[64,3200]{1,0:T(8,128)(2,1)S(1)}, bf16[64,3200]{1,0:T(8,128)(2,1)S(1)}, u32[]{:S(2)}, u32[]{:S(2)}) collective-permute-start(bf16[64,3200]{1,0:T(8,128)(2,1)S(1)} %constant_dynamic-update-slice_fusion.2), channel_id=1, source_target_pairs={{0,6},{1,25},{2,0},{3,27},{4,2},{5,29},{6,4},{7,31},{8,14},{9,1},{... | collective-permute-start | bytes 1228808 | tf_op jit(solution)/shard_map/ppermute | solution.py:36
  28.2 4.6 %shard_map.69.turned = bf16[3072,1408]{1,0:T(8,128)(2,1)S(1)} custom-call(s32[4]{0:T(128)S(1)} %get-tuple-element.38.place, bf16[1408,3072]{1,0:T(8,128)(2,1)} %bitcast.27), custom_call_target="tpu_custom_call" | custom-call | bytes 17301504 | tf_op jit(solution)/shard_map/pallas_call | solution.py:201
  32.9 0.0 collective-permute-done.6.theirs
  32.9 3.4 %shard_map.70 = (f32[192,1408]{1,0:T(8,128)S(1)}, f32[192,128]{1,0:T(8,128)S(1)}) custom-call(s32[4]{0:T(128)S(1)} %get-tuple-element.38.place, bf16[128,3200]{1,0:T(8,128)(2,1)S(1)} %pad_maximum_fusion.mine, bf16[128,3200]{1,0:T(8,128)(2,1)S(1)} %collective-permute-done.6.theirs, bf16[3072,1408]{1,0:T(8,128)(2,1)S(1)} %shard_map.69.turned), custom_call_target="tpu_custom_call" | custom-call | flops 1660944384 | bytes 9732096 | tf_op jit(solution)/shard_map/pallas_call | solution.py:225
  36.2 0.0 collective-permute-done.4.refs_2_
  36.3 0.0 collective-permute-done.5.refs_1_
  36.3 0.0 copy-start
  36.3 1.3 %collective-permute-done.9.refs_0_ = bf16[64,3200]{1,0:T(8,128)(2,1)S(1)} collective-permute-done((bf16[64,3200]{1,0:T(8,128)(2,1)S(1)}, bf16[64,3200]{1,0:T(8,128)(2,1)S(1)}, u32[]{:S(2)}, u32[]{:S(2)}) %collective-permute-start.9) | collective-permute-done | bytes 409632 | tf_op jit(solution)/shard_map/ppermute | solution.py:36
  37.6 0.0 collective-permute-done.10.refs_3_
  37.6 0.1 shard_map.71.mine
  37.7 3.4 %collective-permute-start.11 = (bf16[256,3200]{1,0:T(8,128)(2,1)S(1)}, bf16[256,3200]{1,0:T(8,128)(2,1)S(1)}, u32[]{:S(2)}, u32[]{:S(2)}) collective-permute-start(bf16[256,3200]{1,0:T(8,128)(2,1)S(1)} %shard_map.71.mine), channel_id=1, source_target_pairs={{0,1},{1,0},{2,3},{3,2},{4,5},{5,4},{6,7},{7,6},{8,9},{9,8},{10,11... | collective-permute-start | bytes 4915208 | tf_op jit(solution)/shard_map/ppermute | solution.py:36
  41.1 0.8 %collective-permute-start.7 = (bf16[64,3200]{1,0:T(8,128)(2,1)S(1)}, bf16[64,3200]{1,0:T(8,128)(2,1)S(1)}, u32[]{:S(2)}, u32[]{:S(2)}) collective-permute-start(bf16[64,3200]{1,0:T(8,128)(2,1)S(1)} %collective-permute-done.4.refs_2_), channel_id=1, source_target_pairs={{0,6},{1,25},{2,0},{3,27},{4,2},{5,29},{6,4},{7,31},{8,14},{9,1},{... | collective-permute-start | bytes 1228808 | tf_op jit(solution)/shard_map/ppermute | solution.py:36
  41.9 0.7 collective-permute-start.8
  42.5 1.7 %collective-permute-done.11.theirs = bf16[256,3200]{1,0:T(8,128)(2,1)S(1)} collective-permute-done((bf16[256,3200]{1,0:T(8,128)(2,1)S(1)}, bf16[256,3200]{1,0:T(8,128)(2,1)S(1)}, u32[]{:S(2)}, u32[]{:S(2)}) %collective-permute-start.11) | collective-permute-done | bytes 1638432 | tf_op jit(solution)/shard_map/ppermute | solution.py:36
  44.2 0.0 copy-done
  44.2 6.8 %shard_map.72 = (bf16[768,1408]{1,0:T(8,128)(2,1)}, f32[32,128]{1,0:T(8,128)S(1)}, f32[144,1408]{1,0:T(8,128)S(1)}) custom-call(s32[4]{0:T(128)S(1)} %get-tuple-element.38.place, bf16[256,3200]{1,0:T(8,128)(2,1)S(1)} %shard_map.71.mine, bf16[256,3200]{1,0:T(8,128)(2,1)S(1)} %collective-permute-done.11.theirs, bf16[3072,1408]{1,0:T(8,128)(2,1)S(1)} %shard_map.69.turned, ...), custom_call_target="tpu_custom_call" | custom-call | flops 3321888768 | bytes 10813440 | tf_op jit(solution)/shard_map/pallas_call | solution.py:318
  51.0 0.0 collective-permute-done.7.refs_0_
  51.0 0.0 collective-permute-done.8.refs_1_
  51.0 0.1 shard_map.73.mine
  51.1 0.5 collective-permute-start.12
  51.5 2.0 %collective-permute-done.12.theirs = bf16[128,3200]{1,0:T(8,128)(2,1)S(1)} collective-permute-done((bf16[128,3200]{1,0:T(8,128)(2,1)S(1)}, bf16[128,3200]{1,0:T(8,128)(2,1)S(1)}, u32[]{:S(2)}, u32[]{:S(2)}) %collective-permute-start.12) | collective-permute-done | bytes 819232 | tf_op jit(solution)/shard_map/ppermute | solution.py:36
  53.5 4.6 %shard_map.74 = (bf16[768,1408]{1,0:T(8,128)(2,1)}, f32[32,128]{1,0:T(8,128)S(1)}) custom-call(s32[4]{0:T(128)S(1)} %get-tuple-element.38.place, bf16[128,3200]{1,0:T(8,128)(2,1)S(1)} %shard_map.73.mine, bf16[128,3200]{1,0:T(8,128)(2,1)S(1)} %collective-permute-done.12.theirs, ...), custom_call_target="tpu_custom_call", output_to_operand_aliasing={{0}: (7, {})} | custom-call | flops 1660944384 | bytes 9732096 | tf_op jit(solution)/shard_map/pallas_call | solution.py:371
  58.1 10.0 %all_to_all.11 = f32[32,1,128]{2,1,0:T(1,128)S(1)} all-to-all(f32[32,1,128]{2,1,0:T(1,128)S(1)} %bitcast.24), channel_id=1, replica_groups=mesh['pipe'=8,'dp'=4,'expert'=8] {'dp','expert'}, dimensions={0} | all-to-all | bytes 32768 | tf_op jit(solution)/shard_map/all_to_all | solution.py:440
  68.2 0.8 %shard_map.75 = f32[4,32]{1,0:T(4,128)} custom-call(f32[32,128]{1,0:T(8,128)S(1)} %bitcast.23, s32[8,128]{1,0:T(8,128)S(1)} %get-tuple-element.55.lines), custom_call_target="tpu_custom_call" | custom-call | tf_op jit(solution)/shard_map/pallas_call | solution.py:441
  (5 shorter events, 0.1 us)
Async XLA Ops:
  0.6 10.4 %collective-permute-start = (bf16[32,3072]{1,0:T(8,128)(2,1)}, bf16[32,3072]{1,0:T(8,128)(2,1)S(1)}, u32[]{:S(2)}, u32[]{:S(2)}) collective-permute-start(bf16[32,3072]{1,0:T(8,128)(2,1)} %bitcast.30), channel_id=1, source_target_pairs={{0,224},{1,225},{2,226},{3,227},{4,228},{5,229},{6,230},{7,231},{8... | collective-permute-start | bytes 589832 | tf_op jit(solution)/shard_map/ppermute | solution.py:36
  7.2 0.7 copy-start.1
  7.9 0.7 copy-start.2
  11.0 6.5 %collective-permute-start.3 = (bf16[32,3200]{1,0:T(8,128)(2,1)S(1)}, bf16[32,3200]{1,0:T(8,128)(2,1)S(1)}, u32[]{:S(2)}, u32[]{:S(2)}) collective-permute-start(bf16[32,3200]{1,0:T(8,128)(2,1)S(1)} %pad_maximum_fusion.1), channel_id=1, source_target_pairs={{0,16},{1,5},{2,18},{3,7},{4,20},{5,1},{6,22},{7,3},{8,24},{9,13},... | collective-permute-start | bytes 614408 | tf_op jit(solution)/shard_map/ppermute | solution.py:36
  14.0 6.0 %collective-permute-start.2 = (bf16[32,3200]{1,0:T(8,128)(2,1)S(1)}, bf16[32,3200]{1,0:T(8,128)(2,1)S(1)}, u32[]{:S(2)}, u32[]{:S(2)}) collective-permute-start(bf16[32,3200]{1,0:T(8,128)(2,1)S(1)} %pad_maximum_fusion.1), channel_id=1, source_target_pairs={{0,24},{1,7},{2,26},{3,1},{4,28},{5,3},{6,30},{7,5},{8,0},{9,15},{... | collective-permute-start | bytes 614408 | tf_op jit(solution)/shard_map/ppermute | solution.py:36
  14.8 5.8 %collective-permute-start.1 = (bf16[32,3200]{1,0:T(8,128)(2,1)S(1)}, bf16[32,3200]{1,0:T(8,128)(2,1)S(1)}, u32[]{:S(2)}, u32[]{:S(2)}) collective-permute-start(bf16[32,3200]{1,0:T(8,128)(2,1)S(1)} %pad_maximum_fusion.1), channel_id=1, source_target_pairs={{0,8},{1,3},{2,10},{3,5},{4,12},{5,7},{6,14},{7,1},{8,16},{9,11},{... | collective-permute-start | bytes 614408 | tf_op jit(solution)/shard_map/ppermute | solution.py:36
  20.7 12.2 %collective-permute-start.6 = (bf16[128,3200]{1,0:T(8,128)(2,1)S(1)}, bf16[128,3200]{1,0:T(8,128)(2,1)S(1)}, u32[]{:S(2)}, u32[]{:S(2)}) collective-permute-start(bf16[128,3200]{1,0:T(8,128)(2,1)S(1)} %pad_maximum_fusion.mine), channel_id=1, source_target_pairs={{0,1},{1,0},{2,3},{3,2},{4,5},{5,4},{6,7},{7,6},{8,9},{9,8},{10,11... | collective-permute-start | bytes 2457608 | tf_op jit(solution)/shard_map/ppermute | solution.py:36
  24.0 12.2 %collective-permute-start.4 = (bf16[64,3200]{1,0:T(8,128)(2,1)S(1)}, bf16[64,3200]{1,0:T(8,128)(2,1)S(1)}, u32[]{:S(2)}, u32[]{:S(2)}) collective-permute-start(bf16[64,3200]{1,0:T(8,128)(2,1)S(1)} %constant_dynamic-update-slice_fusion), channel_id=1, source_target_pairs={{0,6},{1,25},{2,0},{3,27},{4,2},{5,29},{6,4},{7,31},{8,14},{9,1},{... | collective-permute-start | bytes 1228808 | tf_op jit(solution)/shard_map/ppermute | solution.py:36
  24.9 11.4 %collective-permute-start.5 = (bf16[64,3200]{1,0:T(8,128)(2,1)S(1)}, bf16[64,3200]{1,0:T(8,128)(2,1)S(1)}, u32[]{:S(2)}, u32[]{:S(2)}) collective-permute-start(bf16[64,3200]{1,0:T(8,128)(2,1)S(1)} %constant_dynamic-update-slice_fusion.2), channel_id=1, source_target_pairs={{0,2},{1,9},{2,4},{3,11},{4,6},{5,13},{6,0},{7,15},{8,10},{9,17},{... | collective-permute-start | bytes 1228808 | tf_op jit(solution)/shard_map/ppermute | solution.py:36
  25.5 12.0 %collective-permute-start.9 = (bf16[64,3200]{1,0:T(8,128)(2,1)S(1)}, bf16[64,3200]{1,0:T(8,128)(2,1)S(1)}, u32[]{:S(2)}, u32[]{:S(2)}) collective-permute-start(bf16[64,3200]{1,0:T(8,128)(2,1)S(1)} %constant_dynamic-update-slice_fusion), channel_id=1, source_target_pairs={{0,2},{1,9},{2,4},{3,11},{4,6},{5,13},{6,0},{7,15},{8,10},{9,17},{... | collective-permute-start | bytes 1228808 | tf_op jit(solution)/shard_map/ppermute | solution.py:36
  25.6 12.0 %collective-permute-start.10 = (bf16[64,3200]{1,0:T(8,128)(2,1)S(1)}, bf16[64,3200]{1,0:T(8,128)(2,1)S(1)}, u32[]{:S(2)}, u32[]{:S(2)}) collective-permute-start(bf16[64,3200]{1,0:T(8,128)(2,1)S(1)} %constant_dynamic-update-slice_fusion.2), channel_id=1, source_target_pairs={{0,6},{1,25},{2,0},{3,27},{4,2},{5,29},{6,4},{7,31},{8,14},{9,1},{... | collective-permute-start | bytes 1228808 | tf_op jit(solution)/shard_map/ppermute | solution.py:36
  36.3 7.9 %copy-start = (bf16[1,1,768,1408]{3,2,1,0:T(8,128)(2,1)S(1)}, bf16[1,1,768,1408]{3,2,1,0:T(8,128)(2,1)}, u32[]{:S(2)}) copy-start(bf16[1,1,768,1408]{3,2,1,0:T(8,128)(2,1)} %param.9) | copy-start | bytes 6488068
  37.7 6.5 %collective-permute-start.11 = (bf16[256,3200]{1,0:T(8,128)(2,1)S(1)}, bf16[256,3200]{1,0:T(8,128)(2,1)S(1)}, u32[]{:S(2)}, u32[]{:S(2)}) collective-permute-start(bf16[256,3200]{1,0:T(8,128)(2,1)S(1)} %shard_map.71.mine), channel_id=1, source_target_pairs={{0,1},{1,0},{2,3},{3,2},{4,5},{5,4},{6,7},{7,6},{8,9},{9,8},{10,11... | collective-permute-start | bytes 4915208 | tf_op jit(solution)/shard_map/ppermute | solution.py:36
  41.1 9.9 %collective-permute-start.7 = (bf16[64,3200]{1,0:T(8,128)(2,1)S(1)}, bf16[64,3200]{1,0:T(8,128)(2,1)S(1)}, u32[]{:S(2)}, u32[]{:S(2)}) collective-permute-start(bf16[64,3200]{1,0:T(8,128)(2,1)S(1)} %collective-permute-done.4.refs_2_), channel_id=1, source_target_pairs={{0,6},{1,25},{2,0},{3,27},{4,2},{5,29},{6,4},{7,31},{8,14},{9,1},{... | collective-permute-start | bytes 1228808 | tf_op jit(solution)/shard_map/ppermute | solution.py:36
  41.9 9.1 %collective-permute-start.8 = (bf16[64,3200]{1,0:T(8,128)(2,1)S(1)}, bf16[64,3200]{1,0:T(8,128)(2,1)S(1)}, u32[]{:S(2)}, u32[]{:S(2)}) collective-permute-start(bf16[64,3200]{1,0:T(8,128)(2,1)S(1)} %collective-permute-done.5.refs_1_), channel_id=1, source_target_pairs={{0,2},{1,9},{2,4},{3,11},{4,6},{5,13},{6,0},{7,15},{8,10},{9,17},{... | collective-permute-start | bytes 1228808 | tf_op jit(solution)/shard_map/ppermute | solution.py:36
  51.1 2.4 %collective-permute-start.12 = (bf16[128,3200]{1,0:T(8,128)(2,1)S(1)}, bf16[128,3200]{1,0:T(8,128)(2,1)S(1)}, u32[]{:S(2)}, u32[]{:S(2)}) collective-permute-start(bf16[128,3200]{1,0:T(8,128)(2,1)S(1)} %shard_map.73.mine), channel_id=1, source_target_pairs={{0,1},{1,0},{2,3},{3,2},{4,5},{5,4},{6,7},{7,6},{8,9},{9,8},{10,11... | collective-permute-start | bytes 2457608 | tf_op jit(solution)/shard_map/ppermute | solution.py:36

commit v3 on v2

--- a/solution.py
+++ b/solution.py
@@ -109,12 +109,8 @@
     return pltpu.CompilerParams(vmem_limit_bytes=mebibytes << 20)
 
 
-def cost(height, units, width):
-    return pl.CostEstimate(
-        flops=2 * height * units * width,
-        bytes_accessed=2 * units * width + 4 * height * units,
-        transcendentals=0,
-    )
+def small():
+    return pl.CostEstimate(flops=1, bytes_accessed=1, transcendentals=0)
 
 
 def meta_kernel(place, ids, gates, meta, lines, spot):
@@ -177,41 +173,77 @@
         in_specs=[vmem()] * len(parts),
         out_specs=vmem(),
         compiler_params=params(6),
+        cost_estimate=small(),
     )(*parts)
 
 
-def turn_kernel(place, weight, turned, held, sems):
+def halves_kernel(high, low, first_half, second_half):
+    half = first_half.shape[0]
+    first_half[...] = high[:half, :]
+    second_half[...] = low[half:, :]
+
+
+def halves_of(high, low):
+    shape = (high.shape[0] // 2, high.shape[1])
+    return pl.pallas_call(
+        halves_kernel,
+        out_shape=(pltpu.VMEM(shape, BF16), pltpu.VMEM(shape, BF16)),
+        in_specs=[vmem()] * 2,
+        out_specs=(vmem(), vmem()),
+        compiler_params=params(6),
+        cost_estimate=small(),
+    )(high, low)
+
+
+def far_block(place, n):
+    which, a = divmod(n, 4)
+    kind = place[2] if which == 0 else 1 - place[2]
+    x = jnp.where(kind == 0, OFFSETS[a], 2)
+    y = jnp.where(kind == 0, 2, OFFSETS[a])
+    return kind, chip_of(place, x, y)
+
+
+def turn_kernel(place, hidden, weight, turned, ahead, held, far, sems):
     units, width = weight.shape
+    starts = range(0, units, TILE)
+    spans = [pl.ds(at, min(TILE, units - at)) for at in starts]
     copies = [
-        pltpu.make_async_copy(
-            weight.at[pl.ds(at, META), :], held.at[pl.ds(at, META), :], sems.at[at // META]
-        )
-        for at in range(0, units, META)
+        pltpu.make_async_copy(weight.at[span, :], held.at[span, :], sems.at[n])
+        for n, span in enumerate(spans)
     ]
     for copy in copies:
         copy.start()
-    for copy, at in zip(copies, range(0, units, META)):
-        copy.wait()
+    for n in range(far.shape[0] // CAP):
+        kind, chip = far_block(place, n)
+        pair = hidden[pair_rows(chip), :].astype(F32)
+        far[n * CAP : (n + 1) * CAP, :] = jnp.where(kind == 0, pair[:CAP], pair[CAP:])
+    for n, at in enumerate(starts):
+        copies[n].wait()
+        to = min(at + TILE, units)
+        left = far[:, at:to].astype(BF16)
         for col in range(0, width, 512):
-            turned[col : col + 512, at : at + META] = held[at : at + META, col : col + 512].T
-
-
-def turn(place, weight):
+            span = slice(col, col + 512)
+            turned[span, at:to] = held[at:to, span].T
+            value = jnp.dot(left, held[at:to, span], preferred_element_type=F32)
+            ahead[:, span] = value if n == 0 else ahead[:, span] + value
+
+
+def turn(place, hidden, weight):
     units, width = weight.shape
+    height = hidden.shape[0] // 4
     return pl.pallas_call(
         turn_kernel,
-        out_shape=pltpu.VMEM((width, units), BF16),
-        in_specs=[smem(), anywhere()],
-        out_specs=vmem(),
+        out_shape=(pltpu.VMEM((width, units), BF16), pltpu.VMEM((height, width), F32)),
+        in_specs=[smem(), vmem(), anywhere()],
+        out_specs=(vmem(), vmem()),
         scratch_shapes=[
             pltpu.VMEM((units, width), BF16),
-            pltpu.SemaphoreType.DMA((units // META,)),
+            pltpu.VMEM((height, units), F32),
+            pltpu.SemaphoreType.DMA((pl.cdiv(units, TILE),)),
         ],
         compiler_params=params(),
-        cost_estimate=pl.CostEstimate(
-            flops=0, bytes_accessed=4 * units * width, transcendentals=0
-        ),
-    )(place, pltpu.with_memory_space_constraint(weight, pltpu.HBM))
+        cost_estimate=small(),
+    )(place, hidden, pltpu.with_memory_space_constraint(weight, pltpu.HBM))
 
 
 def near_kernel(place, mine, theirs, turned, out, gates, packed):
@@ -229,7 +261,7 @@
         out_specs=(vmem(), vmem()),
         scratch_shapes=[pltpu.VMEM((height, width), BF16)],
         compiler_params=params(),
-        cost_estimate=cost(height, units, width),
+        cost_estimate=small(),
     )(place, mine, theirs, turned)
 
 
@@ -282,10 +314,10 @@
 
 
 def mid_kernel(
-    place, mine, theirs, turned, hidden, near, near_gates,
+    place, low, high, low_other, high_other, turned, hidden, near, near_gates,
     grad, sums, halves, packed, mid, mid_gates, stage, sems,
 ):
-    pack(place[3], (mine, theirs), packed, mid_gates)
+    pack(place[3], (low, high, low_other, high_other), packed, mid_gates)
     multiply(packed, turned, mid)
 
     def piece(kind, along, across):
@@ -312,9 +344,9 @@
         copy.wait()
 
 
-def mid_of(place, mine, theirs, turned, hidden, near, near_gates):
+def mid_of(place, tokens, turned, hidden, near, near_gates):
     width, units = turned.shape
-    height = 2 * mine.shape[0] // ROWS * CAP
+    height = sum(t.shape[0] for t in tokens) // ROWS * CAP
     return pl.pallas_call(
         mid_kernel,
         out_shape=(
@@ -322,7 +354,7 @@
             pltpu.VMEM((hidden.shape[0] // CAP, META), F32),
             pltpu.VMEM((len(HALVES) * CAP, units), F32),
         ),
-        in_specs=[smem()] + [vmem()] * 6,
+        in_specs=[smem()] + [vmem()] * 8,
         out_specs=(anywhere(), vmem(), vmem()),
         scratch_shapes=[
             pltpu.VMEM((height, width), BF16),
@@ -332,17 +364,60 @@
             pltpu.SemaphoreType.DMA((9,)),
         ],
         compiler_params=params(),
-        cost_estimate=cost(height, units, width),
-    )(place, mine, theirs, turned, hidden, near, near_gates)
-
-
-def far_kernel(
-    place, mine, theirs, turned, hidden, halves, early, _, grad, sums,
-    packed, far, far_gates, stage, sems,
-):
+        cost_estimate=small(),
+    )(place, *tokens, turned, hidden, near, near_gates)
+
+
+def sums_kernel(place, mine, theirs, ahead, early, sums, packed, gates):
     sums[...] = early[...]
-    pack(place[3], (mine, theirs), packed, far_gates)
-    multiply(packed, turned, far)
+    pack(place[3], (mine, theirs), packed, gates)
+    height, width = packed.shape
+    diagonal = lax.broadcasted_iota(jnp.int32, (CAP, META), 0) == lax.broadcasted_iota(
+        jnp.int32, (CAP, META), 1
+    )
+    for n in range(height // CAP):
+        block = slice(n * CAP, (n + 1) * CAP)
+        total = jnp.zeros((CAP, META), F32)
+        for col in range(0, width, META):
+            span = slice(col, col + META)
+            total += packed[block, span].astype(F32) * ahead[block, span]
+        total = jnp.sum(total, axis=1, keepdims=True)
+        kind, chip = far_block(place, n)
+        sums[pl.ds(chip * 2 + kind, 1), :] = jnp.sum(
+            jnp.where(diagonal, total, 0.0), axis=0, keepdims=True
+        )
+
+
+def sums_of(place, mine, theirs, ahead, early):
+    height, width = ahead.shape
+    return pl.pallas_call(
+        sums_kernel,
+        out_shape=(
+            pltpu.VMEM(early.shape, F32),
+            pltpu.VMEM((height, width), BF16),
+            pltpu.VMEM((height, META), F32),
+        ),
+        in_specs=[smem()] + [vmem()] * 4,
+        out_specs=(vmem(), vmem(), vmem()),
+        compiler_params=params(),
+        cost_estimate=small(),
+    )(place, mine, theirs, ahead, early)
+
+
+def far_kernel(place, packed, gates, turned, halves, _, grad, held, far, stage, sems, loads):
+    units = far.shape[1]
+    spans = [pl.ds(at, 512) for at in range(0, held.shape[0], 512)]
+    copies = [
+        pltpu.make_async_copy(turned.at[span, :], held.at[span, :], loads.at[n])
+        for n, span in enumerate(spans)
+    ]
+    for copy in copies:
+        copy.start()
+    for n, span in enumerate(spans):
+        copies[n].wait()
+        at = slice(span.start, span.start + span.size)
+        value = jnp.dot(packed[:, at], held[at, :], preferred_element_type=F32)
+        far[...] = value if n == 0 else far[...] + value
     copies = []
     for i in OFFSETS:
         for j in OFFSETS:
@@ -351,13 +426,19 @@
             pieces = []
             for kind, along, across in ((0, i, j), (1, j, i)):
                 if across == 2:
-                    rows_of = block_rows(place, kind, 4, OFFSETS.index(along))
-                    pieces.append((far, far_gates, rows_of))
+                    span = block_rows(place, kind, 4, OFFSETS.index(along))
+                    pieces.append((far, gates[span, :], span))
                 else:
                     n = HALVES.index((kind, i, j))
                     pieces.append((halves, None, pl.ds(n * CAP, CAP)))
             chip, slot = chip_of(place, i, j), len(copies)
-            finish(chip, pieces, hidden, sums, staged(stage, slot))
+            for col in range(0, units, META):
+                span = slice(col, col + META)
+                scaled = [
+                    ref[at, span] if scale is None else scale * ref[at, span]
+                    for ref, scale, at in pieces
+                ]
+                stage[slot, :, span] = jnp.concatenate(scaled, axis=0).astype(BF16)
             copy = pltpu.make_async_copy(stage.at[slot], grad.at[pair_rows(chip), :], sems.at[slot])
             copy.start()
             copies.append(copy)
@@ -365,28 +446,27 @@
         copy.wait()
 
 
-def far_of(place, mine, theirs, turned, hidden, halves, early, grad):
+def far_of(place, packed, gates, turned, halves, grad):
     width, units = turned.shape
-    height = 2 * mine.shape[0] // ROWS * CAP
+    height = packed.shape[0]
     return pl.pallas_call(
         far_kernel,
-        out_shape=(
-            jax.ShapeDtypeStruct(grad.shape, BF16),
-            pltpu.VMEM(early.shape, F32),
-        ),
-        in_specs=[smem()] + [vmem()] * 6 + [anywhere()],
-        out_specs=(anywhere(), vmem()),
+        out_shape=jax.ShapeDtypeStruct(grad.shape, BF16),
+        in_specs=[smem(), vmem(), vmem(), anywhere(), vmem(), anywhere()],
+        out_specs=anywhere(),
         scratch_shapes=[
-            pltpu.VMEM((height, width), BF16),
+            pltpu.VMEM((width, units), BF16),
             pltpu.VMEM((height, units), F32),
-            pltpu.VMEM((height, META), F32),
             pltpu.VMEM((7, 2 * CAP, units), BF16),
             pltpu.SemaphoreType.DMA((7,)),
+            pltpu.SemaphoreType.DMA((width // 512,)),
         ],
-        input_output_aliases={7: 0},
+        input_output_aliases={5: 0},
         compiler_params=params(),
-        cost_estimate=cost(height, units, width),
-    )(place, mine, theirs, turned, hidden, halves, early, grad)
+        cost_estimate=pl.CostEstimate(
+            flops=2 * height * units * turned.shape[0], bytes_accessed=1, transcendentals=0
+        ),
+    )(place, packed, gates, pltpu.with_memory_space_constraint(turned, pltpu.HBM), halves, grad)
 
 
 def gather_kernel(totals, lines, out):
@@ -407,37 +487,33 @@
     dp, expert = lax.axis_index("dp"), lax.axis_index("expert")
     place = jnp.stack([dp, expert // 2, expert % 2, expert]).astype(jnp.int32)
     ids = expert_ids[0].T
+    weight, saved = down_weight[0, 0], hidden[0, 0]
     incoming = moved(handoff[0], previous_section)
     meta, lines, place = meta_of(place, ids, gates[0].T)
+    incoming, meta, lines, place = lax.optimization_barrier((incoming, meta, lines, place))
     own = jnp.concatenate([incoming, meta], axis=1)
-    own, lines, place = lax.optimization_barrier((own, lines, place))
+    own, place = lax.optimization_barrier((own, place))
 
     ahead, back, across = [moved(own, first(k)) for k in (1, 3, 2)]
-    ahead, back, across = lax.optimization_barrier((ahead, back, across))
-    near = rows(own, ahead), rows(back, across)
-    high = [moved(near[0], second(3)), None]
-    low = [None, moved(near[1], second(1))]
-    low[0] = moved(near[0], second(1))
-    high[1] = moved(near[1], second(3))
-    near = rows(*near)
-    near, later = lax.optimization_barrier((near, place))
-    turned = turn(later, down_weight[0, 0])
+    turned, ahead_far = turn(place, saved, weight)
+    ahead, back, across, turned, ahead_far = lax.optimization_barrier(
+        (ahead, back, across, turned, ahead_far)
+    )
+    near = rows(own, ahead, back, across)
+    low, high = moved(near, second(1)), moved(near, second(3))
     near_other = moved(near, other_core)
-    near_products, near_gates = near_of(place, near, near_other, turned)
-    high[0], low[1], near_products, near_gates = lax.optimization_barrier(
-        (high[0], low[1], near_products, near_gates)
-    )
-    far = moved(high[0], second(3)), moved(low[1], second(1))
-    mid = join(*low, *high)
-    mid_other = moved(mid, other_core)
-    grad, sums, halves = mid_of(
-        place, mid, mid_other, turned, hidden[0, 0], near_products, near_gates
-    )
-    far, grad, sums, halves = lax.optimization_barrier((far, grad, sums, halves))
+    near_done = near_of(place, near, near_other, turned)
+    low, high, *near_done = lax.optimization_barrier((low, high, *near_done))
+    left, right = halves_of(high, low)
+    far = moved(left, second(3)), moved(right, second(1))
+    tokens = low, high, moved(low, other_core), moved(high, other_core)
+    grad, sums, halves = mid_of(place, tokens, turned, saved, *near_done)
+    *far, grad, sums, halves = lax.optimization_barrier((*far, grad, sums, halves))
     far = join(*far)
     far_other = moved(far, other_core)
-    grad, sums = far_of(place, far, far_other, turned, hidden[0, 0], halves, sums, grad)
+    sums, packed, far_gates = sums_of(place, far, far_other, ahead_far, sums)
     totals = lax.all_to_all(sums, ("dp", "expert"), split_axis=0, concat_axis=0, tiled=True)
+    grad = far_of(place, packed, far_gates, turned, halves, grad)
     gate_grad = pl.pallas_call(
         gather_kernel,
         out_shape=jax.ShapeDtypeStruct(ids.shape, F32),

time: 69.1 us -> 67.6 us (0.978)
  blocking collectives: 10 us -> 0 us
  Pallas kernels: 21.5 us -> 25.4 us
  starting transfers between devices: 23.7 us -> 25.9 us
  local copies, waits for them, and re-layouts: 1.44 us -> 3.06 us
  waiting for transfers between devices: 11.3 us -> 12.2 us
    all_to_all x1 -> x0, blocking collectives: 10 us -> none  [on_device(): lax.all_to_all(sums, ('dp', 'expert'), split_axis=0, concat_axis=0, tiled...]
    all_to_all x0 -> x1, starting transfers between devices: none -> 4.14 us  [on_device(): lax.all_to_all(sums, ('dp', 'expert'), split_axis=0, concat_axis=0, tiled...]
    pallas_call x2 -> x4, Pallas kernels: 9.22 us -> 12.9 us  [the longest x1 5.86 us: far_of(): pl.pallas_call(far_kernel, out_shape=jax.ShapeDtypeStruct(grad.shape, BF1...]
    ppermute x13 -> x12, starting transfers between devices: 23.7 us -> 21.8 us  [moved(): return lax.ppermute(x, AXES, pairs)]
    unnamed x8 -> x13, local copies, waits for them, and re-layouts: 1.4 us -> 3.03 us
    all_to_all x0 -> x1, waiting for transfers between devices: none -> 1.07 us  [on_device(): lax.all_to_all(sums, ('dp', 'expert'), split_axis=0, concat_axis=0, tiled...]
    ppermute x13 -> x12, waiting for transfers between devices: 11.3 us -> 11.1 us  [moved(): return lax.ppermute(x, AXES, pairs)]
  transfers between devices with their start and end apart: 13 -> 13, of which waited for: 7 -> 6; matrix products, arithmetic and copies ran while one was open for 0% -> 0% of each run, Pallas kernels for 23% -> 33%
where the time goes in v3:
time: 67.6 us; the launch traced here: 67.4 us
  starting transfers between devices  25.9 us (38%)
  Pallas kernels  25.4 us (38%)
  waiting for transfers between devices  12.2 us (18%)
  local copies, waits for them, and re-layouts  3.06 us (5%)
  between operations  0.77 us (1%)
    ppermute x12, starting transfers between devices, moved(): return lax.ppermute(x, AXES, pairs)  21.8 us
    ppermute x12, waiting for transfers between devices, moved(): return lax.ppermute(x, AXES, pairs)  11.1 us
    pallas_call x1, Pallas kernels, mid_of(): pl.pallas_call(mid_kernel, out_shape=(jax.ShapeDtypeStruct(hidden.shape,...  7.05 us
    pallas_call x1, Pallas kernels, far_of(): pl.pallas_call(far_kernel, out_shape=jax.ShapeDtypeStruct(grad.shape, BF1...  5.86 us
    pallas_call x1, Pallas kernels, turn(): pl.pallas_call(turn_kernel, out_shape=(pltpu.VMEM((width, units), BF16),...  4.94 us
    all_to_all x1, starting transfers between devices, on_device(): lax.all_to_all(sums, ('dp', 'expert'), split_axis=0, concat_axis=0, tiled...  4.14 us
    pallas_call x1, Pallas kernels, near_of(): pl.pallas_call(near_kernel, out_shape=(pltpu.VMEM((height, units), F32),...  3.37 us
    unnamed x13, local copies, waits for them, and re-layouts  3.03 us
  transfers between devices with their start and end apart: 13, of which 6 were waited for; matrix products, arithmetic and copies ran while one was open for 0% of the time, Pallas kernels for 33%

profile of v3, /device:TPU:1, one launch (start us, length us, event | category | flops | bytes accessed | tf_op | source)
XLA Modules:
  0.0 67.4 jit_solution(10377385252359955382)
XLA Ops:
  0.6 6.5 %collective-permute-start = (bf16[32,3072]{1,0:T(8,128)(2,1)}, bf16[32,3072]{1,0:T(8,128)(2,1)S(1)}, u32[]{:S(2)}, u32[]{:S(2)}) collective-permute-start(bf16[32,3072]{1,0:T(8,128)(2,1)} %bitcast.29), channel_id=1, source_target_pairs={{0,224},{1,225},{2,226},{3,227},{4,228},{5,229},{6,230},{7,231},{8... | collective-permute-start | bytes 589832 | tf_op jit(solution)/shard_map/ppermute | solution.py:36
  7.1 0.1 pad_add_fusion.place
  7.2 0.0 copy-start.3
  7.2 0.7 %copy-done.3 = s32[1,32,4]{1,2,0:T(4,128)S(1)} copy-done((s32[1,32,4]{1,2,0:T(4,128)S(1)}, s32[1,32,4]{1,2,0:T(4,128)}, u32[]{:S(2)}) %copy-start.3) | copy-done | bytes 536
  7.9 0.0 copy-start.4
  7.9 0.7 %copy-done.4 = bf16[1,32,4]{1,2,0:T(4,128)(2,1)S(1)} copy-done((bf16[1,32,4]{1,2,0:T(4,128)(2,1)S(1)}, bf16[1,32,4]{1,2,0:T(4,128)(2,1)}, u32[]{:S(2)}) %copy-start.4) | copy-done | bytes 280
  8.6 1.1 %shard_map.68 = (bf16[32,128]{1,0:T(8,128)(2,1)S(1)}, s32[8,128]{1,0:T(8,128)S(1)}, s32[4]{0:T(128)S(1)}) custom-call(s32[4]{0:T(128)S(1)} %pad_add_fusion.place, s32[4,32]{1,0:T(4,128)S(1)} %bitcast.24, bf16[4,32]{1,0:T(4,128)(2,1)S(1)} %bitcast.25), custom_call_target="tpu_custom_call" | custom-call | tf_op jit(solution)/shard_map/pallas_call | solution.py:148
  9.7 1.3 %collective-permute-done = bf16[32,3072]{1,0:T(8,128)(2,1)S(1)} collective-permute-done((bf16[32,3072]{1,0:T(8,128)(2,1)}, bf16[32,3072]{1,0:T(8,128)(2,1)S(1)}, u32[]{:S(2)}, u32[]{:S(2)}) %collective-permute-start) | collective-permute-done | bytes 196640 | tf_op jit(solution)/shard_map/ppermute | solution.py:36
  11.0 1.4 %collective-permute-start.1 = (bf16[32,3200]{1,0:T(8,128)(2,1)S(1)}, bf16[32,3200]{1,0:T(8,128)(2,1)S(1)}, u32[]{:S(2)}, u32[]{:S(2)}) collective-permute-start(bf16[32,3200]{1,0:T(8,128)(2,1)S(1)} %pad_maximum_fusion), channel_id=1, source_target_pairs={{0,8},{1,3},{2,10},{3,5},{4,12},{5,7},{6,14},{7,1},{8,16},{9,11},{... | collective-permute-start | bytes 614408 | tf_op jit(solution)/shard_map/ppermute | solution.py:36
  12.4 1.5 %collective-permute-start.2 = (bf16[32,3200]{1,0:T(8,128)(2,1)S(1)}, bf16[32,3200]{1,0:T(8,128)(2,1)S(1)}, u32[]{:S(2)}, u32[]{:S(2)}) collective-permute-start(bf16[32,3200]{1,0:T(8,128)(2,1)S(1)} %pad_maximum_fusion), channel_id=1, source_target_pairs={{0,24},{1,7},{2,26},{3,1},{4,28},{5,3},{6,30},{7,5},{8,0},{9,15},{... | collective-permute-start | bytes 614408 | tf_op jit(solution)/shard_map/ppermute | solution.py:36
  13.9 1.6 %collective-permute-start.3 = (bf16[32,3200]{1,0:T(8,128)(2,1)S(1)}, bf16[32,3200]{1,0:T(8,128)(2,1)S(1)}, u32[]{:S(2)}, u32[]{:S(2)}) collective-permute-start(bf16[32,3200]{1,0:T(8,128)(2,1)S(1)} %pad_maximum_fusion), channel_id=1, source_target_pairs={{0,16},{1,5},{2,18},{3,7},{4,20},{5,1},{6,22},{7,3},{8,24},{9,13},... | collective-permute-start | bytes 614408 | tf_op jit(solution)/shard_map/ppermute | solution.py:36
  15.5 0.0 copy-start.1
  15.5 1.6 %copy-done.1 = bf16[1,1,768,1408]{3,2,1,0:T(8,128)(2,1)S(1)} copy-done((bf16[1,1,768,1408]{3,2,1,0:T(8,128)(2,1)S(1)}, bf16[1,1,768,1408]{3,2,1,0:T(8,128)(2,1)}, u32[]{:S(2)}) %copy-start.1) | copy-done | bytes 2162712
  17.1 4.9 %shard_map.69 = (bf16[3072,1408]{1,0:T(8,128)(2,1)S(1)}, f32[192,3072]{1,0:T(8,128)S(1)}) custom-call(s32[4]{0:T(128)S(1)} %get-tuple-element.43.place, bf16[768,1408]{1,0:T(8,128)(2,1)S(1)} %bitcast.21, bf16[1408,3072]{1,0:T(8,128)(2,1)} %bitcast.26), custom_call_target="tpu_custom_call" | custom-call | flops 1 | bytes 1 | tf_op jit(solution)/shard_map/pallas_call | solution.py:234
  22.1 0.0 copy-start
  22.1 0.0 collective-permute-done.1
  22.1 0.0 collective-permute-done.2
  22.1 0.0 collective-permute-done.3
  22.2 2.3 %collective-permute-start.6 = (bf16[128,3200]{1,0:T(8,128)(2,1)S(1)}, bf16[128,3200]{1,0:T(8,128)(2,1)S(1)}, u32[]{:S(2)}, u32[]{:S(2)}) collective-permute-start(bf16[128,3200]{1,0:T(8,128)(2,1)S(1)} %constant_dynamic-update-slice_fusion.mine), channel_id=1, source_target_pairs={{0,1},{1,0},{2,3},{3,2},{4,5},{5,4},{6,7},{7,6},{8,9},{9,8},{10,11... | collective-permute-start | bytes 2457608 | tf_op jit(solution)/shard_map/ppermute | solution.py:36
  24.5 0.3 collective-permute-start.4
  24.8 2.4 %collective-permute-start.5 = (bf16[128,3200]{1,0:T(8,128)(2,1)S(1)}, bf16[128,3200]{1,0:T(8,128)(2,1)S(1)}, u32[]{:S(2)}, u32[]{:S(2)}) collective-permute-start(bf16[128,3200]{1,0:T(8,128)(2,1)S(1)} %constant_dynamic-update-slice_fusion.mine), channel_id=1, source_target_pairs={{0,6},{1,25},{2,0},{3,27},{4,2},{5,29},{6,4},{7,31},{8,14},{9,1},{... | collective-permute-start | bytes 2457608 | tf_op jit(solution)/shard_map/ppermute | solution.py:36
  27.1 0.0 collective-permute-done.6.theirs
  27.1 0.0 copy-start.2
  27.2 3.4 %shard_map.70 = (f32[192,1408]{1,0:T(8,128)S(1)}, f32[192,128]{1,0:T(8,128)S(1)}) custom-call(s32[4]{0:T(128)S(1)} %get-tuple-element.43.place, bf16[128,3200]{1,0:T(8,128)(2,1)S(1)} %constant_dynamic-update-slice_fusion.mine, bf16[128,3200]{1,0:T(8,128)(2,1)S(1)} %collective-permute-done.6.theirs, bf16[3072,1408]{1,0:T(8,128)(2,1)S(1)} %get-tuple-element.50.turned), custom_call_target="tpu_custom_call" | custom-call | flops 1 | bytes 1 | tf_op jit(solution)/shard_map/pallas_call | solution.py:257
  30.5 6.6 %collective-permute-done.4.low = bf16[128,3200]{1,0:T(8,128)(2,1)S(1)} collective-permute-done((bf16[128,3200]{1,0:T(8,128)(2,1)S(1)}, bf16[128,3200]{1,0:T(8,128)(2,1)S(1)}, u32[]{:S(2)}, u32[]{:S(2)}) %collective-permute-start.4) | collective-permute-done | bytes 819232 | tf_op jit(solution)/shard_map/ppermute | solution.py:36
  37.2 0.0 collective-permute-done.5.high
  37.2 1.3 %collective-permute-start.10 = (bf16[128,3200]{1,0:T(8,128)(2,1)S(1)}, bf16[128,3200]{1,0:T(8,128)(2,1)S(1)}, u32[]{:S(2)}, u32[]{:S(2)}) collective-permute-start(bf16[128,3200]{1,0:T(8,128)(2,1)S(1)} %collective-permute-done.5.high), channel_id=1, source_target_pairs={{0,1},{1,0},{2,3},{3,2},{4,5},{5,4},{6,7},{7,6},{8,9},{9,8},{10,11... | collective-permute-start | bytes 2457608 | tf_op jit(solution)/shard_map/ppermute | solution.py:36
  38.5 0.0 collective-permute-start.9
  38.5 0.1 shard_map.71
  38.5 1.8 %collective-permute-start.7 = (bf16[64,3200]{1,0:T(8,128)(2,1)S(1)}, bf16[64,3200]{1,0:T(8,128)(2,1)S(1)}, u32[]{:S(2)}, u32[]{:S(2)}) collective-permute-start(bf16[64,3200]{1,0:T(8,128)(2,1)S(1)} %get-tuple-element.55), channel_id=1, source_target_pairs={{0,6},{1,25},{2,0},{3,27},{4,2},{5,29},{6,4},{7,31},{8,14},{9,1},{... | collective-permute-start | bytes 1228808 | tf_op jit(solution)/shard_map/ppermute | solution.py:36
  40.4 0.0 collective-permute-start.8
  40.4 0.1 collective-permute-done.10.high_other
  40.4 1.2 %collective-permute-done.9.low_other = bf16[128,3200]{1,0:T(8,128)(2,1)S(1)} collective-permute-done((bf16[128,3200]{1,0:T(8,128)(2,1)S(1)}, bf16[128,3200]{1,0:T(8,128)(2,1)S(1)}, u32[]{:S(2)}, u32[]{:S(2)}) %collective-permute-start.9) | collective-permute-done | bytes 819232 | tf_op jit(solution)/shard_map/ppermute | solution.py:36
  41.6 0.0 copy-done
  41.6 0.0 copy-done.2
  41.6 7.1 %shard_map.72 = (bf16[768,1408]{1,0:T(8,128)(2,1)}, f32[32,128]{1,0:T(8,128)S(1)}, f32[144,1408]{1,0:T(8,128)S(1)}) custom-call(s32[4]{0:T(128)S(1)} %get-tuple-element.43.place, bf16[128,3200]{1,0:T(8,128)(2,1)S(1)} %collective-permute-done.4.low, bf16[128,3200]{1,0:T(8,128)(2,1)S(1)} %collective-permute-done.5.high, ...), custom_call_target="tpu_custom_call" | custom-call | flops 1 | bytes 1 | tf_op jit(solution)/shard_map/pallas_call | solution.py:350
  48.7 0.0 collective-permute-done.7.refs_0_
  48.7 0.0 collective-permute-done.8.refs_1_
  48.7 0.1 shard_map.73.mine
  48.8 2.7 %collective-permute-start.11 = (bf16[128,3200]{1,0:T(8,128)(2,1)S(1)}, bf16[128,3200]{1,0:T(8,128)(2,1)S(1)}, u32[]{:S(2)}, u32[]{:S(2)}) collective-permute-start(bf16[128,3200]{1,0:T(8,128)(2,1)S(1)} %shard_map.73.mine), channel_id=1, source_target_pairs={{0,1},{1,0},{2,3},{3,2},{4,5},{5,4},{6,7},{7,6},{8,9},{9,8},{10,11... | collective-permute-start | bytes 2457608 | tf_op jit(solution)/shard_map/ppermute | solution.py:36
  51.5 2.0 %collective-permute-done.11.theirs = bf16[128,3200]{1,0:T(8,128)(2,1)S(1)} collective-permute-done((bf16[128,3200]{1,0:T(8,128)(2,1)S(1)}, bf16[128,3200]{1,0:T(8,128)(2,1)S(1)}, u32[]{:S(2)}, u32[]{:S(2)}) %collective-permute-start.11) | collective-permute-done | bytes 819232 | tf_op jit(solution)/shard_map/ppermute | solution.py:36
  53.4 2.1 %shard_map.74 = (f32[32,128]{1,0:T(8,128)}, bf16[192,3072]{1,0:T(8,128)(2,1)S(1)}, f32[192,128]{1,0:T(8,128)S(1)}) custom-call(s32[4]{0:T(128)S(1)} %get-tuple-element.43.place, bf16[128,3200]{1,0:T(8,128)(2,1)S(1)} %shard_map.73.mine, bf16[128,3200]{1,0:T(8,128)(2,1)S(1)} %collective-permute-done.11.theirs, f32[192,3072]{1,0:T(8,128)S(1)} %get-tuple-element.64.ahead, ...), custom_call_target="tpu_custom_call" | custom-call | flops 1 | bytes 1 | tf_op jit(solution)/shard_map/pallas_call | solution.py:393
  55.5 4.1 %all-to-all-start = ((f32[32,1,128]{2,1,0:T(1,128)}), f32[32,1,128]{2,1,0:T(1,128)S(1)}, u32[]{:S(2)}, u32[]{:S(2)}) async-start(f32[32,1,128]{2,1,0:T(1,128)} %bitcast.13), calls=%async_computation | async-start | bytes 32768 | tf_op jit(solution)/shard_map/all_to_all | solution.py:515
  59.7 5.9 %shard_map.75 = bf16[768,1408]{1,0:T(8,128)(2,1)} custom-call(s32[4]{0:T(128)S(1)} %get-tuple-element.43.place, bf16[192,3072]{1,0:T(8,128)(2,1)S(1)} %get-tuple-element.66.packed, f32[192,128]{1,0:T(8,128)S(1)} %get-tuple-element.67.gates, bf16[3072,1408]{1,0:T(8,128)(2,1)} %copy-done, ...), custom_call_target="tpu_custom_call", output_to_operand_aliasing={{}: (5, {})} | custom-call | flops 1660944384 | bytes 1 | tf_op jit(solution)/shard_map/pallas_call | solution.py:452
  65.5 1.1 %all-to-all-done = f32[32,1,128]{2,1,0:T(1,128)S(1)} async-done(((f32[32,1,128]{2,1,0:T(1,128)}), f32[32,1,128]{2,1,0:T(1,128)S(1)}, u32[]{:S(2)}, u32[]{:S(2)}) %all-to-all-start) | async-done | bytes 16416 | tf_op jit(solution)/shard_map/all_to_all | solution.py:515
  66.6 0.8 %shard_map.76 = f32[4,32]{1,0:T(4,128)} custom-call(f32[32,128]{1,0:T(8,128)S(1)} %bitcast.23, s32[8,128]{1,0:T(8,128)S(1)} %get-tuple-element.71.lines), custom_call_target="tpu_custom_call" | custom-call | tf_op jit(solution)/shard_map/pallas_call | solution.py:517
  (5 shorter events, 0.1 us)
Async XLA Ops:
  0.6 10.4 %collective-permute-start = (bf16[32,3072]{1,0:T(8,128)(2,1)}, bf16[32,3072]{1,0:T(8,128)(2,1)S(1)}, u32[]{:S(2)}, u32[]{:S(2)}) collective-permute-start(bf16[32,3072]{1,0:T(8,128)(2,1)} %bitcast.29), channel_id=1, source_target_pairs={{0,224},{1,225},{2,226},{3,227},{4,228},{5,229},{6,230},{7,231},{8... | collective-permute-start | bytes 589832 | tf_op jit(solution)/shard_map/ppermute | solution.py:36
  7.2 0.7 %copy-start.3 = (s32[1,32,4]{1,2,0:T(4,128)S(1)}, s32[1,32,4]{1,2,0:T(4,128)}, u32[]{:S(2)}) copy-start(s32[1,32,4]{1,2,0:T(4,128)} %param.6) | copy-start | bytes 1540
  7.9 0.7 %copy-start.4 = (bf16[1,32,4]{1,2,0:T(4,128)(2,1)S(1)}, bf16[1,32,4]{1,2,0:T(4,128)(2,1)}, u32[]{:S(2)}) copy-start(bf16[1,32,4]{1,2,0:T(4,128)(2,1)} %param.7) | copy-start | bytes 772
  11.0 11.0 %collective-permute-start.1 = (bf16[32,3200]{1,0:T(8,128)(2,1)S(1)}, bf16[32,3200]{1,0:T(8,128)(2,1)S(1)}, u32[]{:S(2)}, u32[]{:S(2)}) collective-permute-start(bf16[32,3200]{1,0:T(8,128)(2,1)S(1)} %pad_maximum_fusion), channel_id=1, source_target_pairs={{0,8},{1,3},{2,10},{3,5},{4,12},{5,7},{6,14},{7,1},{8,16},{9,11},{... | collective-permute-start | bytes 614408 | tf_op jit(solution)/shard_map/ppermute | solution.py:36
  12.4 9.7 %collective-permute-start.2 = (bf16[32,3200]{1,0:T(8,128)(2,1)S(1)}, bf16[32,3200]{1,0:T(8,128)(2,1)S(1)}, u32[]{:S(2)}, u32[]{:S(2)}) collective-permute-start(bf16[32,3200]{1,0:T(8,128)(2,1)S(1)} %pad_maximum_fusion), channel_id=1, source_target_pairs={{0,24},{1,7},{2,26},{3,1},{4,28},{5,3},{6,30},{7,5},{8,0},{9,15},{... | collective-permute-start | bytes 614408 | tf_op jit(solution)/shard_map/ppermute | solution.py:36
  13.9 8.2 %collective-permute-start.3 = (bf16[32,3200]{1,0:T(8,128)(2,1)S(1)}, bf16[32,3200]{1,0:T(8,128)(2,1)S(1)}, u32[]{:S(2)}, u32[]{:S(2)}) collective-permute-start(bf16[32,3200]{1,0:T(8,128)(2,1)S(1)} %pad_maximum_fusion), channel_id=1, source_target_pairs={{0,16},{1,5},{2,18},{3,7},{4,20},{5,1},{6,22},{7,3},{8,24},{9,13},... | collective-permute-start | bytes 614408 | tf_op jit(solution)/shard_map/ppermute | solution.py:36
  15.5 1.6 %copy-start.1 = (bf16[1,1,768,1408]{3,2,1,0:T(8,128)(2,1)S(1)}, bf16[1,1,768,1408]{3,2,1,0:T(8,128)(2,1)}, u32[]{:S(2)}) copy-start(bf16[1,1,768,1408]{3,2,1,0:T(8,128)(2,1)} %param.9) | copy-start | bytes 6488068
  22.1 19.6 %copy-start = (bf16[3072,1408]{1,0:T(8,128)(2,1)}, bf16[3072,1408]{1,0:T(8,128)(2,1)S(1)}, u32[]{:S(2)}) copy-start(bf16[3072,1408]{1,0:T(8,128)(2,1)S(1)} %get-tuple-element.50.turned) | copy-start | bytes 25952260
  22.2 5.0 %collective-permute-start.6 = (bf16[128,3200]{1,0:T(8,128)(2,1)S(1)}, bf16[128,3200]{1,0:T(8,128)(2,1)S(1)}, u32[]{:S(2)}, u32[]{:S(2)}) collective-permute-start(bf16[128,3200]{1,0:T(8,128)(2,1)S(1)} %constant_dynamic-update-slice_fusion.mine), channel_id=1, source_target_pairs={{0,1},{1,0},{2,3},{3,2},{4,5},{5,4},{6,7},{7,6},{8,9},{9,8},{10,11... | collective-permute-start | bytes 2457608 | tf_op jit(solution)/shard_map/ppermute | solution.py:36
  24.5 12.7 %collective-permute-start.4 = (bf16[128,3200]{1,0:T(8,128)(2,1)S(1)}, bf16[128,3200]{1,0:T(8,128)(2,1)S(1)}, u32[]{:S(2)}, u32[]{:S(2)}) collective-permute-start(bf16[128,3200]{1,0:T(8,128)(2,1)S(1)} %constant_dynamic-update-slice_fusion.mine), channel_id=1, source_target_pairs={{0,2},{1,9},{2,4},{3,11},{4,6},{5,13},{6,0},{7,15},{8,10},{9,17},{... | collective-permute-start | bytes 2457608 | tf_op jit(solution)/shard_map/ppermute | solution.py:36
  24.8 12.4 %collective-permute-start.5 = (bf16[128,3200]{1,0:T(8,128)(2,1)S(1)}, bf16[128,3200]{1,0:T(8,128)(2,1)S(1)}, u32[]{:S(2)}, u32[]{:S(2)}) collective-permute-start(bf16[128,3200]{1,0:T(8,128)(2,1)S(1)} %constant_dynamic-update-slice_fusion.mine), channel_id=1, source_target_pairs={{0,6},{1,25},{2,0},{3,27},{4,2},{5,29},{6,4},{7,31},{8,14},{9,1},{... | collective-permute-start | bytes 2457608 | tf_op jit(solution)/shard_map/ppermute | solution.py:36
  27.1 14.5 %copy-start.2 = (bf16[1,1,768,1408]{3,2,1,0:T(8,128)(2,1)S(1)}, bf16[1,1,768,1408]{3,2,1,0:T(8,128)(2,1)}, u32[]{:S(2)}) copy-start(bf16[1,1,768,1408]{3,2,1,0:T(8,128)(2,1)} %param.9) | copy-start | bytes 6488068
  37.2 3.3 %collective-permute-start.10 = (bf16[128,3200]{1,0:T(8,128)(2,1)S(1)}, bf16[128,3200]{1,0:T(8,128)(2,1)S(1)}, u32[]{:S(2)}, u32[]{:S(2)}) collective-permute-start(bf16[128,3200]{1,0:T(8,128)(2,1)S(1)} %collective-permute-done.5.high), channel_id=1, source_target_pairs={{0,1},{1,0},{2,3},{3,2},{4,5},{5,4},{6,7},{7,6},{8,9},{9,8},{10,11... | collective-permute-start | bytes 2457608 | tf_op jit(solution)/shard_map/ppermute | solution.py:36
  38.5 3.1 %collective-permute-start.9 = (bf16[128,3200]{1,0:T(8,128)(2,1)S(1)}, bf16[128,3200]{1,0:T(8,128)(2,1)S(1)}, u32[]{:S(2)}, u32[]{:S(2)}) collective-permute-start(bf16[128,3200]{1,0:T(8,128)(2,1)S(1)} %collective-permute-done.4.low), channel_id=1, source_target_pairs={{0,1},{1,0},{2,3},{3,2},{4,5},{5,4},{6,7},{7,6},{8,9},{9,8},{10,11... | collective-permute-start | bytes 2457608 | tf_op jit(solution)/shard_map/ppermute | solution.py:36
  38.5 10.1 %collective-permute-start.7 = (bf16[64,3200]{1,0:T(8,128)(2,1)S(1)}, bf16[64,3200]{1,0:T(8,128)(2,1)S(1)}, u32[]{:S(2)}, u32[]{:S(2)}) collective-permute-start(bf16[64,3200]{1,0:T(8,128)(2,1)S(1)} %get-tuple-element.55), channel_id=1, source_target_pairs={{0,6},{1,25},{2,0},{3,27},{4,2},{5,29},{6,4},{7,31},{8,14},{9,1},{... | collective-permute-start | bytes 1228808 | tf_op jit(solution)/shard_map/ppermute | solution.py:36
  40.4 8.3 %collective-permute-start.8 = (bf16[64,3200]{1,0:T(8,128)(2,1)S(1)}, bf16[64,3200]{1,0:T(8,128)(2,1)S(1)}, u32[]{:S(2)}, u32[]{:S(2)}) collective-permute-start(bf16[64,3200]{1,0:T(8,128)(2,1)S(1)} %get-tuple-element.56), channel_id=1, source_target_pairs={{0,2},{1,9},{2,4},{3,11},{4,6},{5,13},{6,0},{7,15},{8,10},{9,17},{... | collective-permute-start | bytes 1228808 | tf_op jit(solution)/shard_map/ppermute | solution.py:36
  48.8 4.7 %collective-permute-start.11 = (bf16[128,3200]{1,0:T(8,128)(2,1)S(1)}, bf16[128,3200]{1,0:T(8,128)(2,1)S(1)}, u32[]{:S(2)}, u32[]{:S(2)}) collective-permute-start(bf16[128,3200]{1,0:T(8,128)(2,1)S(1)} %shard_map.73.mine), channel_id=1, source_target_pairs={{0,1},{1,0},{2,3},{3,2},{4,5},{5,4},{6,7},{7,6},{8,9},{9,8},{10,11... | collective-permute-start | bytes 2457608 | tf_op jit(solution)/shard_map/ppermute | solution.py:36
  55.5 11.1 %all-to-all-start = ((f32[32,1,128]{2,1,0:T(1,128)}), f32[32,1,128]{2,1,0:T(1,128)S(1)}, u32[]{:S(2)}, u32[]{:S(2)}) async-start(f32[32,1,128]{2,1,0:T(1,128)} %bitcast.13), calls=%async_computation | async-start | bytes 32768 | tf_op jit(solution)/shard_map/all_to_all | solution.py:515

commit v4 on v3

--- a/solution.py
+++ b/solution.py
@@ -1,3 +1,5 @@
+import functools
+
 import jax
 import jax.numpy as jnp
 from jax import lax
@@ -56,7 +58,8 @@
     return jnp.concatenate(parts, axis=0)
 
 
-def pack(expert, token_refs, packed, gates):
+def pack(expert, token_refs, packed, gates, weights=None):
+    dots = []
     lane = lax.broadcasted_iota(jnp.int32, (16, META), 1)
     line = lax.broadcasted_iota(jnp.int32, (16, META), 0)
     pick = ((line == 0) & (lane == expert)).astype(F32).astype(BF16)
@@ -75,13 +78,20 @@
         chosen = (
             lax.broadcasted_iota(jnp.int32, (height, count), 0) == target
         ).astype(F32).astype(BF16)
+        dot = jnp.zeros((height, META), F32)
         for start in range(0, width, 512):
-            packed[at : at + height, start : start + 512] = jnp.dot(
-                chosen, ref[:, start : start + 512], preferred_element_type=F32
-            ).astype(BF16)
+            value = jnp.dot(chosen, ref[:, start : start + 512], preferred_element_type=F32)
+            packed[at : at + height, start : start + 512] = value.astype(BF16)
+            if weights is None:
+                continue
+            for col in range(0, 512, META):
+                factor = weights[at : at + height, start + col : start + col + META]
+                dot += value[:, col : col + META] * factor
+        dots.append(jnp.sum(dot, axis=1, keepdims=True))
         own = jnp.dot(chosen, meta, preferred_element_type=F32).astype(BF16)
         gates[at : at + height, :] = jnp.dot(own, spread, preferred_element_type=F32)
         at += height
+    return dots
 
 
 def multiply(packed, turned, out):
@@ -203,10 +213,41 @@
     return kind, chip_of(place, x, y)
 
 
-def turn_kernel(place, hidden, weight, turned, ahead, held, far, sems):
+def turn_kernel(place, weight, turned, held, sems):
     units, width = weight.shape
-    starts = range(0, units, TILE)
-    spans = [pl.ds(at, min(TILE, units - at)) for at in starts]
+    copies = [
+        pltpu.make_async_copy(
+            weight.at[pl.ds(at, META), :], held.at[pl.ds(at, META), :], sems.at[at // META]
+        )
+        for at in range(0, units, META)
+    ]
+    for copy in copies:
+        copy.start()
+    for copy, at in zip(copies, range(0, units, META)):
+        copy.wait()
+        for col in range(0, width, 512):
+            turned[col : col + 512, at : at + META] = held[at : at + META, col : col + 512].T
+
+
+def turn(place, weight):
+    units, width = weight.shape
+    return pl.pallas_call(
+        turn_kernel,
+        out_shape=pltpu.VMEM((width, units), BF16),
+        in_specs=[smem(), anywhere()],
+        out_specs=vmem(),
+        scratch_shapes=[
+            pltpu.VMEM((units, width), BF16),
+            pltpu.SemaphoreType.DMA((units // META,)),
+        ],
+        compiler_params=params(),
+        cost_estimate=small(),
+    )(place, pltpu.with_memory_space_constraint(weight, pltpu.HBM))
+
+
+def ahead_kernel(place, hidden, weight, out, held, far, sems):
+    units, width = weight.shape
+    spans = [pl.ds(at, min(512, units - at)) for at in range(0, units, 512)]
     copies = [
         pltpu.make_async_copy(weight.at[span, :], held.at[span, :], sems.at[n])
         for n, span in enumerate(spans)
@@ -217,29 +258,29 @@
         kind, chip = far_block(place, n)
         pair = hidden[pair_rows(chip), :].astype(F32)
         far[n * CAP : (n + 1) * CAP, :] = jnp.where(kind == 0, pair[:CAP], pair[CAP:])
-    for n, at in enumerate(starts):
+    for n, span in enumerate(spans):
         copies[n].wait()
-        to = min(at + TILE, units)
-        left = far[:, at:to].astype(BF16)
+        at = slice(span.start, span.start + span.size)
+        left = far[:, at].astype(BF16)
         for col in range(0, width, 512):
-            span = slice(col, col + 512)
-            turned[span, at:to] = held[at:to, span].T
-            value = jnp.dot(left, held[at:to, span], preferred_element_type=F32)
-            ahead[:, span] = value if n == 0 else ahead[:, span] + value
-
-
-def turn(place, hidden, weight):
+            value = jnp.dot(left, held[at, col : col + 512], preferred_element_type=F32)
+            if n:
+                value = out[:, col : col + 512] + value
+            out[:, col : col + 512] = value
+
+
+def ahead_of(place, hidden, weight):
     units, width = weight.shape
     height = hidden.shape[0] // 4
     return pl.pallas_call(
-        turn_kernel,
-        out_shape=(pltpu.VMEM((width, units), BF16), pltpu.VMEM((height, width), F32)),
+        ahead_kernel,
+        out_shape=pltpu.VMEM((height, width), F32),
         in_specs=[smem(), vmem(), anywhere()],
-        out_specs=(vmem(), vmem()),
+        out_specs=vmem(),
         scratch_shapes=[
             pltpu.VMEM((units, width), BF16),
             pltpu.VMEM((height, units), F32),
-            pltpu.SemaphoreType.DMA((pl.cdiv(units, TILE),)),
+            pltpu.SemaphoreType.DMA((pl.cdiv(units, 512),)),
         ],
         compiler_params=params(),
         cost_estimate=small(),
@@ -368,43 +409,39 @@
     )(place, *tokens, turned, hidden, near, near_gates)
 
 
-def sums_kernel(place, mine, theirs, ahead, early, sums, packed, gates):
+def sums_kernel(which, place, tokens, ahead, early, sums, packed, gates):
     sums[...] = early[...]
-    pack(place[3], (mine, theirs), packed, gates)
-    height, width = packed.shape
+    height = packed.shape[0]
+    at = slice(which * height, (which + 1) * height)
+    (total,) = pack(place[3], (tokens,), packed, gates, ahead.at[at, :])
     diagonal = lax.broadcasted_iota(jnp.int32, (CAP, META), 0) == lax.broadcasted_iota(
         jnp.int32, (CAP, META), 1
     )
-    for n in range(height // CAP):
-        block = slice(n * CAP, (n + 1) * CAP)
-        total = jnp.zeros((CAP, META), F32)
-        for col in range(0, width, META):
-            span = slice(col, col + META)
-            total += packed[block, span].astype(F32) * ahead[block, span]
-        total = jnp.sum(total, axis=1, keepdims=True)
-        kind, chip = far_block(place, n)
-        sums[pl.ds(chip * 2 + kind, 1), :] = jnp.sum(
-            jnp.where(diagonal, total, 0.0), axis=0, keepdims=True
-        )
-
-
-def sums_of(place, mine, theirs, ahead, early):
+    for n in range(4):
+        kind, chip = far_block(place, which * 4 + n)
+        line = jnp.where(diagonal, total[n * CAP : (n + 1) * CAP], 0.0)
+        sums[pl.ds(chip * 2 + kind, 1), :] = jnp.sum(line, axis=0, keepdims=True)
+
+
+def sums_of(which, place, tokens, ahead, early):
     height, width = ahead.shape
     return pl.pallas_call(
-        sums_kernel,
+        functools.partial(sums_kernel, which),
         out_shape=(
             pltpu.VMEM(early.shape, F32),
-            pltpu.VMEM((height, width), BF16),
-            pltpu.VMEM((height, META), F32),
+            pltpu.VMEM((height // 2, width), BF16),
+            pltpu.VMEM((height // 2, META), F32),
         ),
-        in_specs=[smem()] + [vmem()] * 4,
+        in_specs=[smem()] + [vmem()] * 3,
         out_specs=(vmem(), vmem(), vmem()),
         compiler_params=params(),
         cost_estimate=small(),
-    )(place, mine, theirs, ahead, early)
-
-
-def far_kernel(place, packed, gates, turned, halves, _, grad, held, far, stage, sems, loads):
+    )(place, tokens, ahead, early)
+
+
+def far_kernel(
+    place, mine, theirs, gates, other_gates, turned, halves, _, grad, held, far, far_scales, stage, sems, loads
+):
     units = far.shape[1]
     spans = [pl.ds(at, 512) for at in range(0, held.shape[0], 512)]
     copies = [
@@ -416,9 +453,12 @@
     for n, span in enumerate(spans):
         copies[n].wait()
         at = slice(span.start, span.start + span.size)
-        value = jnp.dot(packed[:, at], held[at, :], preferred_element_type=F32)
+        rows_of = jnp.concatenate([mine[:, at], theirs[:, at]], axis=0)
+        value = jnp.dot(rows_of, held[at, :], preferred_element_type=F32)
         far[...] = value if n == 0 else far[...] + value
     copies = []
+    scales = jnp.concatenate([gates[...], other_gates[...]], axis=0)
+    far_scales[...] = scales
     for i in OFFSETS:
         for j in OFFSETS:
             if i != 2 and j != 2:
@@ -427,7 +467,7 @@
             for kind, along, across in ((0, i, j), (1, j, i)):
                 if across == 2:
                     span = block_rows(place, kind, 4, OFFSETS.index(along))
-                    pieces.append((far, gates[span, :], span))
+                    pieces.append((far, far_scales[span, :], span))
                 else:
                     n = HALVES.index((kind, i, j))
                     pieces.append((halves, None, pl.ds(n * CAP, CAP)))
@@ -446,27 +486,31 @@
         copy.wait()
 
 
-def far_of(place, packed, gates, turned, halves, grad):
+def far_of(place, mine, theirs, gates, other_gates, turned, halves, grad):
     width, units = turned.shape
-    height = packed.shape[0]
+    height = 2 * mine.shape[0]
     return pl.pallas_call(
         far_kernel,
         out_shape=jax.ShapeDtypeStruct(grad.shape, BF16),
-        in_specs=[smem(), vmem(), vmem(), anywhere(), vmem(), anywhere()],
+        in_specs=[smem()] + [vmem()] * 4 + [anywhere(), vmem(), anywhere()],
         out_specs=anywhere(),
         scratch_shapes=[
             pltpu.VMEM((width, units), BF16),
             pltpu.VMEM((height, units), F32),
+            pltpu.VMEM((height, META), F32),
             pltpu.VMEM((7, 2 * CAP, units), BF16),
             pltpu.SemaphoreType.DMA((7,)),
             pltpu.SemaphoreType.DMA((width // 512,)),
         ],
-        input_output_aliases={5: 0},
+        input_output_aliases={7: 0},
         compiler_params=params(),
         cost_estimate=pl.CostEstimate(
             flops=2 * height * units * turned.shape[0], bytes_accessed=1, transcendentals=0
         ),
-    )(place, packed, gates, pltpu.with_memory_space_constraint(turned, pltpu.HBM), halves, grad)
+    )(
+        place, mine, theirs, gates, other_gates,
+        pltpu.with_memory_space_constraint(turned, pltpu.HBM), halves, grad,
+    )
 
 
 def gather_kernel(totals, lines, out):
@@ -495,15 +539,15 @@
     own, place = lax.optimization_barrier((own, place))
 
     ahead, back, across = [moved(own, first(k)) for k in (1, 3, 2)]
-    turned, ahead_far = turn(place, saved, weight)
-    ahead, back, across, turned, ahead_far = lax.optimization_barrier(
-        (ahead, back, across, turned, ahead_far)
-    )
+    turned = turn(place, weight)
+    ahead, back, across, turned = lax.optimization_barrier((ahead, back, across, turned))
     near = rows(own, ahead, back, across)
     low, high = moved(near, second(1)), moved(near, second(3))
     near_other = moved(near, other_core)
+    near_other, later = lax.optimization_barrier((near_other, place))
     near_done = near_of(place, near, near_other, turned)
-    low, high, *near_done = lax.optimization_barrier((low, high, *near_done))
+    ahead_far = ahead_of(later, saved, weight)
+    low, high, ahead_far, *near_done = lax.optimization_barrier((low, high, ahead_far, *near_done))
     left, right = halves_of(high, low)
     far = moved(left, second(3)), moved(right, second(1))
     tokens = low, high, moved(low, other_core), moved(high, other_core)
@@ -511,9 +555,10 @@
     *far, grad, sums, halves = lax.optimization_barrier((*far, grad, sums, halves))
     far = join(*far)
     far_other = moved(far, other_core)
-    sums, packed, far_gates = sums_of(place, far, far_other, ahead_far, sums)
+    sums, mine, far_gates = sums_of(0, place, far, ahead_far, sums)
+    sums, theirs, other_gates = sums_of(1, place, far_other, ahead_far, sums)
     totals = lax.all_to_all(sums, ("dp", "expert"), split_axis=0, concat_axis=0, tiled=True)
-    grad = far_of(place, packed, far_gates, turned, halves, grad)
+    grad = far_of(place, mine, theirs, far_gates, other_gates, turned, halves, grad)
     gate_grad = pl.pallas_call(
         gather_kernel,
         out_shape=jax.ShapeDtypeStruct(ids.shape, F32),

time: 67.6 us -> 66.1 us (0.978)
  waiting for transfers between devices: 12.2 us -> 6.69 us
  Pallas kernels: 25.4 us -> 30.8 us
  local copies, waits for them, and re-layouts: 3.06 us -> 1.45 us
    ppermute x12, waiting for transfers between devices: 11.1 us -> 5.65 us  [moved(): return lax.ppermute(x, AXES, pairs)]
    pallas_call x2 -> x4, Pallas kernels: 7.02 us -> 12.4 us  [the longest x1 4.98 us: ahead_of(): pl.pallas_call(ahead_kernel, out_shape=pltpu.VMEM((height, width), F32),...]
    unnamed x13 -> x11, local copies, waits for them, and re-layouts: 3.03 us -> 1.43 us
  transfers between devices with their start and end apart: 13 -> 13, of which waited for: 6 -> 7; matrix products, arithmetic and copies ran while one was open for 0% -> 0% of each run, Pallas kernels for 33% -> 43%
where the time goes in v4:
time: 66.1 us; the launch traced here: 65.9 us
  Pallas kernels  30.8 us (47%)
  starting transfers between devices  26.1 us (39%)
  waiting for transfers between devices  6.69 us (10%)
  local copies, waits for them, and re-layouts  1.45 us (2%)
  between operations  0.78 us (1%)
    ppermute x12, starting transfers between devices, moved(): return lax.ppermute(x, AXES, pairs)  21.8 us
    pallas_call x1, Pallas kernels, mid_of(): pl.pallas_call(mid_kernel, out_shape=(jax.ShapeDtypeStruct(hidden.shape,...  7.04 us
    pallas_call x1, Pallas kernels, far_of(): pl.pallas_call(far_kernel, out_shape=jax.ShapeDtypeStruct(grad.shape, BF1...  5.9 us
    ppermute x12, waiting for transfers between devices, moved(): return lax.ppermute(x, AXES, pairs)  5.65 us
    pallas_call x1, Pallas kernels, ahead_of(): pl.pallas_call(ahead_kernel, out_shape=pltpu.VMEM((height, width), F32),...  4.98 us
    pallas_call x1, Pallas kernels, turn(): pl.pallas_call(turn_kernel, out_shape=pltpu.VMEM((width, units), BF16), i...  4.63 us
    all_to_all x1, starting transfers between devices, on_device(): lax.all_to_all(sums, ('dp', 'expert'), split_axis=0, concat_axis=0, tiled...  4.34 us
    pallas_call x1, Pallas kernels, near_of(): pl.pallas_call(near_kernel, out_shape=(pltpu.VMEM((height, units), F32),...  3.38 us
  transfers between devices with their start and end apart: 13, of which 7 were waited for; matrix products, arithmetic and copies ran while one was open for 0% of the time, Pallas kernels for 43%

profile of v4, /device:TPU:1, one launch (start us, length us, event | category | flops | bytes accessed | tf_op | source)
XLA Modules:
  0.0 65.9 jit_solution(12989882186170213047)
XLA Ops:
  0.6 6.5 %collective-permute-start = (bf16[32,3072]{1,0:T(8,128)(2,1)}, bf16[32,3072]{1,0:T(8,128)(2,1)S(1)}, u32[]{:S(2)}, u32[]{:S(2)}) collective-permute-start(bf16[32,3072]{1,0:T(8,128)(2,1)} %bitcast.30), channel_id=1, source_target_pairs={{0,224},{1,225},{2,226},{3,227},{4,228},{5,229},{6,230},{7,231},{8... | collective-permute-start | bytes 589832 | tf_op jit(solution)/shard_map/ppermute | solution.py:38
  7.1 0.1 pad_add_fusion.place
  7.2 0.0 copy-start.2
  7.2 0.7 %copy-done.2 = s32[1,32,4]{1,2,0:T(4,128)S(1)} copy-done((s32[1,32,4]{1,2,0:T(4,128)S(1)}, s32[1,32,4]{1,2,0:T(4,128)}, u32[]{:S(2)}) %copy-start.2) | copy-done | bytes 536
  7.9 0.0 copy-start.3
  7.9 0.7 %copy-done.3 = bf16[1,32,4]{1,2,0:T(4,128)(2,1)S(1)} copy-done((bf16[1,32,4]{1,2,0:T(4,128)(2,1)S(1)}, bf16[1,32,4]{1,2,0:T(4,128)(2,1)}, u32[]{:S(2)}) %copy-start.3) | copy-done | bytes 280
  8.6 1.1 %shard_map.68 = (bf16[32,128]{1,0:T(8,128)(2,1)S(1)}, s32[8,128]{1,0:T(8,128)S(1)}, s32[4]{0:T(128)S(1)}) custom-call(s32[4]{0:T(128)S(1)} %pad_add_fusion.place, s32[4,32]{1,0:T(4,128)S(1)} %bitcast.24, bf16[4,32]{1,0:T(4,128)(2,1)S(1)} %bitcast.25), custom_call_target="tpu_custom_call" | custom-call | tf_op jit(solution)/shard_map/pallas_call | solution.py:158
  9.7 1.3 %collective-permute-done = bf16[32,3072]{1,0:T(8,128)(2,1)S(1)} collective-permute-done((bf16[32,3072]{1,0:T(8,128)(2,1)}, bf16[32,3072]{1,0:T(8,128)(2,1)S(1)}, u32[]{:S(2)}, u32[]{:S(2)}) %collective-permute-start) | collective-permute-done | bytes 196640 | tf_op jit(solution)/shard_map/ppermute | solution.py:38
  11.0 1.4 %collective-permute-start.1 = (bf16[32,3200]{1,0:T(8,128)(2,1)S(1)}, bf16[32,3200]{1,0:T(8,128)(2,1)S(1)}, u32[]{:S(2)}, u32[]{:S(2)}) collective-permute-start(bf16[32,3200]{1,0:T(8,128)(2,1)S(1)} %pad_maximum_fusion), channel_id=1, source_target_pairs={{0,8},{1,3},{2,10},{3,5},{4,12},{5,7},{6,14},{7,1},{8,16},{9,11},{... | collective-permute-start | bytes 614408 | tf_op jit(solution)/shard_map/ppermute | solution.py:38
  12.4 1.5 %collective-permute-start.2 = (bf16[32,3200]{1,0:T(8,128)(2,1)S(1)}, bf16[32,3200]{1,0:T(8,128)(2,1)S(1)}, u32[]{:S(2)}, u32[]{:S(2)}) collective-permute-start(bf16[32,3200]{1,0:T(8,128)(2,1)S(1)} %pad_maximum_fusion), channel_id=1, source_target_pairs={{0,24},{1,7},{2,26},{3,1},{4,28},{5,3},{6,30},{7,5},{8,0},{9,15},{... | collective-permute-start | bytes 614408 | tf_op jit(solution)/shard_map/ppermute | solution.py:38
  13.9 1.6 %collective-permute-start.3 = (bf16[32,3200]{1,0:T(8,128)(2,1)S(1)}, bf16[32,3200]{1,0:T(8,128)(2,1)S(1)}, u32[]{:S(2)}, u32[]{:S(2)}) collective-permute-start(bf16[32,3200]{1,0:T(8,128)(2,1)S(1)} %pad_maximum_fusion), channel_id=1, source_target_pairs={{0,16},{1,5},{2,18},{3,7},{4,20},{5,1},{6,22},{7,3},{8,24},{9,13},... | collective-permute-start | bytes 614408 | tf_op jit(solution)/shard_map/ppermute | solution.py:38
  15.5 4.6 %shard_map.69.turned = bf16[3072,1408]{1,0:T(8,128)(2,1)S(1)} custom-call(s32[4]{0:T(128)S(1)} %get-tuple-element.51.place, bf16[1408,3072]{1,0:T(8,128)(2,1)} %bitcast.26), custom_call_target="tpu_custom_call" | custom-call | flops 1 | bytes 1 | tf_op jit(solution)/shard_map/pallas_call | solution.py:234
  20.1 0.0 copy-start
  20.1 0.0 collective-permute-done.1
  20.1 0.0 collective-permute-done.2
  20.2 0.5 collective-permute-done.3
  20.7 0.0 copy-start.1
  20.7 2.6 %collective-permute-start.6 = (bf16[128,3200]{1,0:T(8,128)(2,1)S(1)}, bf16[128,3200]{1,0:T(8,128)(2,1)S(1)}, u32[]{:S(2)}, u32[]{:S(2)}) collective-permute-start(bf16[128,3200]{1,0:T(8,128)(2,1)S(1)} %constant_dynamic-update-slice_fusion.mine), channel_id=1, source_target_pairs={{0,1},{1,0},{2,3},{3,2},{4,5},{5,4},{6,7},{7,6},{8,9},{9,8},{10,11... | collective-permute-start | bytes 2457608 | tf_op jit(solution)/shard_map/ppermute | solution.py:38
  23.3 0.8 %collective-permute-start.4 = (bf16[128,3200]{1,0:T(8,128)(2,1)S(1)}, bf16[128,3200]{1,0:T(8,128)(2,1)S(1)}, u32[]{:S(2)}, u32[]{:S(2)}) collective-permute-start(bf16[128,3200]{1,0:T(8,128)(2,1)S(1)} %constant_dynamic-update-slice_fusion.mine), channel_id=1, source_target_pairs={{0,2},{1,9},{2,4},{3,11},{4,6},{5,13},{6,0},{7,15},{8,10},{9,17},{... | collective-permute-start | bytes 2457608 | tf_op jit(solution)/shard_map/ppermute | solution.py:38
  24.1 1.9 %collective-permute-start.5 = (bf16[128,3200]{1,0:T(8,128)(2,1)S(1)}, bf16[128,3200]{1,0:T(8,128)(2,1)S(1)}, u32[]{:S(2)}, u32[]{:S(2)}) collective-permute-start(bf16[128,3200]{1,0:T(8,128)(2,1)S(1)} %constant_dynamic-update-slice_fusion.mine), channel_id=1, source_target_pairs={{0,6},{1,25},{2,0},{3,27},{4,2},{5,29},{6,4},{7,31},{8,14},{9,1},{... | collective-permute-start | bytes 2457608 | tf_op jit(solution)/shard_map/ppermute | solution.py:38
  26.0 0.0 collective-permute-done.6.theirs
  26.0 3.4 %shard_map.71 = (f32[192,1408]{1,0:T(8,128)S(1)}, f32[192,128]{1,0:T(8,128)S(1)}) custom-call(s32[4]{0:T(128)S(1)} %get-tuple-element.51.place, bf16[128,3200]{1,0:T(8,128)(2,1)S(1)} %constant_dynamic-update-slice_fusion.mine, bf16[128,3200]{1,0:T(8,128)(2,1)S(1)} %collective-permute-done.6.theirs, bf16[3072,1408]{1,0:T(8,128)(2,1)S(1)} %shard_map.69.turned), custom_call_target="tpu_custom_call" | custom-call | flops 1 | bytes 1 | tf_op jit(solution)/shard_map/pallas_call | solution.py:298
  29.4 0.0 copy-done.1
  29.4 5.0 %shard_map.70.ahead = f32[192,3072]{1,0:T(8,128)S(1)} custom-call(s32[4]{0:T(128)S(1)} %get-tuple-element.51.place, bf16[768,1408]{1,0:T(8,128)(2,1)S(1)} %bitcast.21, bf16[1408,3072]{1,0:T(8,128)(2,1)} %bitcast.27), custom_call_target="tpu_custom_call" | custom-call | flops 1 | bytes 1 | tf_op jit(solution)/shard_map/pallas_call | solution.py:275
  34.4 1.6 %collective-permute-done.4.low = bf16[128,3200]{1,0:T(8,128)(2,1)S(1)} collective-permute-done((bf16[128,3200]{1,0:T(8,128)(2,1)S(1)}, bf16[128,3200]{1,0:T(8,128)(2,1)S(1)}, u32[]{:S(2)}, u32[]{:S(2)}) %collective-permute-start.4) | collective-permute-done | bytes 819232 | tf_op jit(solution)/shard_map/ppermute | solution.py:38
  36.0 0.0 collective-permute-done.5.high
  36.0 1.3 %collective-permute-start.10 = (bf16[128,3200]{1,0:T(8,128)(2,1)S(1)}, bf16[128,3200]{1,0:T(8,128)(2,1)S(1)}, u32[]{:S(2)}, u32[]{:S(2)}) collective-permute-start(bf16[128,3200]{1,0:T(8,128)(2,1)S(1)} %collective-permute-done.5.high), channel_id=1, source_target_pairs={{0,1},{1,0},{2,3},{3,2},{4,5},{5,4},{6,7},{7,6},{8,9},{9,8},{10,11... | collective-permute-start | bytes 2457608 | tf_op jit(solution)/shard_map/ppermute | solution.py:38
  37.3 0.0 collective-permute-start.9
  37.3 0.1 shard_map.72
  37.4 1.7 %collective-permute-start.7 = (bf16[64,3200]{1,0:T(8,128)(2,1)S(1)}, bf16[64,3200]{1,0:T(8,128)(2,1)S(1)}, u32[]{:S(2)}, u32[]{:S(2)}) collective-permute-start(bf16[64,3200]{1,0:T(8,128)(2,1)S(1)} %get-tuple-element.58), channel_id=1, source_target_pairs={{0,6},{1,25},{2,0},{3,27},{4,2},{5,29},{6,4},{7,31},{8,14},{9,1},{... | collective-permute-start | bytes 1228808 | tf_op jit(solution)/shard_map/ppermute | solution.py:38
  39.1 0.0 collective-permute-start.8
  39.1 0.2 collective-permute-done.10.high_other
  39.3 1.2 %collective-permute-done.9.low_other = bf16[128,3200]{1,0:T(8,128)(2,1)S(1)} collective-permute-done((bf16[128,3200]{1,0:T(8,128)(2,1)S(1)}, bf16[128,3200]{1,0:T(8,128)(2,1)S(1)}, u32[]{:S(2)}, u32[]{:S(2)}) %collective-permute-start.9) | collective-permute-done | bytes 819232 | tf_op jit(solution)/shard_map/ppermute | solution.py:38
  40.5 0.0 copy-done
  40.5 7.0 %shard_map.73 = (bf16[768,1408]{1,0:T(8,128)(2,1)}, f32[32,128]{1,0:T(8,128)S(1)}, f32[144,1408]{1,0:T(8,128)S(1)}) custom-call(s32[4]{0:T(128)S(1)} %get-tuple-element.51.place, bf16[128,3200]{1,0:T(8,128)(2,1)S(1)} %collective-permute-done.4.low, bf16[128,3200]{1,0:T(8,128)(2,1)S(1)} %collective-permute-done.5.high, ...), custom_call_target="tpu_custom_call" | custom-call | flops 1 | bytes 1 | tf_op jit(solution)/shard_map/pallas_call | solution.py:391
  47.5 0.0 collective-permute-done.7.refs_0_
  47.5 0.0 collective-permute-done.8.refs_1_
  47.5 0.1 shard_map.74.tokens
  47.6 2.6 %collective-permute-start.11 = (bf16[128,3200]{1,0:T(8,128)(2,1)S(1)}, bf16[128,3200]{1,0:T(8,128)(2,1)S(1)}, u32[]{:S(2)}, u32[]{:S(2)}) collective-permute-start(bf16[128,3200]{1,0:T(8,128)(2,1)S(1)} %shard_map.74.tokens), channel_id=1, source_target_pairs={{0,1},{1,0},{2,3},{3,2},{4,5},{5,4},{6,7},{7,6},{8,9},{9,8},{10,11... | collective-permute-start | bytes 2457608 | tf_op jit(solution)/shard_map/ppermute | solution.py:38
  50.1 1.1 %shard_map.75 = (f32[32,128]{1,0:T(8,128)S(1)}, bf16[96,3072]{1,0:T(8,128)(2,1)S(1)}, f32[96,128]{1,0:T(8,128)S(1)}) custom-call(s32[4]{0:T(128)S(1)} %get-tuple-element.51.place, bf16[128,3200]{1,0:T(8,128)(2,1)S(1)} %shard_map.74.tokens, f32[192,3072]{1,0:T(8,128)S(1)} %shard_map.70.ahead, f32[32,128]{1,0:T(8,128)S(1)} %get-tuple-element.68.early), custom_call_target="tpu_custom_call" | custom-call | flops 1 | bytes 1 | tf_op jit(solution)/shard_map/pallas_call | solution.py:428
  51.2 0.9 %collective-permute-done.11.tokens = bf16[128,3200]{1,0:T(8,128)(2,1)S(1)} collective-permute-done((bf16[128,3200]{1,0:T(8,128)(2,1)S(1)}, bf16[128,3200]{1,0:T(8,128)(2,1)S(1)}, u32[]{:S(2)}, u32[]{:S(2)}) %collective-permute-start.11) | collective-permute-done | bytes 819232 | tf_op jit(solution)/shard_map/ppermute | solution.py:38
  52.1 1.7 %shard_map.76 = (f32[32,128]{1,0:T(8,128)}, bf16[96,3072]{1,0:T(8,128)(2,1)S(1)}, f32[96,128]{1,0:T(8,128)S(1)}) custom-call(s32[4]{0:T(128)S(1)} %get-tuple-element.51.place, bf16[128,3200]{1,0:T(8,128)(2,1)S(1)} %collective-permute-done.11.tokens, f32[192,3072]{1,0:T(8,128)S(1)} %shard_map.70.ahead, f32[32,128]{1,0:T(8,128)S(1)} %get-tuple-element.70.early), custom_call_target="tpu_custom_call" | custom-call | flops 1 | bytes 1 | tf_op jit(solution)/shard_map/pallas_call | solution.py:428
  53.8 4.3 %all-to-all-start = ((f32[32,1,128]{2,1,0:T(1,128)}), f32[32,1,128]{2,1,0:T(1,128)S(1)}, u32[]{:S(2)}, u32[]{:S(2)}) async-start(f32[32,1,128]{2,1,0:T(1,128)} %bitcast.13), calls=%async_computation | async-start | bytes 32768 | tf_op jit(solution)/shard_map/all_to_all | solution.py:560
  58.1 5.9 %shard_map.77 = bf16[768,1408]{1,0:T(8,128)(2,1)} custom-call(s32[4]{0:T(128)S(1)} %get-tuple-element.51.place, bf16[96,3072]{1,0:T(8,128)(2,1)S(1)} %get-tuple-element.69.mine, bf16[96,3072]{1,0:T(8,128)(2,1)S(1)} %get-tuple-element.71.theirs, f32[96,128]{1,0:T(8,128)S(1)} %get-tuple-element.72.gates, ...), custom_call_target="tpu_custom_call", output_to_operand_aliasing={{}: (7, {})} | custom-call | flops 1660944384 | bytes 1 | tf_op jit(solution)/shard_map/pallas_call | solution.py:492
  64.1 1.0 %all-to-all-done = f32[32,1,128]{2,1,0:T(1,128)S(1)} async-done(((f32[32,1,128]{2,1,0:T(1,128)}), f32[32,1,128]{2,1,0:T(1,128)S(1)}, u32[]{:S(2)}, u32[]{:S(2)}) %all-to-all-start) | async-done | bytes 16416 | tf_op jit(solution)/shard_map/all_to_all | solution.py:560
  65.1 0.8 %shard_map.78 = f32[4,32]{1,0:T(4,128)} custom-call(f32[32,128]{1,0:T(8,128)S(1)} %bitcast.23, s32[8,128]{1,0:T(8,128)S(1)} %get-tuple-element.77.lines), custom_call_target="tpu_custom_call" | custom-call | tf_op jit(solution)/shard_map/pallas_call | solution.py:562
  (5 shorter events, 0.1 us)
Async XLA Ops:
  0.6 10.4 %collective-permute-start = (bf16[32,3072]{1,0:T(8,128)(2,1)}, bf16[32,3072]{1,0:T(8,128)(2,1)S(1)}, u32[]{:S(2)}, u32[]{:S(2)}) collective-permute-start(bf16[32,3072]{1,0:T(8,128)(2,1)} %bitcast.30), channel_id=1, source_target_pairs={{0,224},{1,225},{2,226},{3,227},{4,228},{5,229},{6,230},{7,231},{8... | collective-permute-start | bytes 589832 | tf_op jit(solution)/shard_map/ppermute | solution.py:38
  7.2 0.7 %copy-start.2 = (s32[1,32,4]{1,2,0:T(4,128)S(1)}, s32[1,32,4]{1,2,0:T(4,128)}, u32[]{:S(2)}) copy-start(s32[1,32,4]{1,2,0:T(4,128)} %param.6) | copy-start | bytes 1540
  7.9 0.7 %copy-start.3 = (bf16[1,32,4]{1,2,0:T(4,128)(2,1)S(1)}, bf16[1,32,4]{1,2,0:T(4,128)(2,1)}, u32[]{:S(2)}) copy-start(bf16[1,32,4]{1,2,0:T(4,128)(2,1)} %param.7) | copy-start | bytes 772
  11.0 9.1 %collective-permute-start.1 = (bf16[32,3200]{1,0:T(8,128)(2,1)S(1)}, bf16[32,3200]{1,0:T(8,128)(2,1)S(1)}, u32[]{:S(2)}, u32[]{:S(2)}) collective-permute-start(bf16[32,3200]{1,0:T(8,128)(2,1)S(1)} %pad_maximum_fusion), channel_id=1, source_target_pairs={{0,8},{1,3},{2,10},{3,5},{4,12},{5,7},{6,14},{7,1},{8,16},{9,11},{... | collective-permute-start | bytes 614408 | tf_op jit(solution)/shard_map/ppermute | solution.py:38
  12.4 7.8 %collective-permute-start.2 = (bf16[32,3200]{1,0:T(8,128)(2,1)S(1)}, bf16[32,3200]{1,0:T(8,128)(2,1)S(1)}, u32[]{:S(2)}, u32[]{:S(2)}) collective-permute-start(bf16[32,3200]{1,0:T(8,128)(2,1)S(1)} %pad_maximum_fusion), channel_id=1, source_target_pairs={{0,24},{1,7},{2,26},{3,1},{4,28},{5,3},{6,30},{7,5},{8,0},{9,15},{... | collective-permute-start | bytes 614408 | tf_op jit(solution)/shard_map/ppermute | solution.py:38
  13.9 6.7 %collective-permute-start.3 = (bf16[32,3200]{1,0:T(8,128)(2,1)S(1)}, bf16[32,3200]{1,0:T(8,128)(2,1)S(1)}, u32[]{:S(2)}, u32[]{:S(2)}) collective-permute-start(bf16[32,3200]{1,0:T(8,128)(2,1)S(1)} %pad_maximum_fusion), channel_id=1, source_target_pairs={{0,16},{1,5},{2,18},{3,7},{4,20},{5,1},{6,22},{7,3},{8,24},{9,13},... | collective-permute-start | bytes 614408 | tf_op jit(solution)/shard_map/ppermute | solution.py:38
  20.1 20.3 %copy-start = (bf16[3072,1408]{1,0:T(8,128)(2,1)}, bf16[3072,1408]{1,0:T(8,128)(2,1)S(1)}, u32[]{:S(2)}) copy-start(bf16[3072,1408]{1,0:T(8,128)(2,1)S(1)} %shard_map.69.turned) | copy-start | bytes 25952260
  20.7 8.7 %copy-start.1 = (bf16[1,1,768,1408]{3,2,1,0:T(8,128)(2,1)S(1)}, bf16[1,1,768,1408]{3,2,1,0:T(8,128)(2,1)}, u32[]{:S(2)}) copy-start(bf16[1,1,768,1408]{3,2,1,0:T(8,128)(2,1)} %param.9) | copy-start | bytes 6488068
  20.7 5.3 %collective-permute-start.6 = (bf16[128,3200]{1,0:T(8,128)(2,1)S(1)}, bf16[128,3200]{1,0:T(8,128)(2,1)S(1)}, u32[]{:S(2)}, u32[]{:S(2)}) collective-permute-start(bf16[128,3200]{1,0:T(8,128)(2,1)S(1)} %constant_dynamic-update-slice_fusion.mine), channel_id=1, source_target_pairs={{0,1},{1,0},{2,3},{3,2},{4,5},{5,4},{6,7},{7,6},{8,9},{9,8},{10,11... | collective-permute-start | bytes 2457608 | tf_op jit(solution)/shard_map/ppermute | solution.py:38
  23.3 12.7 %collective-permute-start.4 = (bf16[128,3200]{1,0:T(8,128)(2,1)S(1)}, bf16[128,3200]{1,0:T(8,128)(2,1)S(1)}, u32[]{:S(2)}, u32[]{:S(2)}) collective-permute-start(bf16[128,3200]{1,0:T(8,128)(2,1)S(1)} %constant_dynamic-update-slice_fusion.mine), channel_id=1, source_target_pairs={{0,2},{1,9},{2,4},{3,11},{4,6},{5,13},{6,0},{7,15},{8,10},{9,17},{... | collective-permute-start | bytes 2457608 | tf_op jit(solution)/shard_map/ppermute | solution.py:38
  24.1 11.9 %collective-permute-start.5 = (bf16[128,3200]{1,0:T(8,128)(2,1)S(1)}, bf16[128,3200]{1,0:T(8,128)(2,1)S(1)}, u32[]{:S(2)}, u32[]{:S(2)}) collective-permute-start(bf16[128,3200]{1,0:T(8,128)(2,1)S(1)} %constant_dynamic-update-slice_fusion.mine), channel_id=1, source_target_pairs={{0,6},{1,25},{2,0},{3,27},{4,2},{5,29},{6,4},{7,31},{8,14},{9,1},{... | collective-permute-start | bytes 2457608 | tf_op jit(solution)/shard_map/ppermute | solution.py:38
  36.0 3.3 %collective-permute-start.10 = (bf16[128,3200]{1,0:T(8,128)(2,1)S(1)}, bf16[128,3200]{1,0:T(8,128)(2,1)S(1)}, u32[]{:S(2)}, u32[]{:S(2)}) collective-permute-start(bf16[128,3200]{1,0:T(8,128)(2,1)S(1)} %collective-permute-done.5.high), channel_id=1, source_target_pairs={{0,1},{1,0},{2,3},{3,2},{4,5},{5,4},{6,7},{7,6},{8,9},{9,8},{10,11... | collective-permute-start | bytes 2457608 | tf_op jit(solution)/shard_map/ppermute | solution.py:38
  37.3 3.1 %collective-permute-start.9 = (bf16[128,3200]{1,0:T(8,128)(2,1)S(1)}, bf16[128,3200]{1,0:T(8,128)(2,1)S(1)}, u32[]{:S(2)}, u32[]{:S(2)}) collective-permute-start(bf16[128,3200]{1,0:T(8,128)(2,1)S(1)} %collective-permute-done.4.low), channel_id=1, source_target_pairs={{0,1},{1,0},{2,3},{3,2},{4,5},{5,4},{6,7},{7,6},{8,9},{9,8},{10,11... | collective-permute-start | bytes 2457608 | tf_op jit(solution)/shard_map/ppermute | solution.py:38
  37.4 10.1 %collective-permute-start.7 = (bf16[64,3200]{1,0:T(8,128)(2,1)S(1)}, bf16[64,3200]{1,0:T(8,128)(2,1)S(1)}, u32[]{:S(2)}, u32[]{:S(2)}) collective-permute-start(bf16[64,3200]{1,0:T(8,128)(2,1)S(1)} %get-tuple-element.58), channel_id=1, source_target_pairs={{0,6},{1,25},{2,0},{3,27},{4,2},{5,29},{6,4},{7,31},{8,14},{9,1},{... | collective-permute-start | bytes 1228808 | tf_op jit(solution)/shard_map/ppermute | solution.py:38
  39.1 8.4 %collective-permute-start.8 = (bf16[64,3200]{1,0:T(8,128)(2,1)S(1)}, bf16[64,3200]{1,0:T(8,128)(2,1)S(1)}, u32[]{:S(2)}, u32[]{:S(2)}) collective-permute-start(bf16[64,3200]{1,0:T(8,128)(2,1)S(1)} %get-tuple-element.59), channel_id=1, source_target_pairs={{0,2},{1,9},{2,4},{3,11},{4,6},{5,13},{6,0},{7,15},{8,10},{9,17},{... | collective-permute-start | bytes 1228808 | tf_op jit(solution)/shard_map/ppermute | solution.py:38
  47.6 4.5 %collective-permute-start.11 = (bf16[128,3200]{1,0:T(8,128)(2,1)S(1)}, bf16[128,3200]{1,0:T(8,128)(2,1)S(1)}, u32[]{:S(2)}, u32[]{:S(2)}) collective-permute-start(bf16[128,3200]{1,0:T(8,128)(2,1)S(1)} %shard_map.74.tokens), channel_id=1, source_target_pairs={{0,1},{1,0},{2,3},{3,2},{4,5},{5,4},{6,7},{7,6},{8,9},{9,8},{10,11... | collective-permute-start | bytes 2457608 | tf_op jit(solution)/shard_map/ppermute | solution.py:38
  53.8 11.3 %all-to-all-start = ((f32[32,1,128]{2,1,0:T(1,128)}), f32[32,1,128]{2,1,0:T(1,128)S(1)}, u32[]{:S(2)}, u32[]{:S(2)}) async-start(f32[32,1,128]{2,1,0:T(1,128)} %bitcast.13), calls=%async_computation | async-start | bytes 32768 | tf_op jit(solution)/shard_map/all_to_all | solution.py:560

commit v5 on v4

--- a/solution.py
+++ b/solution.py
@@ -1,5 +1,3 @@
-import functools
-
 import jax
 import jax.numpy as jnp
 from jax import lax
@@ -12,6 +10,7 @@
 CAP = 24
 ROWS = 32
 META = 128
+LANES = 32
 TILE = 256
 OFFSETS = (0, -1, 1, 2)
 HALVES = tuple((0, 2, j) for j in (0, -1, 1)) + tuple((1, i, 2) for i in (0, -1, 1))
@@ -81,15 +80,17 @@
         dot = jnp.zeros((height, META), F32)
         for start in range(0, width, 512):
             value = jnp.dot(chosen, ref[:, start : start + 512], preferred_element_type=F32)
-            packed[at : at + height, start : start + 512] = value.astype(BF16)
+            if packed is not None:
+                packed[at : at + height, start : start + 512] = value.astype(BF16)
             if weights is None:
                 continue
             for col in range(0, 512, META):
                 factor = weights[at : at + height, start + col : start + col + META]
                 dot += value[:, col : col + META] * factor
         dots.append(jnp.sum(dot, axis=1, keepdims=True))
-        own = jnp.dot(chosen, meta, preferred_element_type=F32).astype(BF16)
-        gates[at : at + height, :] = jnp.dot(own, spread, preferred_element_type=F32)
+        if packed is not None:
+            own = jnp.dot(chosen, meta, preferred_element_type=F32).astype(BF16)
+            gates[at : at + height, :] = jnp.dot(own, spread, preferred_element_type=F32)
         at += height
     return dots
 
@@ -143,7 +144,9 @@
     lines[...] = jnp.zeros(lines.shape, jnp.int32)
     for k in range(TOP):
         own = jnp.sum(jnp.where(named[k], before, 0.0), axis=0, keepdims=True)
-        lines[0:1, k * tokens : (k + 1) * tokens] = own.astype(jnp.int32)
+        lines[0:1, k * tokens : (k + 1) * tokens] = (
+            own.astype(jnp.int32) + (ids[k : k + 1, :] & 1) * LANES
+        )
         lines[1:2, k * tokens : (k + 1) * tokens] = ids[k : k + 1, :]
     table = jnp.concatenate(
         [slot, gate, jnp.zeros((META - 2 * EXPERTS, tokens), F32)], axis=0
@@ -245,7 +248,7 @@
     )(place, pltpu.with_memory_space_constraint(weight, pltpu.HBM))
 
 
-def ahead_kernel(place, hidden, weight, out, held, far, sems):
+def ahead_kernel(place, hidden, weight, mine, theirs, held, far, sems):
     units, width = weight.shape
     spans = [pl.ds(at, min(512, units - at)) for at in range(0, units, 512)]
     copies = [
@@ -264,9 +267,11 @@
         left = far[:, at].astype(BF16)
         for col in range(0, width, 512):
             value = jnp.dot(left, held[at, col : col + 512], preferred_element_type=F32)
-            if n:
-                value = out[:, col : col + 512] + value
-            out[:, col : col + 512] = value
+            half = mine.shape[0]
+            for ref, part in ((mine, value[:half]), (theirs, value[half:])):
+                if n:
+                    part = ref[:, col : col + 512] + part
+                ref[:, col : col + 512] = part
 
 
 def ahead_of(place, hidden, weight):
@@ -274,9 +279,9 @@
     height = hidden.shape[0] // 4
     return pl.pallas_call(
         ahead_kernel,
-        out_shape=pltpu.VMEM((height, width), F32),
+        out_shape=(pltpu.VMEM((height // 2, width), F32),) * 2,
         in_specs=[smem(), vmem(), anywhere()],
-        out_specs=vmem(),
+        out_specs=(vmem(), vmem()),
         scratch_shapes=[
             pltpu.VMEM((units, width), BF16),
             pltpu.VMEM((height, units), F32),
@@ -319,10 +324,14 @@
     return pl.ds(pl.multiple_of((which * group + along) * CAP, 8), CAP)
 
 
-def finish(chip, pieces, saved, sums, write):
-    diagonal = lax.broadcasted_iota(jnp.int32, (CAP, META), 0) == lax.broadcasted_iota(
-        jnp.int32, (CAP, META), 1
-    )
+def diagonal_of(core):
+    line = lax.broadcasted_iota(jnp.int32, (CAP, META), 0)
+    lane = lax.broadcasted_iota(jnp.int32, (CAP, META), 1)
+    return lane == line + core * LANES
+
+
+def finish(core, chip, pieces, saved, sums, write):
+    diagonal = diagonal_of(core)
     scales = [None if p is None or p[1] is None else p[1][p[2], :] for p in pieces]
     totals = [jnp.zeros((CAP, META), F32) for _ in pieces]
     for col in range(0, saved.shape[1], META):
@@ -358,6 +367,7 @@
     place, low, high, low_other, high_other, turned, hidden, near, near_gates,
     grad, sums, halves, packed, mid, mid_gates, stage, sems,
 ):
+    sums[...] = jnp.zeros(sums.shape, F32)
     pack(place[3], (low, high, low_other, high_other), packed, mid_gates)
     multiply(packed, turned, mid)
 
@@ -371,7 +381,8 @@
     for i in (0, -1, 1):
         for j in (0, -1, 1):
             chip, slot = chip_of(place, i, j), len(copies)
-            finish(chip, (piece(0, i, j), piece(1, j, i)), hidden, sums, staged(stage, slot))
+            pair = piece(0, i, j), piece(1, j, i)
+            finish(place[2], chip, pair, hidden, sums, staged(stage, slot))
             copy = pltpu.make_async_copy(stage.at[slot], grad.at[pair_rows(chip), :], sems.at[slot])
             copy.start()
             copies.append(copy)
@@ -380,7 +391,7 @@
             halves[n * CAP : (n + 1) * CAP, span] = scaled[kind]
 
         pieces = (piece(0, i, j), None) if kind == 0 else (None, piece(1, j, i))
-        finish(chip_of(place, i, j), pieces, hidden, sums, write)
+        finish(place[2], chip_of(place, i, j), pieces, hidden, sums, write)
     for copy in copies:
         copy.wait()
 
@@ -409,38 +420,38 @@
     )(place, *tokens, turned, hidden, near, near_gates)
 
 
-def sums_kernel(which, place, tokens, ahead, early, sums, packed, gates):
+def sums_kernel(place, tokens, ahead, other_ahead, early, sums, packed, gates):
     sums[...] = early[...]
-    height = packed.shape[0]
-    at = slice(which * height, (which + 1) * height)
-    (total,) = pack(place[3], (tokens,), packed, gates, ahead.at[at, :])
-    diagonal = lax.broadcasted_iota(jnp.int32, (CAP, META), 0) == lax.broadcasted_iota(
-        jnp.int32, (CAP, META), 1
-    )
+    core = place[2]
+    (total,) = pack(place[3], (tokens,), packed, gates, ahead)
+    (other,) = pack(place[3] + 1 - 2 * core, (tokens,), None, None, other_ahead)
+    diagonal, other_diagonal = diagonal_of(core), diagonal_of(1 - core)
     for n in range(4):
-        kind, chip = far_block(place, which * 4 + n)
-        line = jnp.where(diagonal, total[n * CAP : (n + 1) * CAP], 0.0)
+        kind, chip = far_block(place, n)
+        block = slice(n * CAP, (n + 1) * CAP)
+        line = jnp.where(diagonal, total[block], jnp.where(other_diagonal, other[block], 0.0))
         sums[pl.ds(chip * 2 + kind, 1), :] = jnp.sum(line, axis=0, keepdims=True)
 
 
-def sums_of(which, place, tokens, ahead, early):
+def sums_of(place, tokens, ahead, other_ahead, early):
     height, width = ahead.shape
     return pl.pallas_call(
-        functools.partial(sums_kernel, which),
+        sums_kernel,
         out_shape=(
             pltpu.VMEM(early.shape, F32),
-            pltpu.VMEM((height // 2, width), BF16),
-            pltpu.VMEM((height // 2, META), F32),
+            pltpu.VMEM((height, width), BF16),
+            pltpu.VMEM((height, META), F32),
         ),
-        in_specs=[smem()] + [vmem()] * 3,
+        in_specs=[smem()] + [vmem()] * 4,
         out_specs=(vmem(), vmem(), vmem()),
         compiler_params=params(),
         cost_estimate=small(),
-    )(place, tokens, ahead, early)
+    )(place, tokens, ahead, other_ahead, early)
 
 
 def far_kernel(
-    place, mine, theirs, gates, other_gates, turned, halves, _, grad, held, far, far_scales, stage, sems, loads
+    place, mine, gates, tokens, turned, halves, _, grad,
+    held, theirs, other_gates, far, far_scales, stage, sems, loads,
 ):
     units = far.shape[1]
     spans = [pl.ds(at, 512) for at in range(0, held.shape[0], 512)]
@@ -450,6 +461,7 @@
     ]
     for copy in copies:
         copy.start()
+    pack(place[3], (tokens,), theirs, other_gates)
     for n, span in enumerate(spans):
         copies[n].wait()
         at = slice(span.start, span.start + span.size)
@@ -486,29 +498,31 @@
         copy.wait()
 
 
-def far_of(place, mine, theirs, gates, other_gates, turned, halves, grad):
+def far_of(place, mine, gates, tokens, turned, halves, grad):
     width, units = turned.shape
     height = 2 * mine.shape[0]
     return pl.pallas_call(
         far_kernel,
         out_shape=jax.ShapeDtypeStruct(grad.shape, BF16),
-        in_specs=[smem()] + [vmem()] * 4 + [anywhere(), vmem(), anywhere()],
+        in_specs=[smem()] + [vmem()] * 3 + [anywhere(), vmem(), anywhere()],
         out_specs=anywhere(),
         scratch_shapes=[
             pltpu.VMEM((width, units), BF16),
+            pltpu.VMEM((height // 2, width), BF16),
+            pltpu.VMEM((height // 2, META), F32),
             pltpu.VMEM((height, units), F32),
             pltpu.VMEM((height, META), F32),
             pltpu.VMEM((7, 2 * CAP, units), BF16),
             pltpu.SemaphoreType.DMA((7,)),
             pltpu.SemaphoreType.DMA((width // 512,)),
         ],
-        input_output_aliases={7: 0},
+        input_output_aliases={6: 0},
         compiler_params=params(),
         cost_estimate=pl.CostEstimate(
             flops=2 * height * units * turned.shape[0], bytes_accessed=1, transcendentals=0
         ),
     )(
-        place, mine, theirs, gates, other_gates,
+        place, mine, gates, tokens,
         pltpu.with_memory_space_constraint(turned, pltpu.HBM), halves, grad,
     )
 
@@ -520,7 +534,7 @@
         total = total + totals[n * quarter : (n + 1) * quarter, :]
     pick = (lax.broadcasted_iota(jnp.int32, (META, META), 0) == lines[0:1, :]).astype(F32)
     line = jnp.dot(total, pick, precision=lax.Precision.HIGHEST, preferred_element_type=F32)
-    chosen = lax.broadcasted_iota(jnp.int32, line.shape, 0) == lines[1:2, :]
+    chosen = (lax.broadcasted_iota(jnp.int32, line.shape, 0) >> 1) == (lines[1:2, :] >> 1)
     line = jnp.sum(jnp.where(chosen, line, 0.0), axis=0, keepdims=True)
     tokens = out.shape[1]
     for k in range(TOP):
@@ -546,8 +560,11 @@
     near_other = moved(near, other_core)
     near_other, later = lax.optimization_barrier((near_other, place))
     near_done = near_of(place, near, near_other, turned)
-    ahead_far = ahead_of(later, saved, weight)
-    low, high, ahead_far, *near_done = lax.optimization_barrier((low, high, ahead_far, *near_done))
+    ahead_far, ahead_other = ahead_of(later, saved, weight)
+    low, high, ahead_far, ahead_other, *near_done = lax.optimization_barrier(
+        (low, high, ahead_far, ahead_other, *near_done)
+    )
+    ahead_other = moved(ahead_other, other_core)
     left, right = halves_of(high, low)
     far = moved(left, second(3)), moved(right, second(1))
     tokens = low, high, moved(low, other_core), moved(high, other_core)
@@ -555,10 +572,10 @@
     *far, grad, sums, halves = lax.optimization_barrier((*far, grad, sums, halves))
     far = join(*far)
     far_other = moved(far, other_core)
-    sums, mine, far_gates = sums_of(0, place, far, ahead_far, sums)
-    sums, theirs, other_gates = sums_of(1, place, far_other, ahead_far, sums)
+    sums, mine, far_gates = sums_of(place, far, ahead_far, ahead_other, sums)
+    sums, far_other = lax.optimization_barrier((sums, far_other))
     totals = lax.all_to_all(sums, ("dp", "expert"), split_axis=0, concat_axis=0, tiled=True)
-    grad = far_of(place, mine, theirs, far_gates, other_gates, turned, halves, grad)
+    grad = far_of(place, mine, far_gates, far_other, turned, halves, grad)
     gate_grad = pl.pallas_call(
         gather_kernel,
         out_shape=jax.ShapeDtypeStruct(ids.shape, F32),

time: 66.1 us -> 64.6 us (0.977)
  waiting for transfers between devices: 6.69 us -> 4.46 us
  starting transfers between devices: 26.1 us -> 27.6 us
  Pallas kernels: 30.8 us -> 30 us
    ppermute x12 -> x13, waiting for transfers between devices: 5.65 us -> 3.43 us  [moved(): return lax.ppermute(x, AXES, pairs)]
    ppermute x12 -> x13, starting transfers between devices: 21.8 us -> 23.1 us  [moved(): return lax.ppermute(x, AXES, pairs)]
    pallas_call x3 -> x2, Pallas kernels: 7.77 us -> 7 us  [the longest x1 4.99 us: ahead_of(): pl.pallas_call(ahead_kernel, out_shape=(pltpu.VMEM((height // 2, width),...]
  transfers between devices with their start and end apart: 13 -> 14, of which waited for: 7 -> 4; matrix products, arithmetic and copies ran while one was open for 0% -> 0% of each run, Pallas kernels for 43% -> 45%
where the time goes in v5:
time: 64.6 us; the launch traced here: 64.4 us
  Pallas kernels  30 us (46%)
  starting transfers between devices  27.6 us (43%)
  waiting for transfers between devices  4.46 us (7%)
  local copies, waits for them, and re-layouts  1.45 us (2%)
  between operations  0.78 us (1%)
    ppermute x13, starting transfers between devices, moved(): return lax.ppermute(x, AXES, pairs)  23.1 us
    pallas_call x1, Pallas kernels, mid_of(): pl.pallas_call(mid_kernel, out_shape=(jax.ShapeDtypeStruct(hidden.shape,...  7.06 us
    pallas_call x1, Pallas kernels, far_of(): pl.pallas_call(far_kernel, out_shape=jax.ShapeDtypeStruct(grad.shape, BF1...  5.91 us
    pallas_call x1, Pallas kernels, ahead_of(): pl.pallas_call(ahead_kernel, out_shape=(pltpu.VMEM((height // 2, width),...  4.99 us
    pallas_call x1, Pallas kernels, turn(): pl.pallas_call(turn_kernel, out_shape=pltpu.VMEM((width, units), BF16), i...  4.63 us
    all_to_all x1, starting transfers between devices, on_device(): lax.all_to_all(sums, ('dp', 'expert'), split_axis=0, concat_axis=0, tiled...  4.47 us
    ppermute x13, waiting for transfers between devices, moved(): return lax.ppermute(x, AXES, pairs)  3.43 us
    pallas_call x1, Pallas kernels, near_of(): pl.pallas_call(near_kernel, out_shape=(pltpu.VMEM((height, units), F32),...  3.38 us
  transfers between devices with their start and end apart: 14, of which 4 were waited for; matrix products, arithmetic and copies ran while one was open for 0% of the time, Pallas kernels for 45%

profile of v5, /device:TPU:1, one launch (start us, length us, event | category | flops | bytes accessed | tf_op | source)
XLA Modules:
  0.0 64.4 jit_solution(8646418986204364624)
XLA Ops:
  0.6 6.5 %collective-permute-start = (bf16[32,3072]{1,0:T(8,128)(2,1)}, bf16[32,3072]{1,0:T(8,128)(2,1)S(1)}, u32[]{:S(2)}, u32[]{:S(2)}) collective-permute-start(bf16[32,3072]{1,0:T(8,128)(2,1)} %bitcast.30), channel_id=1, source_target_pairs={{0,224},{1,225},{2,226},{3,227},{4,228},{5,229},{6,230},{7,231},{8... | collective-permute-start | bytes 589832 | tf_op jit(solution)/shard_map/ppermute | solution.py:37
  7.1 0.1 pad_add_fusion.place
  7.2 0.0 copy-start.2
  7.2 0.7 %copy-done.2 = s32[1,32,4]{1,2,0:T(4,128)S(1)} copy-done((s32[1,32,4]{1,2,0:T(4,128)S(1)}, s32[1,32,4]{1,2,0:T(4,128)}, u32[]{:S(2)}) %copy-start.2) | copy-done | bytes 536
  7.9 0.0 copy-start.3
  7.9 0.7 %copy-done.3 = bf16[1,32,4]{1,2,0:T(4,128)(2,1)S(1)} copy-done((bf16[1,32,4]{1,2,0:T(4,128)(2,1)S(1)}, bf16[1,32,4]{1,2,0:T(4,128)(2,1)}, u32[]{:S(2)}) %copy-start.3) | copy-done | bytes 280
  8.6 1.1 %shard_map.68 = (bf16[32,128]{1,0:T(8,128)(2,1)S(1)}, s32[8,128]{1,0:T(8,128)S(1)}, s32[4]{0:T(128)S(1)}) custom-call(s32[4]{0:T(128)S(1)} %pad_add_fusion.place, s32[4,32]{1,0:T(4,128)S(1)} %bitcast.24, bf16[4,32]{1,0:T(4,128)(2,1)S(1)} %bitcast.25), custom_call_target="tpu_custom_call" | custom-call | tf_op jit(solution)/shard_map/pallas_call | solution.py:161
  9.7 1.3 %collective-permute-done = bf16[32,3072]{1,0:T(8,128)(2,1)S(1)} collective-permute-done((bf16[32,3072]{1,0:T(8,128)(2,1)}, bf16[32,3072]{1,0:T(8,128)(2,1)S(1)}, u32[]{:S(2)}, u32[]{:S(2)}) %collective-permute-start) | collective-permute-done | bytes 196640 | tf_op jit(solution)/shard_map/ppermute | solution.py:37
  11.0 1.4 %collective-permute-start.1 = (bf16[32,3200]{1,0:T(8,128)(2,1)S(1)}, bf16[32,3200]{1,0:T(8,128)(2,1)S(1)}, u32[]{:S(2)}, u32[]{:S(2)}) collective-permute-start(bf16[32,3200]{1,0:T(8,128)(2,1)S(1)} %pad_maximum_fusion), channel_id=1, source_target_pairs={{0,8},{1,3},{2,10},{3,5},{4,12},{5,7},{6,14},{7,1},{8,16},{9,11},{... | collective-permute-start | bytes 614408 | tf_op jit(solution)/shard_map/ppermute | solution.py:37
  12.4 1.5 %collective-permute-start.2 = (bf16[32,3200]{1,0:T(8,128)(2,1)S(1)}, bf16[32,3200]{1,0:T(8,128)(2,1)S(1)}, u32[]{:S(2)}, u32[]{:S(2)}) collective-permute-start(bf16[32,3200]{1,0:T(8,128)(2,1)S(1)} %pad_maximum_fusion), channel_id=1, source_target_pairs={{0,24},{1,7},{2,26},{3,1},{4,28},{5,3},{6,30},{7,5},{8,0},{9,15},{... | collective-permute-start | bytes 614408 | tf_op jit(solution)/shard_map/ppermute | solution.py:37
  13.9 1.6 %collective-permute-start.3 = (bf16[32,3200]{1,0:T(8,128)(2,1)S(1)}, bf16[32,3200]{1,0:T(8,128)(2,1)S(1)}, u32[]{:S(2)}, u32[]{:S(2)}) collective-permute-start(bf16[32,3200]{1,0:T(8,128)(2,1)S(1)} %pad_maximum_fusion), channel_id=1, source_target_pairs={{0,16},{1,5},{2,18},{3,7},{4,20},{5,1},{6,22},{7,3},{8,24},{9,13},... | collective-permute-start | bytes 614408 | tf_op jit(solution)/shard_map/ppermute | solution.py:37
  15.5 4.6 %shard_map.69.turned = bf16[3072,1408]{1,0:T(8,128)(2,1)S(1)} custom-call(s32[4]{0:T(128)S(1)} %get-tuple-element.53.place, bf16[1408,3072]{1,0:T(8,128)(2,1)} %bitcast.26), custom_call_target="tpu_custom_call" | custom-call | flops 1 | bytes 1 | tf_op jit(solution)/shard_map/pallas_call | solution.py:237
  20.1 0.0 copy-start
  20.1 0.0 collective-permute-done.1
  20.1 0.0 collective-permute-done.2
  20.2 0.5 collective-permute-done.3
  20.7 0.0 copy-start.1
  20.7 2.6 %collective-permute-start.6 = (bf16[128,3200]{1,0:T(8,128)(2,1)S(1)}, bf16[128,3200]{1,0:T(8,128)(2,1)S(1)}, u32[]{:S(2)}, u32[]{:S(2)}) collective-permute-start(bf16[128,3200]{1,0:T(8,128)(2,1)S(1)} %constant_dynamic-update-slice_fusion.mine), channel_id=1, source_target_pairs={{0,1},{1,0},{2,3},{3,2},{4,5},{5,4},{6,7},{7,6},{8,9},{9,8},{10,11... | collective-permute-start | bytes 2457608 | tf_op jit(solution)/shard_map/ppermute | solution.py:37
  23.3 0.8 %collective-permute-start.4 = (bf16[128,3200]{1,0:T(8,128)(2,1)S(1)}, bf16[128,3200]{1,0:T(8,128)(2,1)S(1)}, u32[]{:S(2)}, u32[]{:S(2)}) collective-permute-start(bf16[128,3200]{1,0:T(8,128)(2,1)S(1)} %constant_dynamic-update-slice_fusion.mine), channel_id=1, source_target_pairs={{0,2},{1,9},{2,4},{3,11},{4,6},{5,13},{6,0},{7,15},{8,10},{9,17},{... | collective-permute-start | bytes 2457608 | tf_op jit(solution)/shard_map/ppermute | solution.py:37
  24.1 1.9 %collective-permute-start.5 = (bf16[128,3200]{1,0:T(8,128)(2,1)S(1)}, bf16[128,3200]{1,0:T(8,128)(2,1)S(1)}, u32[]{:S(2)}, u32[]{:S(2)}) collective-permute-start(bf16[128,3200]{1,0:T(8,128)(2,1)S(1)} %constant_dynamic-update-slice_fusion.mine), channel_id=1, source_target_pairs={{0,6},{1,25},{2,0},{3,27},{4,2},{5,29},{6,4},{7,31},{8,14},{9,1},{... | collective-permute-start | bytes 2457608 | tf_op jit(solution)/shard_map/ppermute | solution.py:37
  26.0 0.0 collective-permute-done.6.theirs
  26.0 3.4 %shard_map.71 = (f32[192,1408]{1,0:T(8,128)S(1)}, f32[192,128]{1,0:T(8,128)S(1)}) custom-call(s32[4]{0:T(128)S(1)} %get-tuple-element.53.place, bf16[128,3200]{1,0:T(8,128)(2,1)S(1)} %constant_dynamic-update-slice_fusion.mine, bf16[128,3200]{1,0:T(8,128)(2,1)S(1)} %collective-permute-done.6.theirs, bf16[3072,1408]{1,0:T(8,128)(2,1)S(1)} %shard_map.69.turned), custom_call_target="tpu_custom_call" | custom-call | flops 1 | bytes 1 | tf_op jit(solution)/shard_map/pallas_call | solution.py:303
  29.4 0.0 copy-done.1
  29.4 5.0 %shard_map.70 = (f32[96,3072]{1,0:T(8,128)S(1)}, f32[96,3072]{1,0:T(8,128)S(1)}) custom-call(s32[4]{0:T(128)S(1)} %get-tuple-element.53.place, bf16[768,1408]{1,0:T(8,128)(2,1)S(1)} %bitcast.21, bf16[1408,3072]{1,0:T(8,128)(2,1)} %bitcast.27), custom_call_target="tpu_custom_call" | custom-call | flops 1 | bytes 1 | tf_op jit(solution)/shard_map/pallas_call | solution.py:280
  34.4 1.6 %collective-permute-done.4.low = bf16[128,3200]{1,0:T(8,128)(2,1)S(1)} collective-permute-done((bf16[128,3200]{1,0:T(8,128)(2,1)S(1)}, bf16[128,3200]{1,0:T(8,128)(2,1)S(1)}, u32[]{:S(2)}, u32[]{:S(2)}) %collective-permute-start.4) | collective-permute-done | bytes 819232 | tf_op jit(solution)/shard_map/ppermute | solution.py:37
  36.0 0.0 collective-permute-done.5.high
  36.0 1.3 %collective-permute-start.10 = (bf16[128,3200]{1,0:T(8,128)(2,1)S(1)}, bf16[128,3200]{1,0:T(8,128)(2,1)S(1)}, u32[]{:S(2)}, u32[]{:S(2)}) collective-permute-start(bf16[128,3200]{1,0:T(8,128)(2,1)S(1)} %collective-permute-done.5.high), channel_id=1, source_target_pairs={{0,1},{1,0},{2,3},{3,2},{4,5},{5,4},{6,7},{7,6},{8,9},{9,8},{10,11... | collective-permute-start | bytes 2457608 | tf_op jit(solution)/shard_map/ppermute | solution.py:37
  37.3 0.0 collective-permute-start.9
  37.3 0.1 shard_map.72
  37.4 1.7 %collective-permute-start.7 = (bf16[64,3200]{1,0:T(8,128)(2,1)S(1)}, bf16[64,3200]{1,0:T(8,128)(2,1)S(1)}, u32[]{:S(2)}, u32[]{:S(2)}) collective-permute-start(bf16[64,3200]{1,0:T(8,128)(2,1)S(1)} %get-tuple-element.62), channel_id=1, source_target_pairs={{0,6},{1,25},{2,0},{3,27},{4,2},{5,29},{6,4},{7,31},{8,14},{9,1},{... | collective-permute-start | bytes 1228808 | tf_op jit(solution)/shard_map/ppermute | solution.py:37
  39.1 0.0 collective-permute-start.8
  39.1 1.8 %collective-permute-start.11 = (f32[96,3072]{1,0:T(8,128)S(1)}, f32[96,3072]{1,0:T(8,128)S(1)}, u32[]{:S(2)}, u32[]{:S(2)}) collective-permute-start(f32[96,3072]{1,0:T(8,128)S(1)} %get-tuple-element.72), channel_id=1, source_target_pairs={{0,1},{1,0},{2,3},{3,2},{4,5},{5,4},{6,7},{7,6},{8,9},{9,8},{10,11... | collective-permute-start | bytes 3538952 | tf_op jit(solution)/shard_map/ppermute | solution.py:37
  40.8 0.0 collective-permute-done.10.high_other
  40.8 0.0 collective-permute-done.9.low_other
  40.9 0.0 copy-done
  40.9 7.1 %shard_map.73 = (bf16[768,1408]{1,0:T(8,128)(2,1)}, f32[32,128]{1,0:T(8,128)S(1)}, f32[144,1408]{1,0:T(8,128)S(1)}) custom-call(s32[4]{0:T(128)S(1)} %get-tuple-element.53.place, bf16[128,3200]{1,0:T(8,128)(2,1)S(1)} %collective-permute-done.4.low, bf16[128,3200]{1,0:T(8,128)(2,1)S(1)} %collective-permute-done.5.high, ...), custom_call_target="tpu_custom_call" | custom-call | flops 1 | bytes 1 | tf_op jit(solution)/shard_map/pallas_call | solution.py:402
  47.9 0.0 collective-permute-done.7.refs_0_
  47.9 0.0 collective-permute-done.8.refs_1_
  47.9 0.1 shard_map.74.tokens
  48.0 2.1 %collective-permute-start.12 = (bf16[128,3200]{1,0:T(8,128)(2,1)S(1)}, bf16[128,3200]{1,0:T(8,128)(2,1)S(1)}, u32[]{:S(2)}, u32[]{:S(2)}) collective-permute-start(bf16[128,3200]{1,0:T(8,128)(2,1)S(1)} %shard_map.74.tokens), channel_id=1, source_target_pairs={{0,1},{1,0},{2,3},{3,2},{4,5},{5,4},{6,7},{7,6},{8,9},{9,8},{10,11... | collective-permute-start | bytes 2457608 | tf_op jit(solution)/shard_map/ppermute | solution.py:37
  50.1 0.0 collective-permute-done.11.other_ahead
  50.2 2.0 %shard_map.75 = (f32[32,128]{1,0:T(8,128)}, bf16[96,3072]{1,0:T(8,128)(2,1)S(1)}, f32[96,128]{1,0:T(8,128)S(1)}) custom-call(s32[4]{0:T(128)S(1)} %get-tuple-element.53.place, bf16[128,3200]{1,0:T(8,128)(2,1)S(1)} %shard_map.74.tokens, f32[96,3072]{1,0:T(8,128)S(1)} %get-tuple-element.71.ahead, f32[96,3072]{1,0:T(8,128)S(1)} %collective-permute-done.11.other_ahead, ...), custom_call_target="tpu_custom_call" | custom-call | flops 1 | bytes 1 | tf_op jit(solution)/shard_map/pallas_call | solution.py:438
  52.2 0.0 collective-permute-done.12.tokens
  52.2 4.5 %all-to-all-start = ((f32[32,1,128]{2,1,0:T(1,128)}), f32[32,1,128]{2,1,0:T(1,128)S(1)}, u32[]{:S(2)}, u32[]{:S(2)}) async-start(f32[32,1,128]{2,1,0:T(1,128)} %bitcast.13), calls=%async_computation | async-start | bytes 32768 | tf_op jit(solution)/shard_map/all_to_all | solution.py:577
  56.6 5.9 %shard_map.76 = bf16[768,1408]{1,0:T(8,128)(2,1)} custom-call(s32[4]{0:T(128)S(1)} %get-tuple-element.53.place, bf16[96,3072]{1,0:T(8,128)(2,1)S(1)} %get-tuple-element.74.mine, f32[96,128]{1,0:T(8,128)S(1)} %get-tuple-element.75.gates, bf16[128,3200]{1,0:T(8,128)(2,1)S(1)} %collective-permute-done.12.tokens, ...), custom_call_target="tpu_custom_call", output_to_operand_aliasing={{}: (6, {})} | custom-call | flops 1660944384 | bytes 1 | tf_op jit(solution)/shard_map/pallas_call | solution.py:504
  62.6 1.0 %all-to-all-done = f32[32,1,128]{2,1,0:T(1,128)S(1)} async-done(((f32[32,1,128]{2,1,0:T(1,128)}), f32[32,1,128]{2,1,0:T(1,128)S(1)}, u32[]{:S(2)}, u32[]{:S(2)}) %all-to-all-start) | async-done | bytes 16416 | tf_op jit(solution)/shard_map/all_to_all | solution.py:577
  63.6 0.8 %shard_map.77 = f32[4,32]{1,0:T(4,128)} custom-call(f32[32,128]{1,0:T(8,128)S(1)} %bitcast.23, s32[8,128]{1,0:T(8,128)S(1)} %get-tuple-element.81.lines), custom_call_target="tpu_custom_call" | custom-call | tf_op jit(solution)/shard_map/pallas_call | solution.py:579
  (5 shorter events, 0.1 us)
Async XLA Ops:
  0.6 10.4 %collective-permute-start = (bf16[32,3072]{1,0:T(8,128)(2,1)}, bf16[32,3072]{1,0:T(8,128)(2,1)S(1)}, u32[]{:S(2)}, u32[]{:S(2)}) collective-permute-start(bf16[32,3072]{1,0:T(8,128)(2,1)} %bitcast.30), channel_id=1, source_target_pairs={{0,224},{1,225},{2,226},{3,227},{4,228},{5,229},{6,230},{7,231},{8... | collective-permute-start | bytes 589832 | tf_op jit(solution)/shard_map/ppermute | solution.py:37
  7.2 0.7 %copy-start.2 = (s32[1,32,4]{1,2,0:T(4,128)S(1)}, s32[1,32,4]{1,2,0:T(4,128)}, u32[]{:S(2)}) copy-start(s32[1,32,4]{1,2,0:T(4,128)} %param.6) | copy-start | bytes 1540
  7.9 0.7 %copy-start.3 = (bf16[1,32,4]{1,2,0:T(4,128)(2,1)S(1)}, bf16[1,32,4]{1,2,0:T(4,128)(2,1)}, u32[]{:S(2)}) copy-start(bf16[1,32,4]{1,2,0:T(4,128)(2,1)} %param.7) | copy-start | bytes 772
  11.0 9.1 %collective-permute-start.1 = (bf16[32,3200]{1,0:T(8,128)(2,1)S(1)}, bf16[32,3200]{1,0:T(8,128)(2,1)S(1)}, u32[]{:S(2)}, u32[]{:S(2)}) collective-permute-start(bf16[32,3200]{1,0:T(8,128)(2,1)S(1)} %pad_maximum_fusion), channel_id=1, source_target_pairs={{0,8},{1,3},{2,10},{3,5},{4,12},{5,7},{6,14},{7,1},{8,16},{9,11},{... | collective-permute-start | bytes 614408 | tf_op jit(solution)/shard_map/ppermute | solution.py:37
  12.4 7.8 %collective-permute-start.2 = (bf16[32,3200]{1,0:T(8,128)(2,1)S(1)}, bf16[32,3200]{1,0:T(8,128)(2,1)S(1)}, u32[]{:S(2)}, u32[]{:S(2)}) collective-permute-start(bf16[32,3200]{1,0:T(8,128)(2,1)S(1)} %pad_maximum_fusion), channel_id=1, source_target_pairs={{0,24},{1,7},{2,26},{3,1},{4,28},{5,3},{6,30},{7,5},{8,0},{9,15},{... | collective-permute-start | bytes 614408 | tf_op jit(solution)/shard_map/ppermute | solution.py:37
  13.9 6.7 %collective-permute-start.3 = (bf16[32,3200]{1,0:T(8,128)(2,1)S(1)}, bf16[32,3200]{1,0:T(8,128)(2,1)S(1)}, u32[]{:S(2)}, u32[]{:S(2)}) collective-permute-start(bf16[32,3200]{1,0:T(8,128)(2,1)S(1)} %pad_maximum_fusion), channel_id=1, source_target_pairs={{0,16},{1,5},{2,18},{3,7},{4,20},{5,1},{6,22},{7,3},{8,24},{9,13},... | collective-permute-start | bytes 614408 | tf_op jit(solution)/shard_map/ppermute | solution.py:37
  20.1 20.7 %copy-start = (bf16[3072,1408]{1,0:T(8,128)(2,1)}, bf16[3072,1408]{1,0:T(8,128)(2,1)S(1)}, u32[]{:S(2)}) copy-start(bf16[3072,1408]{1,0:T(8,128)(2,1)S(1)} %shard_map.69.turned) | copy-start | bytes 25952260
  20.7 8.7 %copy-start.1 = (bf16[1,1,768,1408]{3,2,1,0:T(8,128)(2,1)S(1)}, bf16[1,1,768,1408]{3,2,1,0:T(8,128)(2,1)}, u32[]{:S(2)}) copy-start(bf16[1,1,768,1408]{3,2,1,0:T(8,128)(2,1)} %param.9) | copy-start | bytes 6488068
  20.7 5.3 %collective-permute-start.6 = (bf16[128,3200]{1,0:T(8,128)(2,1)S(1)}, bf16[128,3200]{1,0:T(8,128)(2,1)S(1)}, u32[]{:S(2)}, u32[]{:S(2)}) collective-permute-start(bf16[128,3200]{1,0:T(8,128)(2,1)S(1)} %constant_dynamic-update-slice_fusion.mine), channel_id=1, source_target_pairs={{0,1},{1,0},{2,3},{3,2},{4,5},{5,4},{6,7},{7,6},{8,9},{9,8},{10,11... | collective-permute-start | bytes 2457608 | tf_op jit(solution)/shard_map/ppermute | solution.py:37
  23.3 12.7 %collective-permute-start.4 = (bf16[128,3200]{1,0:T(8,128)(2,1)S(1)}, bf16[128,3200]{1,0:T(8,128)(2,1)S(1)}, u32[]{:S(2)}, u32[]{:S(2)}) collective-permute-start(bf16[128,3200]{1,0:T(8,128)(2,1)S(1)} %constant_dynamic-update-slice_fusion.mine), channel_id=1, source_target_pairs={{0,2},{1,9},{2,4},{3,11},{4,6},{5,13},{6,0},{7,15},{8,10},{9,17},{... | collective-permute-start | bytes 2457608 | tf_op jit(solution)/shard_map/ppermute | solution.py:37
  24.1 11.9 %collective-permute-start.5 = (bf16[128,3200]{1,0:T(8,128)(2,1)S(1)}, bf16[128,3200]{1,0:T(8,128)(2,1)S(1)}, u32[]{:S(2)}, u32[]{:S(2)}) collective-permute-start(bf16[128,3200]{1,0:T(8,128)(2,1)S(1)} %constant_dynamic-update-slice_fusion.mine), channel_id=1, source_target_pairs={{0,6},{1,25},{2,0},{3,27},{4,2},{5,29},{6,4},{7,31},{8,14},{9,1},{... | collective-permute-start | bytes 2457608 | tf_op jit(solution)/shard_map/ppermute | solution.py:37
  36.0 4.8 %collective-permute-start.10 = (bf16[128,3200]{1,0:T(8,128)(2,1)S(1)}, bf16[128,3200]{1,0:T(8,128)(2,1)S(1)}, u32[]{:S(2)}, u32[]{:S(2)}) collective-permute-start(bf16[128,3200]{1,0:T(8,128)(2,1)S(1)} %collective-permute-done.5.high), channel_id=1, source_target_pairs={{0,1},{1,0},{2,3},{3,2},{4,5},{5,4},{6,7},{7,6},{8,9},{9,8},{10,11... | collective-permute-start | bytes 2457608 | tf_op jit(solution)/shard_map/ppermute | solution.py:37
  37.3 3.5 %collective-permute-start.9 = (bf16[128,3200]{1,0:T(8,128)(2,1)S(1)}, bf16[128,3200]{1,0:T(8,128)(2,1)S(1)}, u32[]{:S(2)}, u32[]{:S(2)}) collective-permute-start(bf16[128,3200]{1,0:T(8,128)(2,1)S(1)} %collective-permute-done.4.low), channel_id=1, source_target_pairs={{0,1},{1,0},{2,3},{3,2},{4,5},{5,4},{6,7},{7,6},{8,9},{9,8},{10,11... | collective-permute-start | bytes 2457608 | tf_op jit(solution)/shard_map/ppermute | solution.py:37
  37.4 10.5 %collective-permute-start.7 = (bf16[64,3200]{1,0:T(8,128)(2,1)S(1)}, bf16[64,3200]{1,0:T(8,128)(2,1)S(1)}, u32[]{:S(2)}, u32[]{:S(2)}) collective-permute-start(bf16[64,3200]{1,0:T(8,128)(2,1)S(1)} %get-tuple-element.62), channel_id=1, source_target_pairs={{0,6},{1,25},{2,0},{3,27},{4,2},{5,29},{6,4},{7,31},{8,14},{9,1},{... | collective-permute-start | bytes 1228808 | tf_op jit(solution)/shard_map/ppermute | solution.py:37
  39.1 8.8 %collective-permute-start.8 = (bf16[64,3200]{1,0:T(8,128)(2,1)S(1)}, bf16[64,3200]{1,0:T(8,128)(2,1)S(1)}, u32[]{:S(2)}, u32[]{:S(2)}) collective-permute-start(bf16[64,3200]{1,0:T(8,128)(2,1)S(1)} %get-tuple-element.63), channel_id=1, source_target_pairs={{0,2},{1,9},{2,4},{3,11},{4,6},{5,13},{6,0},{7,15},{8,10},{9,17},{... | collective-permute-start | bytes 1228808 | tf_op jit(solution)/shard_map/ppermute | solution.py:37
  39.1 11.1 %collective-permute-start.11 = (f32[96,3072]{1,0:T(8,128)S(1)}, f32[96,3072]{1,0:T(8,128)S(1)}, u32[]{:S(2)}, u32[]{:S(2)}) collective-permute-start(f32[96,3072]{1,0:T(8,128)S(1)} %get-tuple-element.72), channel_id=1, source_target_pairs={{0,1},{1,0},{2,3},{3,2},{4,5},{5,4},{6,7},{7,6},{8,9},{9,8},{10,11... | collective-permute-start | bytes 3538952 | tf_op jit(solution)/shard_map/ppermute | solution.py:37
  48.0 4.2 %collective-permute-start.12 = (bf16[128,3200]{1,0:T(8,128)(2,1)S(1)}, bf16[128,3200]{1,0:T(8,128)(2,1)S(1)}, u32[]{:S(2)}, u32[]{:S(2)}) collective-permute-start(bf16[128,3200]{1,0:T(8,128)(2,1)S(1)} %shard_map.74.tokens), channel_id=1, source_target_pairs={{0,1},{1,0},{2,3},{3,2},{4,5},{5,4},{6,7},{7,6},{8,9},{9,8},{10,11... | collective-permute-start | bytes 2457608 | tf_op jit(solution)/shard_map/ppermute | solution.py:37
  52.2 11.4 %all-to-all-start = ((f32[32,1,128]{2,1,0:T(1,128)}), f32[32,1,128]{2,1,0:T(1,128)S(1)}, u32[]{:S(2)}, u32[]{:S(2)}) async-start(f32[32,1,128]{2,1,0:T(1,128)} %bitcast.13), calls=%async_computation | async-start | bytes 32768 | tf_op jit(solution)/shard_map/all_to_all | solution.py:577

commit v6 on v5

--- a/solution.py
+++ b/solution.py
@@ -57,42 +57,36 @@
     return jnp.concatenate(parts, axis=0)
 
 
-def pack(expert, token_refs, packed, gates, weights=None):
-    dots = []
+def chosen_rows(expert, ref):
+    count, width = ref.shape
     lane = lax.broadcasted_iota(jnp.int32, (16, META), 1)
     line = lax.broadcasted_iota(jnp.int32, (16, META), 0)
     pick = ((line == 0) & (lane == expert)).astype(F32).astype(BF16)
+    slot = lax.dot_general(
+        pick, ref[:, width - META :], (((1,), (1,)), ((), ())), preferred_element_type=F32
+    )[0:1, :]
+    block = lax.broadcasted_iota(jnp.int32, (1, count), 1) // ROWS
+    target = jnp.where(slot >= 0.0, slot.astype(jnp.int32) + block * CAP, -1)
+    place = lax.broadcasted_iota(jnp.int32, (count // ROWS * CAP, count), 0)
+    return (place == target).astype(F32).astype(BF16)
+
+
+def pack(expert, token_refs, packed, gates):
     spread = (
         lax.broadcasted_iota(jnp.int32, (META, META), 0) == EXPERTS + expert
     ).astype(F32).astype(BF16)
     at = 0
     for ref in token_refs:
-        count, width = ref.shape
-        width = width - META
-        height = count // ROWS * CAP
-        meta = ref[:, width:]
-        slot = lax.dot_general(pick, meta, (((1,), (1,)), ((), ())), preferred_element_type=F32)[0:1, :]
-        block = lax.broadcasted_iota(jnp.int32, (1, count), 1) // ROWS
-        target = jnp.where(slot >= 0.0, slot.astype(jnp.int32) + block * CAP, -1)
-        chosen = (
-            lax.broadcasted_iota(jnp.int32, (height, count), 0) == target
-        ).astype(F32).astype(BF16)
-        dot = jnp.zeros((height, META), F32)
+        width = ref.shape[1] - META
+        chosen = chosen_rows(expert, ref)
+        height = chosen.shape[0]
         for start in range(0, width, 512):
-            value = jnp.dot(chosen, ref[:, start : start + 512], preferred_element_type=F32)
-            if packed is not None:
-                packed[at : at + height, start : start + 512] = value.astype(BF16)
-            if weights is None:
-                continue
-            for col in range(0, 512, META):
-                factor = weights[at : at + height, start + col : start + col + META]
-                dot += value[:, col : col + META] * factor
-        dots.append(jnp.sum(dot, axis=1, keepdims=True))
-        if packed is not None:
-            own = jnp.dot(chosen, meta, preferred_element_type=F32).astype(BF16)
-            gates[at : at + height, :] = jnp.dot(own, spread, preferred_element_type=F32)
+            packed[at : at + height, start : start + 512] = jnp.dot(
+                chosen, ref[:, start : start + 512], preferred_element_type=F32
+            ).astype(BF16)
+        own = jnp.dot(chosen, ref[:, width:], preferred_element_type=F32).astype(BF16)
+        gates[at : at + height, :] = jnp.dot(own, spread, preferred_element_type=F32)
         at += height
-    return dots
 
 
 def multiply(packed, turned, out):
@@ -420,38 +414,43 @@
     )(place, *tokens, turned, hidden, near, near_gates)
 
 
-def sums_kernel(place, tokens, ahead, other_ahead, early, sums, packed, gates):
+def sums_kernel(place, tokens, ahead, other_ahead, early, sums):
     sums[...] = early[...]
     core = place[2]
-    (total,) = pack(place[3], (tokens,), packed, gates, ahead)
-    (other,) = pack(place[3] + 1 - 2 * core, (tokens,), None, None, other_ahead)
+    height, width = ahead.shape
+    chosen = jnp.concatenate(
+        [chosen_rows(e, tokens) for e in (place[3], place[3] + 1 - 2 * core)], axis=0
+    )
+    total = jnp.zeros((2 * height, META), F32)
+    for start in range(0, width, 512):
+        value = jnp.dot(chosen, tokens[:, start : start + 512], preferred_element_type=F32)
+        for col in range(0, 512, META):
+            span = slice(start + col, start + col + META)
+            factor = jnp.concatenate([ahead[:, span], other_ahead[:, span]], axis=0)
+            total += value[:, col : col + META] * factor
+    total = jnp.sum(total, axis=1, keepdims=True)
     diagonal, other_diagonal = diagonal_of(core), diagonal_of(1 - core)
     for n in range(4):
         kind, chip = far_block(place, n)
-        block = slice(n * CAP, (n + 1) * CAP)
-        line = jnp.where(diagonal, total[block], jnp.where(other_diagonal, other[block], 0.0))
+        own = total[n * CAP : (n + 1) * CAP]
+        other = total[height + n * CAP : height + (n + 1) * CAP]
+        line = jnp.where(diagonal, own, jnp.where(other_diagonal, other, 0.0))
         sums[pl.ds(chip * 2 + kind, 1), :] = jnp.sum(line, axis=0, keepdims=True)
 
 
 def sums_of(place, tokens, ahead, other_ahead, early):
-    height, width = ahead.shape
     return pl.pallas_call(
         sums_kernel,
-        out_shape=(
-            pltpu.VMEM(early.shape, F32),
-            pltpu.VMEM((height, width), BF16),
-            pltpu.VMEM((height, META), F32),
-        ),
+        out_shape=jax.ShapeDtypeStruct(early.shape, F32),
         in_specs=[smem()] + [vmem()] * 4,
-        out_specs=(vmem(), vmem(), vmem()),
+        out_specs=vmem(),
         compiler_params=params(),
         cost_estimate=small(),
     )(place, tokens, ahead, other_ahead, early)
 
 
 def far_kernel(
-    place, mine, gates, tokens, turned, halves, _, grad,
-    held, theirs, other_gates, far, far_scales, stage, sems, loads,
+    place, mine, theirs, turned, halves, _, grad, held, packed, far, far_scales, stage, sems, loads
 ):
     units = far.shape[1]
     spans = [pl.ds(at, 512) for at in range(0, held.shape[0], 512)]
@@ -461,16 +460,13 @@
     ]
     for copy in copies:
         copy.start()
-    pack(place[3], (tokens,), theirs, other_gates)
+    pack(place[3], (mine, theirs), packed, far_scales)
     for n, span in enumerate(spans):
         copies[n].wait()
         at = slice(span.start, span.start + span.size)
-        rows_of = jnp.concatenate([mine[:, at], theirs[:, at]], axis=0)
-        value = jnp.dot(rows_of, held[at, :], preferred_element_type=F32)
+        value = jnp.dot(packed[:, at], held[at, :], preferred_element_type=F32)
         far[...] = value if n == 0 else far[...] + value
     copies = []
-    scales = jnp.concatenate([gates[...], other_gates[...]], axis=0)
-    far_scales[...] = scales
     for i in OFFSETS:
         for j in OFFSETS:
             if i != 2 and j != 2:
@@ -498,31 +494,30 @@
         copy.wait()
 
 
-def far_of(place, mine, gates, tokens, turned, halves, grad):
+def far_of(place, mine, theirs, turned, halves, grad):
     width, units = turned.shape
-    height = 2 * mine.shape[0]
+    height = 2 * mine.shape[0] // ROWS * CAP
     return pl.pallas_call(
         far_kernel,
         out_shape=jax.ShapeDtypeStruct(grad.shape, BF16),
-        in_specs=[smem()] + [vmem()] * 3 + [anywhere(), vmem(), anywhere()],
+        in_specs=[smem()] + [vmem()] * 2 + [anywhere(), vmem(), anywhere()],
         out_specs=anywhere(),
         scratch_shapes=[
             pltpu.VMEM((width, units), BF16),
-            pltpu.VMEM((height // 2, width), BF16),
-            pltpu.VMEM((height // 2, META), F32),
+            pltpu.VMEM((height, width), BF16),
             pltpu.VMEM((height, units), F32),
             pltpu.VMEM((height, META), F32),
             pltpu.VMEM((7, 2 * CAP, units), BF16),
             pltpu.SemaphoreType.DMA((7,)),
             pltpu.SemaphoreType.DMA((width // 512,)),
         ],
-        input_output_aliases={6: 0},
+        input_output_aliases={5: 0},
         compiler_params=params(),
         cost_estimate=pl.CostEstimate(
             flops=2 * height * units * turned.shape[0], bytes_accessed=1, transcendentals=0
         ),
     )(
-        place, mine, gates, tokens,
+        place, mine, theirs,
         pltpu.with_memory_space_constraint(turned, pltpu.HBM), halves, grad,
     )
 
@@ -572,10 +567,10 @@
     *far, grad, sums, halves = lax.optimization_barrier((*far, grad, sums, halves))
     far = join(*far)
     far_other = moved(far, other_core)
-    sums, mine, far_gates = sums_of(place, far, ahead_far, ahead_other, sums)
-    sums, far_other = lax.optimization_barrier((sums, far_other))
+    sums = sums_of(place, far, ahead_far, ahead_other, sums)
     totals = lax.all_to_all(sums, ("dp", "expert"), split_axis=0, concat_axis=0, tiled=True)
-    grad = far_of(place, mine, far_gates, far_other, turned, halves, grad)
+    grad = far_of(place, far, far_other, turned, halves, grad)
+    totals, grad = lax.optimization_barrier((totals, grad))
     gate_grad = pl.pallas_call(
         gather_kernel,
         out_shape=jax.ShapeDtypeStruct(ids.shape, F32),

time: 64.6 us -> 64.4 us (level)
  no operation moved by 1% of the time
where the time goes in v6:
time: 64.4 us; the launch traced here: 64.2 us
  Pallas kernels  29.9 us (46%)
  starting transfers between devices  27.6 us (43%)
  waiting for transfers between devices  4.43 us (7%)
  local copies, waits for them, and re-layouts  1.45 us (2%)
  between operations  0.79 us (1%)
    ppermute x13, starting transfers between devices, moved(): return lax.ppermute(x, AXES, pairs)  23.1 us
    pallas_call x1, Pallas kernels, mid_of(): pl.pallas_call(mid_kernel, out_shape=(jax.ShapeDtypeStruct(hidden.shape,...  7.06 us
    pallas_call x1, Pallas kernels, far_of(): pl.pallas_call(far_kernel, out_shape=jax.ShapeDtypeStruct(grad.shape, BF1...  5.94 us
    pallas_call x1, Pallas kernels, ahead_of(): pl.pallas_call(ahead_kernel, out_shape=(pltpu.VMEM((height // 2, width),...  4.98 us
    pallas_call x1, Pallas kernels, turn(): pl.pallas_call(turn_kernel, out_shape=pltpu.VMEM((width, units), BF16), i...  4.63 us
    all_to_all x1, starting transfers between devices, on_device(): lax.all_to_all(sums, ('dp', 'expert'), split_axis=0, concat_axis=0, tiled...  4.48 us
    ppermute x13, waiting for transfers between devices, moved(): return lax.ppermute(x, AXES, pairs)  3.45 us
    pallas_call x1, Pallas kernels, near_of(): pl.pallas_call(near_kernel, out_shape=(pltpu.VMEM((height, units), F32),...  3.37 us
  transfers between devices with their start and end apart: 14, of which 4 were waited for; matrix products, arithmetic and copies ran while one was open for 0% of the time, Pallas kernels for 45%

profile of v6, /device:TPU:1, one launch (start us, length us, event | category | flops | bytes accessed | tf_op | source)
XLA Modules:
  0.0 64.2 jit_solution(5489404678963410611)
XLA Ops:
  0.6 6.5 %collective-permute-start = (bf16[32,3072]{1,0:T(8,128)(2,1)}, bf16[32,3072]{1,0:T(8,128)(2,1)S(1)}, u32[]{:S(2)}, u32[]{:S(2)}) collective-permute-start(bf16[32,3072]{1,0:T(8,128)(2,1)} %bitcast.30), channel_id=1, source_target_pairs={{0,224},{1,225},{2,226},{3,227},{4,228},{5,229},{6,230},{7,231},{8... | collective-permute-start | bytes 589832 | tf_op jit(solution)/shard_map/ppermute | solution.py:37
  7.1 0.1 pad_add_fusion.place
  7.2 0.0 copy-start.2
  7.2 0.7 %copy-done.2 = s32[1,32,4]{1,2,0:T(4,128)S(1)} copy-done((s32[1,32,4]{1,2,0:T(4,128)S(1)}, s32[1,32,4]{1,2,0:T(4,128)}, u32[]{:S(2)}) %copy-start.2) | copy-done | bytes 536
  7.9 0.0 copy-start.3
  7.9 0.7 %copy-done.3 = bf16[1,32,4]{1,2,0:T(4,128)(2,1)S(1)} copy-done((bf16[1,32,4]{1,2,0:T(4,128)(2,1)S(1)}, bf16[1,32,4]{1,2,0:T(4,128)(2,1)}, u32[]{:S(2)}) %copy-start.3) | copy-done | bytes 280
  8.6 1.1 %shard_map.68 = (bf16[32,128]{1,0:T(8,128)(2,1)S(1)}, s32[8,128]{1,0:T(8,128)S(1)}, s32[4]{0:T(128)S(1)}) custom-call(s32[4]{0:T(128)S(1)} %pad_add_fusion.place, s32[4,32]{1,0:T(4,128)S(1)} %bitcast.24, bf16[4,32]{1,0:T(4,128)(2,1)S(1)} %bitcast.25), custom_call_target="tpu_custom_call" | custom-call | tf_op jit(solution)/shard_map/pallas_call | solution.py:155
  9.7 1.3 %collective-permute-done = bf16[32,3072]{1,0:T(8,128)(2,1)S(1)} collective-permute-done((bf16[32,3072]{1,0:T(8,128)(2,1)}, bf16[32,3072]{1,0:T(8,128)(2,1)S(1)}, u32[]{:S(2)}, u32[]{:S(2)}) %collective-permute-start) | collective-permute-done | bytes 196640 | tf_op jit(solution)/shard_map/ppermute | solution.py:37
  11.0 1.4 %collective-permute-start.1 = (bf16[32,3200]{1,0:T(8,128)(2,1)S(1)}, bf16[32,3200]{1,0:T(8,128)(2,1)S(1)}, u32[]{:S(2)}, u32[]{:S(2)}) collective-permute-start(bf16[32,3200]{1,0:T(8,128)(2,1)S(1)} %pad_maximum_fusion), channel_id=1, source_target_pairs={{0,8},{1,3},{2,10},{3,5},{4,12},{5,7},{6,14},{7,1},{8,16},{9,11},{... | collective-permute-start | bytes 614408 | tf_op jit(solution)/shard_map/ppermute | solution.py:37
  12.4 1.5 %collective-permute-start.2 = (bf16[32,3200]{1,0:T(8,128)(2,1)S(1)}, bf16[32,3200]{1,0:T(8,128)(2,1)S(1)}, u32[]{:S(2)}, u32[]{:S(2)}) collective-permute-start(bf16[32,3200]{1,0:T(8,128)(2,1)S(1)} %pad_maximum_fusion), channel_id=1, source_target_pairs={{0,24},{1,7},{2,26},{3,1},{4,28},{5,3},{6,30},{7,5},{8,0},{9,15},{... | collective-permute-start | bytes 614408 | tf_op jit(solution)/shard_map/ppermute | solution.py:37
  13.9 1.6 %collective-permute-start.3 = (bf16[32,3200]{1,0:T(8,128)(2,1)S(1)}, bf16[32,3200]{1,0:T(8,128)(2,1)S(1)}, u32[]{:S(2)}, u32[]{:S(2)}) collective-permute-start(bf16[32,3200]{1,0:T(8,128)(2,1)S(1)} %pad_maximum_fusion), channel_id=1, source_target_pairs={{0,16},{1,5},{2,18},{3,7},{4,20},{5,1},{6,22},{7,3},{8,24},{9,13},... | collective-permute-start | bytes 614408 | tf_op jit(solution)/shard_map/ppermute | solution.py:37
  15.5 4.6 %shard_map.69.turned = bf16[3072,1408]{1,0:T(8,128)(2,1)S(1)} custom-call(s32[4]{0:T(128)S(1)} %get-tuple-element.50.place, bf16[1408,3072]{1,0:T(8,128)(2,1)} %bitcast.26), custom_call_target="tpu_custom_call" | custom-call | flops 1 | bytes 1 | tf_op jit(solution)/shard_map/pallas_call | solution.py:231
  20.1 0.0 copy-start
  20.1 0.0 collective-permute-done.1
  20.1 0.0 collective-permute-done.2
  20.2 0.5 collective-permute-done.3
  20.7 0.0 copy-start.1
  20.7 2.6 %collective-permute-start.6 = (bf16[128,3200]{1,0:T(8,128)(2,1)S(1)}, bf16[128,3200]{1,0:T(8,128)(2,1)S(1)}, u32[]{:S(2)}, u32[]{:S(2)}) collective-permute-start(bf16[128,3200]{1,0:T(8,128)(2,1)S(1)} %constant_dynamic-update-slice_fusion.mine), channel_id=1, source_target_pairs={{0,1},{1,0},{2,3},{3,2},{4,5},{5,4},{6,7},{7,6},{8,9},{9,8},{10,11... | collective-permute-start | bytes 2457608 | tf_op jit(solution)/shard_map/ppermute | solution.py:37
  23.3 0.8 %collective-permute-start.4 = (bf16[128,3200]{1,0:T(8,128)(2,1)S(1)}, bf16[128,3200]{1,0:T(8,128)(2,1)S(1)}, u32[]{:S(2)}, u32[]{:S(2)}) collective-permute-start(bf16[128,3200]{1,0:T(8,128)(2,1)S(1)} %constant_dynamic-update-slice_fusion.mine), channel_id=1, source_target_pairs={{0,2},{1,9},{2,4},{3,11},{4,6},{5,13},{6,0},{7,15},{8,10},{9,17},{... | collective-permute-start | bytes 2457608 | tf_op jit(solution)/shard_map/ppermute | solution.py:37
  24.1 1.9 %collective-permute-start.5 = (bf16[128,3200]{1,0:T(8,128)(2,1)S(1)}, bf16[128,3200]{1,0:T(8,128)(2,1)S(1)}, u32[]{:S(2)}, u32[]{:S(2)}) collective-permute-start(bf16[128,3200]{1,0:T(8,128)(2,1)S(1)} %constant_dynamic-update-slice_fusion.mine), channel_id=1, source_target_pairs={{0,6},{1,25},{2,0},{3,27},{4,2},{5,29},{6,4},{7,31},{8,14},{9,1},{... | collective-permute-start | bytes 2457608 | tf_op jit(solution)/shard_map/ppermute | solution.py:37
  26.0 0.0 collective-permute-done.6.theirs
  26.0 3.4 %shard_map.71 = (f32[192,1408]{1,0:T(8,128)S(1)}, f32[192,128]{1,0:T(8,128)S(1)}) custom-call(s32[4]{0:T(128)S(1)} %get-tuple-element.50.place, bf16[128,3200]{1,0:T(8,128)(2,1)S(1)} %constant_dynamic-update-slice_fusion.mine, bf16[128,3200]{1,0:T(8,128)(2,1)S(1)} %collective-permute-done.6.theirs, bf16[3072,1408]{1,0:T(8,128)(2,1)S(1)} %shard_map.69.turned), custom_call_target="tpu_custom_call" | custom-call | flops 1 | bytes 1 | tf_op jit(solution)/shard_map/pallas_call | solution.py:297
  29.4 0.0 copy-done.1
  29.4 5.0 %shard_map.70 = (f32[96,3072]{1,0:T(8,128)S(1)}, f32[96,3072]{1,0:T(8,128)S(1)}) custom-call(s32[4]{0:T(128)S(1)} %get-tuple-element.50.place, bf16[768,1408]{1,0:T(8,128)(2,1)S(1)} %bitcast.21, bf16[1408,3072]{1,0:T(8,128)(2,1)} %bitcast.27), custom_call_target="tpu_custom_call" | custom-call | flops 1 | bytes 1 | tf_op jit(solution)/shard_map/pallas_call | solution.py:274
  34.4 1.6 %collective-permute-done.4.low = bf16[128,3200]{1,0:T(8,128)(2,1)S(1)} collective-permute-done((bf16[128,3200]{1,0:T(8,128)(2,1)S(1)}, bf16[128,3200]{1,0:T(8,128)(2,1)S(1)}, u32[]{:S(2)}, u32[]{:S(2)}) %collective-permute-start.4) | collective-permute-done | bytes 819232 | tf_op jit(solution)/shard_map/ppermute | solution.py:37
  36.0 0.0 collective-permute-done.5.high
  36.0 1.3 %collective-permute-start.10 = (bf16[128,3200]{1,0:T(8,128)(2,1)S(1)}, bf16[128,3200]{1,0:T(8,128)(2,1)S(1)}, u32[]{:S(2)}, u32[]{:S(2)}) collective-permute-start(bf16[128,3200]{1,0:T(8,128)(2,1)S(1)} %collective-permute-done.5.high), channel_id=1, source_target_pairs={{0,1},{1,0},{2,3},{3,2},{4,5},{5,4},{6,7},{7,6},{8,9},{9,8},{10,11... | collective-permute-start | bytes 2457608 | tf_op jit(solution)/shard_map/ppermute | solution.py:37
  37.3 0.0 collective-permute-start.9
  37.3 0.1 shard_map.72
  37.4 1.7 %collective-permute-start.7 = (bf16[64,3200]{1,0:T(8,128)(2,1)S(1)}, bf16[64,3200]{1,0:T(8,128)(2,1)S(1)}, u32[]{:S(2)}, u32[]{:S(2)}) collective-permute-start(bf16[64,3200]{1,0:T(8,128)(2,1)S(1)} %get-tuple-element.59), channel_id=1, source_target_pairs={{0,6},{1,25},{2,0},{3,27},{4,2},{5,29},{6,4},{7,31},{8,14},{9,1},{... | collective-permute-start | bytes 1228808 | tf_op jit(solution)/shard_map/ppermute | solution.py:37
  39.1 0.0 collective-permute-start.8
  39.1 1.8 %collective-permute-start.11 = (f32[96,3072]{1,0:T(8,128)S(1)}, f32[96,3072]{1,0:T(8,128)S(1)}, u32[]{:S(2)}, u32[]{:S(2)}) collective-permute-start(f32[96,3072]{1,0:T(8,128)S(1)} %get-tuple-element.69), channel_id=1, source_target_pairs={{0,1},{1,0},{2,3},{3,2},{4,5},{5,4},{6,7},{7,6},{8,9},{9,8},{10,11... | collective-permute-start | bytes 3538952 | tf_op jit(solution)/shard_map/ppermute | solution.py:37
  40.8 0.0 collective-permute-done.10.high_other
  40.8 0.0 collective-permute-done.9.low_other
  40.9 0.0 copy-done
  40.9 7.1 %shard_map.73 = (bf16[768,1408]{1,0:T(8,128)(2,1)}, f32[32,128]{1,0:T(8,128)S(1)}, f32[144,1408]{1,0:T(8,128)S(1)}) custom-call(s32[4]{0:T(128)S(1)} %get-tuple-element.50.place, bf16[128,3200]{1,0:T(8,128)(2,1)S(1)} %collective-permute-done.4.low, bf16[128,3200]{1,0:T(8,128)(2,1)S(1)} %collective-permute-done.5.high, ...), custom_call_target="tpu_custom_call" | custom-call | flops 1 | bytes 1 | tf_op jit(solution)/shard_map/pallas_call | solution.py:396
  47.9 0.0 collective-permute-done.7.refs_0_
  47.9 0.0 collective-permute-done.8.refs_1_
  47.9 0.1 shard_map.74.tokens.mine
  48.0 2.1 %collective-permute-start.12 = (bf16[128,3200]{1,0:T(8,128)(2,1)S(1)}, bf16[128,3200]{1,0:T(8,128)(2,1)S(1)}, u32[]{:S(2)}, u32[]{:S(2)}) collective-permute-start(bf16[128,3200]{1,0:T(8,128)(2,1)S(1)} %shard_map.74.tokens.mine), channel_id=1, source_target_pairs={{0,1},{1,0},{2,3},{3,2},{4,5},{5,4},{6,7},{7,6},{8,9},{9,8},{10,11... | collective-permute-start | bytes 2457608 | tf_op jit(solution)/shard_map/ppermute | solution.py:37
  50.2 0.0 collective-permute-done.11.other_ahead
  50.2 1.8 %shard_map.75 = f32[32,128]{1,0:T(8,128)} custom-call(s32[4]{0:T(128)S(1)} %get-tuple-element.50.place, bf16[128,3200]{1,0:T(8,128)(2,1)S(1)} %shard_map.74.tokens.mine, f32[96,3072]{1,0:T(8,128)S(1)} %get-tuple-element.68.ahead, f32[96,3072]{1,0:T(8,128)S(1)} %collective-permute-done.11.other_ahead, f32[32,128]{1,0:T(8,128)S(1)} %get-tuple-element.70.early), custom_call_target="tpu_custom_call" | custom-call | flops 1 | bytes 1 | tf_op jit(solution)/shard_map/pallas_call | solution.py:442
  52.0 4.5 %all-to-all-start = ((f32[32,1,128]{2,1,0:T(1,128)}), f32[32,1,128]{2,1,0:T(1,128)S(1)}, u32[]{:S(2)}, u32[]{:S(2)}) async-start(f32[32,1,128]{2,1,0:T(1,128)} %bitcast.12), calls=%async_computation | async-start | bytes 32768 | tf_op jit(solution)/shard_map/all_to_all | solution.py:571
  56.5 0.0 collective-permute-done.12.theirs
  56.5 5.9 %shard_map.76 = bf16[768,1408]{1,0:T(8,128)(2,1)} custom-call(s32[4]{0:T(128)S(1)} %get-tuple-element.50.place, bf16[128,3200]{1,0:T(8,128)(2,1)S(1)} %shard_map.74.tokens.mine, bf16[128,3200]{1,0:T(8,128)(2,1)S(1)} %collective-permute-done.12.theirs, bf16[3072,1408]{1,0:T(8,128)(2,1)} %copy-done, ...), custom_call_target="tpu_custom_call", output_to_operand_aliasing={{}: (5, {})} | custom-call | flops 1660944384 | bytes 1 | tf_op jit(solution)/shard_map/pallas_call | solution.py:500
  62.4 1.0 %all-to-all-done = f32[32,1,128]{2,1,0:T(1,128)S(1)} async-done(((f32[32,1,128]{2,1,0:T(1,128)}), f32[32,1,128]{2,1,0:T(1,128)S(1)}, u32[]{:S(2)}, u32[]{:S(2)}) %all-to-all-start) | async-done | bytes 16416 | tf_op jit(solution)/shard_map/all_to_all | solution.py:571
  63.4 0.8 %shard_map.77 = f32[4,32]{1,0:T(4,128)} custom-call(f32[32,128]{1,0:T(8,128)S(1)} %bitcast.23, s32[8,128]{1,0:T(8,128)S(1)} %get-tuple-element.75.lines), custom_call_target="tpu_custom_call" | custom-call | tf_op jit(solution)/shard_map/pallas_call | solution.py:574
  (5 shorter events, 0.1 us)
Async XLA Ops:
  0.6 10.4 %collective-permute-start = (bf16[32,3072]{1,0:T(8,128)(2,1)}, bf16[32,3072]{1,0:T(8,128)(2,1)S(1)}, u32[]{:S(2)}, u32[]{:S(2)}) collective-permute-start(bf16[32,3072]{1,0:T(8,128)(2,1)} %bitcast.30), channel_id=1, source_target_pairs={{0,224},{1,225},{2,226},{3,227},{4,228},{5,229},{6,230},{7,231},{8... | collective-permute-start | bytes 589832 | tf_op jit(solution)/shard_map/ppermute | solution.py:37
  7.2 0.7 %copy-start.2 = (s32[1,32,4]{1,2,0:T(4,128)S(1)}, s32[1,32,4]{1,2,0:T(4,128)}, u32[]{:S(2)}) copy-start(s32[1,32,4]{1,2,0:T(4,128)} %param.6) | copy-start | bytes 1540
  7.9 0.7 %copy-start.3 = (bf16[1,32,4]{1,2,0:T(4,128)(2,1)S(1)}, bf16[1,32,4]{1,2,0:T(4,128)(2,1)}, u32[]{:S(2)}) copy-start(bf16[1,32,4]{1,2,0:T(4,128)(2,1)} %param.7) | copy-start | bytes 772
  11.0 9.1 %collective-permute-start.1 = (bf16[32,3200]{1,0:T(8,128)(2,1)S(1)}, bf16[32,3200]{1,0:T(8,128)(2,1)S(1)}, u32[]{:S(2)}, u32[]{:S(2)}) collective-permute-start(bf16[32,3200]{1,0:T(8,128)(2,1)S(1)} %pad_maximum_fusion), channel_id=1, source_target_pairs={{0,8},{1,3},{2,10},{3,5},{4,12},{5,7},{6,14},{7,1},{8,16},{9,11},{... | collective-permute-start | bytes 614408 | tf_op jit(solution)/shard_map/ppermute | solution.py:37
  12.4 7.8 %collective-permute-start.2 = (bf16[32,3200]{1,0:T(8,128)(2,1)S(1)}, bf16[32,3200]{1,0:T(8,128)(2,1)S(1)}, u32[]{:S(2)}, u32[]{:S(2)}) collective-permute-start(bf16[32,3200]{1,0:T(8,128)(2,1)S(1)} %pad_maximum_fusion), channel_id=1, source_target_pairs={{0,24},{1,7},{2,26},{3,1},{4,28},{5,3},{6,30},{7,5},{8,0},{9,15},{... | collective-permute-start | bytes 614408 | tf_op jit(solution)/shard_map/ppermute | solution.py:37
  13.9 6.7 %collective-permute-start.3 = (bf16[32,3200]{1,0:T(8,128)(2,1)S(1)}, bf16[32,3200]{1,0:T(8,128)(2,1)S(1)}, u32[]{:S(2)}, u32[]{:S(2)}) collective-permute-start(bf16[32,3200]{1,0:T(8,128)(2,1)S(1)} %pad_maximum_fusion), channel_id=1, source_target_pairs={{0,16},{1,5},{2,18},{3,7},{4,20},{5,1},{6,22},{7,3},{8,24},{9,13},... | collective-permute-start | bytes 614408 | tf_op jit(solution)/shard_map/ppermute | solution.py:37
  20.1 20.7 %copy-start = (bf16[3072,1408]{1,0:T(8,128)(2,1)}, bf16[3072,1408]{1,0:T(8,128)(2,1)S(1)}, u32[]{:S(2)}) copy-start(bf16[3072,1408]{1,0:T(8,128)(2,1)S(1)} %shard_map.69.turned) | copy-start | bytes 25952260
  20.7 8.7 %copy-start.1 = (bf16[1,1,768,1408]{3,2,1,0:T(8,128)(2,1)S(1)}, bf16[1,1,768,1408]{3,2,1,0:T(8,128)(2,1)}, u32[]{:S(2)}) copy-start(bf16[1,1,768,1408]{3,2,1,0:T(8,128)(2,1)} %param.9) | copy-start | bytes 6488068
  20.7 5.3 %collective-permute-start.6 = (bf16[128,3200]{1,0:T(8,128)(2,1)S(1)}, bf16[128,3200]{1,0:T(8,128)(2,1)S(1)}, u32[]{:S(2)}, u32[]{:S(2)}) collective-permute-start(bf16[128,3200]{1,0:T(8,128)(2,1)S(1)} %constant_dynamic-update-slice_fusion.mine), channel_id=1, source_target_pairs={{0,1},{1,0},{2,3},{3,2},{4,5},{5,4},{6,7},{7,6},{8,9},{9,8},{10,11... | collective-permute-start | bytes 2457608 | tf_op jit(solution)/shard_map/ppermute | solution.py:37
  23.3 12.7 %collective-permute-start.4 = (bf16[128,3200]{1,0:T(8,128)(2,1)S(1)}, bf16[128,3200]{1,0:T(8,128)(2,1)S(1)}, u32[]{:S(2)}, u32[]{:S(2)}) collective-permute-start(bf16[128,3200]{1,0:T(8,128)(2,1)S(1)} %constant_dynamic-update-slice_fusion.mine), channel_id=1, source_target_pairs={{0,2},{1,9},{2,4},{3,11},{4,6},{5,13},{6,0},{7,15},{8,10},{9,17},{... | collective-permute-start | bytes 2457608 | tf_op jit(solution)/shard_map/ppermute | solution.py:37
  24.1 11.9 %collective-permute-start.5 = (bf16[128,3200]{1,0:T(8,128)(2,1)S(1)}, bf16[128,3200]{1,0:T(8,128)(2,1)S(1)}, u32[]{:S(2)}, u32[]{:S(2)}) collective-permute-start(bf16[128,3200]{1,0:T(8,128)(2,1)S(1)} %constant_dynamic-update-slice_fusion.mine), channel_id=1, source_target_pairs={{0,6},{1,25},{2,0},{3,27},{4,2},{5,29},{6,4},{7,31},{8,14},{9,1},{... | collective-permute-start | bytes 2457608 | tf_op jit(solution)/shard_map/ppermute | solution.py:37
  36.0 4.8 %collective-permute-start.10 = (bf16[128,3200]{1,0:T(8,128)(2,1)S(1)}, bf16[128,3200]{1,0:T(8,128)(2,1)S(1)}, u32[]{:S(2)}, u32[]{:S(2)}) collective-permute-start(bf16[128,3200]{1,0:T(8,128)(2,1)S(1)} %collective-permute-done.5.high), channel_id=1, source_target_pairs={{0,1},{1,0},{2,3},{3,2},{4,5},{5,4},{6,7},{7,6},{8,9},{9,8},{10,11... | collective-permute-start | bytes 2457608 | tf_op jit(solution)/shard_map/ppermute | solution.py:37
  37.3 3.5 %collective-permute-start.9 = (bf16[128,3200]{1,0:T(8,128)(2,1)S(1)}, bf16[128,3200]{1,0:T(8,128)(2,1)S(1)}, u32[]{:S(2)}, u32[]{:S(2)}) collective-permute-start(bf16[128,3200]{1,0:T(8,128)(2,1)S(1)} %collective-permute-done.4.low), channel_id=1, source_target_pairs={{0,1},{1,0},{2,3},{3,2},{4,5},{5,4},{6,7},{7,6},{8,9},{9,8},{10,11... | collective-permute-start | bytes 2457608 | tf_op jit(solution)/shard_map/ppermute | solution.py:37
  37.4 10.5 %collective-permute-start.7 = (bf16[64,3200]{1,0:T(8,128)(2,1)S(1)}, bf16[64,3200]{1,0:T(8,128)(2,1)S(1)}, u32[]{:S(2)}, u32[]{:S(2)}) collective-permute-start(bf16[64,3200]{1,0:T(8,128)(2,1)S(1)} %get-tuple-element.59), channel_id=1, source_target_pairs={{0,6},{1,25},{2,0},{3,27},{4,2},{5,29},{6,4},{7,31},{8,14},{9,1},{... | collective-permute-start | bytes 1228808 | tf_op jit(solution)/shard_map/ppermute | solution.py:37
  39.1 8.8 %collective-permute-start.8 = (bf16[64,3200]{1,0:T(8,128)(2,1)S(1)}, bf16[64,3200]{1,0:T(8,128)(2,1)S(1)}, u32[]{:S(2)}, u32[]{:S(2)}) collective-permute-start(bf16[64,3200]{1,0:T(8,128)(2,1)S(1)} %get-tuple-element.60), channel_id=1, source_target_pairs={{0,2},{1,9},{2,4},{3,11},{4,6},{5,13},{6,0},{7,15},{8,10},{9,17},{... | collective-permute-start | bytes 1228808 | tf_op jit(solution)/shard_map/ppermute | solution.py:37
  39.1 11.1 %collective-permute-start.11 = (f32[96,3072]{1,0:T(8,128)S(1)}, f32[96,3072]{1,0:T(8,128)S(1)}, u32[]{:S(2)}, u32[]{:S(2)}) collective-permute-start(f32[96,3072]{1,0:T(8,128)S(1)} %get-tuple-element.69), channel_id=1, source_target_pairs={{0,1},{1,0},{2,3},{3,2},{4,5},{5,4},{6,7},{7,6},{8,9},{9,8},{10,11... | collective-permute-start | bytes 3538952 | tf_op jit(solution)/shard_map/ppermute | solution.py:37
  48.0 8.5 %collective-permute-start.12 = (bf16[128,3200]{1,0:T(8,128)(2,1)S(1)}, bf16[128,3200]{1,0:T(8,128)(2,1)S(1)}, u32[]{:S(2)}, u32[]{:S(2)}) collective-permute-start(bf16[128,3200]{1,0:T(8,128)(2,1)S(1)} %shard_map.74.tokens.mine), channel_id=1, source_target_pairs={{0,1},{1,0},{2,3},{3,2},{4,5},{5,4},{6,7},{7,6},{8,9},{9,8},{10,11... | collective-permute-start | bytes 2457608 | tf_op jit(solution)/shard_map/ppermute | solution.py:37
  52.0 11.4 %all-to-all-start = ((f32[32,1,128]{2,1,0:T(1,128)}), f32[32,1,128]{2,1,0:T(1,128)S(1)}, u32[]{:S(2)}, u32[]{:S(2)}) async-start(f32[32,1,128]{2,1,0:T(1,128)} %bitcast.12), calls=%async_computation | async-start | bytes 32768 | tf_op jit(solution)/shard_map/all_to_all | solution.py:571
